TPU v7x, 32 devices: a whole 2x2x4 slice. The times are simulated.
32 devices in a mesh: ex: 16 (over z, y, core), tok: 2 (over x).
Axes of the slice: x: 2, y: 2, z: 4, core: 2. Of those that a mesh axis runs over, the one named last changes fastest.
Arguments:
- activations: bfloat16 [1024, 32, 4096], P(('ex', 'tok')), may hold values from -6 to 6
- out_grads: bfloat16 [1024, 32, 2, 1024], P(('ex', 'tok')), may hold values from -6 to 6
- block_len: int32 [1024], P(('ex', 'tok')), may hold values from 1 to 32
- block_dest: int32 [1024, 1], P(('ex', 'tok')), may hold values from 0 to 15; in each aligned block of 32 rows (0 to 31, 32 to 63, ...) at most 2 rows name the same one
- block_slot: int32 [1024], P(('ex', 'tok')), may hold values from 0 to 3
- in_proj: bfloat16 [4096, 128], replicated, may hold values from -0.09375 to 0.09375
- out_proj: bfloat16 [2, 1024, 64], replicated, may hold values from -0.1875 to 0.1875
- query_grads: float32 [32, 8192], P('ex'), may hold values from -6 to 6
- precond: float32 [2, 2, 64, 64], replicated, may hold values from -2 to 2, as said below
Outputs:
- scores: float32 [32, 64], P('tok', 'ex')
Inputs may be any that keep to these rules, and one draw needn't show every extreme that they name: `block_dest`: among the 32 blocks of one device no index of ex is named more than 2 times, a bound that some device reaches; every index of ex is named by some block of the whole array. `precond`: entries of order one or less.
All inputs are finite; a program needn't handle non-finite values.
Results may differ from a plain program's by a relative error of at most 0.0003.
Values sent between devices are 32-bit elements; how exact they have to be, the bound alone decides.
No kernel may reach another device: no remote copies, remote signals or barrier semaphores. Data moves between devices by JAX's collectives and lax.ppermute only.
A program may use at most 64 MiB of HBM per device.

v0:
```python
import jax
import jax.numpy as jnp
from jax import lax
from jax.sharding import PartitionSpec as P

R = 64
BLK = 32
CAP = 2
EX_DEV = 4
F = 8192


highest = lax.Precision.HIGHEST


def on_device(
    activations,
    out_grads,
    block_len,
    block_dest,
    block_slot,
    in_proj,
    out_proj,
    query_grads,
    precond,
):
    block_count = activations.shape[0]
    block_size = activations.shape[1]
    ex_count = lax.axis_size("ex")
    proj_in = jnp.dot(
        activations.reshape(block_count * block_size, -1),
        in_proj,
        preferred_element_type=jnp.float32,
    )
    proj_in = proj_in.reshape(block_count, block_size, 2, R)
    proj_out = jnp.einsum("btlk,lkr->btlr", out_grads, out_proj, preferred_element_type=jnp.float32)
    position = lax.broadcasted_iota(jnp.int32, (block_count, block_size), 1)
    live_mask = (position < block_len[:, None]).astype(jnp.float32)
    proj_out = proj_out * live_mask[:, :, None, None]
    partial_value = jnp.einsum("btlo,btli->bloi", proj_out, proj_in, precision=highest).reshape(
        block_count, F
    )
    target = block_dest[:, 0]
    target_hot = (target[:, None] == jnp.arange(ex_count, dtype=jnp.int32)[None, :]).astype(
        jnp.int32
    )
    earlier = jnp.cumsum(target_hot, axis=0) - target_hot
    within = jnp.sum(earlier * target_hot, axis=1)
    slot_index = target * CAP + within
    placement = (
        slot_index[None, :] == jnp.arange(ex_count * CAP, dtype=jnp.int32)[:, None]
    ).astype(jnp.float32)
    owner_hot = (block_slot[:, None] == jnp.arange(EX_DEV, dtype=jnp.int32)[None, :]).astype(
        jnp.float32
    )
    outgoing = jnp.dot(placement, partial_value, precision=highest).reshape(ex_count, CAP, F)
    outgoing_hot = jnp.dot(placement, owner_hot, precision=highest).reshape(ex_count, CAP, EX_DEV)
    incoming, incoming_hot = (
        lax.all_to_all(outgoing, "ex", split_axis=0, concat_axis=0, tiled=True),
        lax.all_to_all(outgoing_hot, "ex", split_axis=0, concat_axis=0, tiled=True),
    )
    features = jnp.dot(
        incoming_hot.reshape(-1, EX_DEV).T, incoming.reshape(-1, F), precision=highest
    )
    query_count = query_grads.shape[0]
    queries = query_grads.reshape(query_count, 2, R, R)
    left_side = jnp.einsum("lab,qlbc->qlac", precond[:, 0], queries, precision=highest)
    conditioned = jnp.einsum("qlac,lcd->qlad", left_side, precond[:, 1], precision=highest).reshape(
        query_count, F
    )
    score_terms = jnp.dot(
        lax.all_gather(conditioned, "ex", axis=0, tiled=True), features.T, precision=highest
    ) * (1.0 / (R * BLK))
    return lax.psum_scatter(score_terms, "tok", scatter_dimension=0, tiled=True)


def solution(mesh):
    placed = (
        P(("ex", "tok"), None, None),
        P(("ex", "tok"), None, None, None),
        P(("ex", "tok")),
        P(("ex", "tok"), None),
        P(("ex", "tok")),
        P(),
        P(),
        P("ex", None),
        P(),
    )
    return jax.shard_map(
        on_device, mesh=mesh, in_specs=placed, out_specs=P("tok", "ex"), check_vma=False
    )
```

profile of v0, /device:TPU:0, one launch (start us, length us, event | category | flops | bytes accessed | tf_op | source)
XLA Modules:
  0.0 93.6 jit_solution(16135493801104684893)
XLA Ops:
  6.5 0.0 copy-start
  6.5 0.8 fusion.18
  7.3 0.1 reduce_window_sum.11
  7.4 0.8 select_reduce_fusion
  8.2 0.7 multiply_add_fusion.1
  8.9 1.4 %fusion.19 = f32[32,4]{1,0:T(8,128)} fusion(s32[32]{0:T(128)} %param.13, s32[32]{0:T(128)S(1)} %multiply_add_fusion.1), kind=kOutput, calls=%fused_computation.24 | convolution fusion | flops 9344 | bytes 768 | tf_op jit(solution)/shard_map/dot_general | solution.py:57
  10.3 7.4 %all-to-all-start = ((f32[16,2,4]{2,1,0:T(2,128)}), f32[16,2,4]{2,1,0:T(2,128)S(1)}, u32[]{:S(2)}, u32[]{:S(2)}) async-start(f32[16,2,4]{2,1,0:T(2,128)} %bitcast.9), calls=%async_computation | async-start | bytes 32768 | tf_op jit(solution)/shard_map/all_to_all | solution.py:60
  17.7 0.0 all-gather.3.cloned.1.call-start
  17.7 1.0 %reshape.67 = f32[2,2,64,64]{3,2,1,0:T(8,128)S(1)} reshape(f32[2,8192]{1,0:T(2,128)} %param.16) | data formatting | bytes 131072 | tf_op jit(solution)/shard_map/reshape | solution.py:66
  18.7 1.2 %convolution_bitcast_fusion.2 = f32[2,2,64,64]{2,3,0,1:T(8,128)S(1)} fusion(f32[2,2,64,64]{3,2,1,0:T(8,128)S(1)} %reshape.67, f32[2,2,64,64]{3,2,1,0:T(8,128)} %param.17), kind=kOutput, calls=%fused_computation.8 | convolution fusion | flops 12582912 | bytes 196608 | tf_op jit(solution)/shard_map/lab,qlbc->qlac/dot_general | solution.py:67
  20.0 1.2 %convolution_bitcast_fusion.1 = f32[2,2,64,64]{3,2,0,1:T(8,128)S(1)} fusion(f32[2,2,64,64]{2,3,0,1:T(8,128)S(1)} %convolution_bitcast_fusion.2, f32[2,2,64,64]{3,2,1,0:T(8,128)} %param.17), kind=kOutput, calls=%fused_computation.7 | convolution fusion | flops 12582912 | bytes 196608 | tf_op jit(solution)/shard_map/qlac,lcd->qlad/dot_general | solution.py:68
  21.2 0.7 reshape.71
  21.9 0.0 all-gather.3.cloned.1.call-update
  22.0 1.5 %copy.32 = bf16[4096,128]{0,1:T(8,128)(2,1)S(1)} copy(bf16[4096,128]{1,0:T(8,128)(2,1)} %param.14) | data formatting | bytes 2097152 | tf_op args[5]
  23.5 0.7 fusion.20
  24.2 0.0 copy-start.1
  24.2 5.0 %fusion = f32[32,32,2,64]{3,1,2,0:T(8,128)S(1)} fusion(bf16[2,64,4096,1]{2,1,0,3:T(8,128)(2,1)S(1)} %bitcast.52, bf16[32,32,4096]{2,1,0:T(8,128)(2,1)} %param.9), kind=kOutput, calls=%fused_computation.1 | convolution fusion | flops 1073741824 | bytes 9961472 | tf_op jit(solution)/shard_map/dot_general | solution.py:30
  29.2 0.0 copy-done
  29.2 0.0 copy-done.1
  29.3 1.2 %fusion.7 = f32[32,32,2,64]{3,1,2,0:T(8,128)S(1)} fusion(bf16[32,32,2,1024]{3,2,1,0:T(2,128)(2,1)S(1)} %copy-done.1, f32[32,32]{1,0:T(8,128)S(1)} %fusion.20, bf16[2,1024,64]{1,2,0:T(8,128)(2,1)S(1)} %copy-done), kind=kOutput, calls=%fused_computation.6 | convolution fusion | flops 268566528 | bytes 4984832 | tf_op jit(solution)/shard_map/btlk,lkr->btlr/dot_general | solution.py:36
  30.5 3.7 %fusion.27 = f32[32,2,64,64]{3,2,1,0:T(8,128)S(1)} fusion(f32[32,32,2,64]{3,1,2,0:T(8,128)S(1)} %fusion.7, f32[32,32,2,64]{3,1,2,0:T(8,128)S(1)} %fusion), kind=kOutput, calls=%fused_computation.34 | convolution fusion | flops 100663296 | bytes 2097152 | tf_op jit(solution)/shard_map/btlo,btli->bloi/dot_general | solution.py:40
  34.2 0.7 reshape.79
  34.9 0.6 fusion.21
  35.5 1.8 %copy.33 = f32[16,2,8192]{2,1,0:T(2,128)} copy(f32[16,2,8192]{2,0,1:T(8,128)S(1)} %fusion.21) | data formatting | bytes 2097152 | tf_op jit(solution)/shard_map/dot_general | solution.py:56
  37.4 0.0 all-to-all-done
  37.4 6.0 %all-to-all-start.1 = ((f32[16,2,8192]{2,1,0:T(2,128)}), f32[16,2,8192]{2,1,0:T(2,128)S(1)}, u32[]{:S(2)}, u32[]{:S(2)}) async-start(f32[16,2,8192]{2,1,0:T(2,128)} %copy.33), calls=%async_computation.1 | async-start | bytes 2097152 | tf_op jit(solution)/shard_map/all_to_all | solution.py:59
  43.4 0.2 reduce-scatter.4.cloned.1.call-start
  43.6 25.2 %all-gather.3.cloned.1.call-done = f32[16,2,8192]{2,1,0:T(2,128)} async-done(((f32[1,2,8192]{2,1,0:T(2,128)}), f32[16,2,8192]{2,1,0:T(2,128)}) %all-gather.3.cloned.1.call-update) | async-done | bytes 1048592 | tf_op jit(solution)/shard_map/all_gather | solution.py:72
  68.8 1.9 %reshape.72 = f32[32,8192]{1,0:T(8,128)S(1)} reshape(f32[16,2,8192]{2,1,0:T(2,128)} %all-gather.3.cloned.1.call-done) | data formatting | bytes 2097152
  70.8 0.0 all-to-all-done.1
  70.8 1.2 %convolution_bitcast_fusion = f32[4,8192]{1,0:T(4,128)S(1)} fusion(f32[16,2,8192]{2,1,0:T(2,128)S(1)} %all-to-all-done.1, f32[16,2,4]{2,1,0:T(2,128)S(1)} %all-to-all-done), kind=kOutput, calls=%fused_computation | convolution fusion | flops 12582912 | bytes 1180160 | tf_op jit(solution)/shard_map/dot_general | solution.py:62
  72.0 0.9 convolution_multiply_fusion
  72.9 0.7 copy.43
  73.6 0.0 reduce-scatter.4.cloned.1.call-update
  73.6 11.8 %reduce-scatter.4.cloned.1.call-done = f32[16,4]{1,0:T(8,128)} async-done(((f32[32,4]{1,0:T(8,128)}), f32[16,4]{1,0:T(8,128)}) %reduce-scatter.4.cloned.1.call-update) | async-done | bytes 272
  85.4 1.3 %copy.44 = f32[16,4]{0,1:T(4,128)} copy(f32[16,4]{1,0:T(8,128)} %reduce-scatter.4.cloned.1.call-done) | data formatting | bytes 512
  (2 shorter events, 0.0 us)
Async XLA Ops:
  6.5 22.7 %copy-start = (bf16[2,1024,64]{1,2,0:T(8,128)(2,1)S(1)}, bf16[2,1024,64]{1,2,0:T(8,128)(2,1)}, u32[]{:S(2)}) copy-start(bf16[2,1024,64]{1,2,0:T(8,128)(2,1)} %param.15) | copy-start | bytes 786436
  10.3 27.0 %all-to-all-start = ((f32[16,2,4]{2,1,0:T(2,128)}), f32[16,2,4]{2,1,0:T(2,128)S(1)}, u32[]{:S(2)}, u32[]{:S(2)}) async-start(f32[16,2,4]{2,1,0:T(2,128)} %bitcast.9), calls=%async_computation | async-start | bytes 32768 | tf_op jit(solution)/shard_map/all_to_all | solution.py:60
  17.7 51.1 %all-gather.3.cloned.1.call-start = ((), (), s32[]{:S(2)}) async-start(), calls=%async_computation.3 | async-start | bytes 1114112 | tf_op jit(solution)/shard_map/all_gather | solution.py:72
  24.2 5.1 %copy-start.1 = (bf16[32,32,2,1024]{3,2,1,0:T(2,128)(2,1)S(1)}, bf16[32,32,2,1024]{3,2,1,0:T(2,128)(2,1)}, u32[]{:S(2)}) copy-start(bf16[32,32,2,1024]{3,2,1,0:T(2,128)(2,1)} %param.10) | copy-start | bytes 12582916
  37.4 33.4 %all-to-all-start.1 = ((f32[16,2,8192]{2,1,0:T(2,128)}), f32[16,2,8192]{2,1,0:T(2,128)S(1)}, u32[]{:S(2)}, u32[]{:S(2)}) async-start(f32[16,2,8192]{2,1,0:T(2,128)} %copy.33), calls=%async_computation.1 | async-start | bytes 2097152 | tf_op jit(solution)/shard_map/all_to_all | solution.py:59
  43.4 42.0 %reduce-scatter.4.cloned.1.call-start = ((), (), s32[]{:S(2)}) async-start(), calls=%async_computation.4 | async-start | bytes 24576
Sparse Core Ops, SparseCore 0:
  22.1 46.7 all-gather.2
  73.7 11.6 reduce-scatter.3
where the time goes:
time: 94.1 us; the launch traced here: 93.6 us
  waiting for transfers between devices  37.1 us (39%)
  matrix products  16.6 us (18%)
  starting transfers between devices  13.7 us (15%)
  between operations  13.5 us (14%)
  local copies, waits for them, and re-layouts  9.68 us (10%)
  other arithmetic  3.06 us (3%)
    all_gather x1, waiting for transfers between devices, on_device(): lax.all_gather(conditioned, 'ex', axis=0, tiled=True)  25.2 us
    unnamed x3, waiting for transfers between devices  11.8 us
    all_to_all x1, starting transfers between devices, on_device(): lax.all_to_all(outgoing_hot, 'ex', split_axis=0, concat_axis=0, tiled=True)  7.39 us
    unnamed x9, local copies, waits for them, and re-layouts  6.21 us
    all_to_all x1, starting transfers between devices, on_device(): lax.all_to_all(outgoing, 'ex', split_axis=0, concat_axis=0, tiled=True)  6.01 us
    dot_general x1, matrix products, on_device(): jnp.dot(activations.reshape(block_count * block_size, -1), in_proj, prefe...  5.03 us
    dot_general x1, matrix products, on_device(): jnp.einsum('btlo,btli->bloi', proj_out, proj_in, precision=highest)  3.72 us
  transfers between devices with their start and end apart: 4, of which 2 were waited for; matrix products, arithmetic and copies ran while one was open for 23% of the time, Pallas kernels for 0%

commit v1 on v0

v1 whole, which is shorter than its diff:
```python
import jax
import jax.numpy as jnp
from jax import lax
from jax.experimental import pallas as pl
from jax.experimental.pallas import tpu as pltpu
from jax.sharding import PartitionSpec as P

EX_DEV = 4
SUB = 4
HIGHEST = lax.Precision.HIGHEST
NT = (((1,), (1,)), ((), ()))
TN = (((0,), (0,)), ((), ()))


def split(x):
    high = x.astype(jnp.bfloat16)
    return high, (x - high.astype(jnp.float32)).astype(jnp.bfloat16)


def mm(a, b, dims=(((1,), (0,)), ((), ()))):
    return lax.dot_general(a, b, dims, preferred_element_type=jnp.float32)


def split_mm(a, b, dims=(((1,), (0,)), ((), ()))):
    (ah, al), (bh, bl) = split(a), split(b)
    return mm(ah, bh, dims) + mm(al, bh, dims) + mm(ah, bl, dims)


def iota(shape, axis):
    return lax.broadcasted_iota(jnp.int32, shape, axis)


def features_kernel(
    core_ref, act_ref, out_ref, w_ref, precond_ref, id_ref, mine_ref, theirs_ref, right_ref, left_ref
):
    step = pl.program_id(0)
    blocks, size = act_ref.shape[0], act_ref.shape[1]
    r = precond_ref.shape[-1]
    half = r // 2
    rows = SUB * size

    @pl.when(step == 0)
    def _():
        row, col = iota((r, r), 0), iota((r, r), 1)
        order = (col == 2 * (row % half) + row // half).astype(jnp.float32)
        eye = (col == row).astype(jnp.float32)
        for l in range(2):
            left_ref[l] = lax.dot_general(
                order, precond_ref[l, 0], NT, precision=HIGHEST, preferred_element_type=jnp.float32
            )
            turned = lax.dot_general(
                eye, precond_ref[l, 1], NT, precision=HIGHEST, preferred_element_type=jnp.float32
            )
            both = jnp.concatenate([turned, turned], axis=1)
            zero = jnp.zeros_like(both)
            right_ref[l * r : (l + 1) * r] = jnp.concatenate(
                [both, zero] if l == 0 else [zero, both], axis=1
            )
        mine_ref[half] = jnp.broadcast_to(id_ref[...], mine_ref.shape[1:])
        theirs_ref[half] = jnp.broadcast_to(id_ref[...], theirs_ref.shape[1:])

    acts = act_ref[...].reshape(blocks * size, act_ref.shape[2])
    proj_in = split_mm(mm(acts, w_ref[...]), right_ref[...])
    core = core_ref[0]
    low_lane = iota((half, 2 * r), 1) < r
    lane_block = iota((r, rows), 1) // size
    outs = [split_mm(left_ref[l], out_ref[l], NT) for l in range(2)]
    for s in range(blocks // SUB):
        feats = []
        for l in range(2):
            oh, ol = split(outs[l][:, s * rows : (s + 1) * rows])
            ih, il = split(proj_in[s * rows : (s + 1) * rows, l * 2 * r : (l + 1) * 2 * r])
            zero = jnp.zeros_like(oh)
            lh = jnp.concatenate([jnp.where(lane_block == j, oh, zero) for j in range(SUB)], axis=0)
            ll = jnp.concatenate([jnp.where(lane_block == j, ol, zero) for j in range(SUB)], axis=0)
            got = mm(lh, ih) + mm(ll, ih) + mm(lh, il)
            feats.append(
                [
                    jnp.where(
                        low_lane,
                        got[j * r : j * r + half],
                        got[j * r + half : (j + 1) * r],
                    )
                    for j in range(SUB)
                ]
            )
        for j in range(SUB):
            b = step * blocks + s * SUB + j
            mine_ref[:half, pl.ds(b, 1), :] = jnp.where(core == 0, feats[0][j], feats[1][j])[:, None]
            theirs_ref[:half, pl.ds(b, 1), :] = jnp.where(core == 0, feats[1][j], feats[0][j])[:, None]


def scores_kernel(ex_count, tok_count, q_ref, mine_ref, other_ref, out_ref):
    half = mine_ref.shape[0] - 1
    queries = q_ref.shape[0] // half
    each = queries // tok_count
    acc = None
    for m in range(0, half, 2):
        q = jnp.concatenate([q_ref[pl.ds(m + d, queries, stride=half), :] for d in (0, 1)], axis=1)
        f = jnp.concatenate(
            [jnp.concatenate([ref[m + d] for d in (0, 1)], axis=1) for ref in (mine_ref, other_ref)],
            axis=0,
        )
        part = split_mm(f, q, NT)
        acc = part if acc is None else acc + part
    ids = jnp.concatenate([mine_ref[half], other_ref[half]], axis=0)[:, :1].astype(jnp.int32)
    blocks = acc.shape[0]
    wide = tok_count * EX_DEV * each
    lane = iota((queries, wide), 1)
    spread = (
        iota((queries, wide), 0) == lane // (EX_DEV * each) * each + lane % each
    ).astype(jnp.float32)
    spread = lax.dot_general(
        acc, spread, (((1,), (0,)), ((), ())), precision=HIGHEST, preferred_element_type=jnp.float32
    )
    lane = iota((blocks, wide), 1)
    spread = jnp.where(lane // each % EX_DEV == ids % EX_DEV, spread, 0.0)
    owner = (iota((blocks, ex_count * tok_count), 1) // tok_count == ids // EX_DEV).astype(jnp.float32)
    full = lax.dot_general(
        owner, spread, TN, precision=HIGHEST, preferred_element_type=jnp.float32
    )
    width = EX_DEV * each
    tok = iota((ex_count * tok_count, width), 0) % tok_count
    result = full[:, :width]
    for t in range(1, tok_count):
        result = jnp.where(tok == t, full[:, t * width : (t + 1) * width], result)
    out_ref[...] = result


def total_kernel(scale, in_ref, out_ref):
    total = jnp.sum(in_ref[...], axis=0, keepdims=True) * scale
    each = out_ref.shape[1]
    for k in range(out_ref.shape[0]):
        out_ref[pl.ds(k, 1), :] = total[:, k * each : (k + 1) * each]


def on_device(
    activations,
    out_grads,
    block_len,
    block_dest,
    block_slot,
    in_proj,
    out_proj,
    query_grads,
    precond,
):
    nb, size, depth = activations.shape
    layers, _, r = out_proj.shape
    half = r // 2
    ex_count, tok_count = lax.axis_size("ex"), lax.axis_size("tok")
    own_queries = query_grads.shape[0]
    queries = own_queries * ex_count
    core = lax.axis_index("ex") % 2

    pieces = query_grads.reshape(own_queries, layers, half, 2 * r)
    pieces = jnp.swapaxes(pieces, 0, 1).reshape(layers, own_queries * half, 2 * r)
    pieces = jnp.broadcast_to(pieces[None], (ex_count // 2,) + pieces.shape)
    pieces = pieces.reshape(ex_count, own_queries * half, 2 * r)
    gathered = lax.all_to_all(pieces, "ex", split_axis=0, concat_axis=0, tiled=True)

    live = lax.broadcasted_iota(jnp.int32, (nb, size), 1) < block_len[:, None]
    proj_out = jnp.einsum("btlk,lkr->lbtr", out_grads, out_proj, preferred_element_type=jnp.float32)
    proj_out = jnp.where(live[None, :, :, None], proj_out, 0.0).reshape(layers, nb * size, r)
    ids = (block_dest * EX_DEV + block_slot[:, None]).astype(jnp.float32)

    step_blocks = 8
    shape = jax.ShapeDtypeStruct((half + 1, nb, 2 * r), jnp.float32)
    whole = pl.BlockSpec((half + 1, nb, 2 * r), lambda i: (0, 0, 0))
    mine, theirs = pl.pallas_call(
        features_kernel,
        grid=(nb // step_blocks,),
        in_specs=[
            pl.BlockSpec(memory_space=pltpu.SMEM),
            pl.BlockSpec((step_blocks, size, depth), lambda i: (i, 0, 0)),
            pl.BlockSpec((layers, step_blocks * size, r), lambda i: (0, i, 0)),
            pl.BlockSpec((depth, layers * r), lambda i: (0, 0)),
            pl.BlockSpec((layers, 2, r, r), lambda i: (0, 0, 0, 0)),
            pl.BlockSpec((nb, 1), lambda i: (0, 0)),
        ],
        out_specs=[whole, whole],
        out_shape=[shape, shape],
        scratch_shapes=[
            pltpu.VMEM((layers * r, layers * 2 * r), jnp.float32),
            pltpu.VMEM((layers, r, r), jnp.float32),
        ],
        compiler_params=pltpu.CompilerParams(vmem_limit_bytes=32 * 1024 * 1024),
        cost_estimate=pl.CostEstimate(
            flops=2 * nb * size * depth * layers * r * 2,
            bytes_accessed=nb * size * depth * 2 + depth * layers * r * 2,
            transcendentals=0,
        ),
        name="features",
    )(core[None], activations, proj_out, in_proj, precond, ids)

    other = lax.ppermute(theirs, "ex", [(i, i ^ 1) for i in range(ex_count)])

    width = EX_DEV * queries // tok_count
    chunks = pl.pallas_call(
        lambda *refs: scores_kernel(ex_count, tok_count, *refs),
        out_shape=jax.ShapeDtypeStruct((ex_count * tok_count, width), jnp.float32),
        name="scores",
    )(gathered.reshape(queries * half, 2 * r), mine, other)
    arrived = lax.all_to_all(chunks, ("ex", "tok"), split_axis=0, concat_axis=0, tiled=True)
    total = pl.pallas_call(
        lambda *refs: total_kernel(1.0 / (r * size), *refs),
        out_shape=jax.ShapeDtypeStruct((EX_DEV, queries // tok_count), jnp.float32),
        name="total",
    )(arrived)
    return total.T


def solution(mesh):
    placed = (
        P(("ex", "tok"), None, None),
        P(("ex", "tok"), None, None, None),
        P(("ex", "tok")),
        P(("ex", "tok"), None),
        P(("ex", "tok")),
        P(),
        P(),
        P("ex", None),
        P(),
    )
    return jax.shard_map(
        on_device, mesh=mesh, in_specs=placed, out_specs=P("tok", "ex"), check_vma=False
    )
```

time: 94.1 us -> 45.8 us (0.49)
  waiting for transfers between devices: 37.1 us -> 1.56 us
  between operations: 13.5 us -> 0.08 us
  blocking collectives: 0 us -> 13.2 us
  matrix products: 16.6 us -> 3.42 us
  Pallas kernels: 0 us -> 10.7 us
  starting transfers between devices: 13.7 us -> 7.93 us
  local copies, waits for them, and re-layouts: 9.68 us -> 7.01 us
  other arithmetic: 3.06 us -> 1.41 us
    all_gather x1 -> x0, waiting for transfers between devices: 25.2 us -> none  [on_device(): lax.all_gather(conditioned, 'ex', axis=0, tiled=True)]
    dot_general x9 -> x1, matrix products: 16.6 us -> 3.42 us  [on_device(): jnp.einsum('btlk,lkr->lbtr', out_grads, out_proj, preferred_element_type=...]
    all_to_all x0 -> x1, blocking collectives: none -> 13.2 us  [on_device(): lax.all_to_all(chunks, ('ex', 'tok'), split_axis=0, concat_axis=0, tiled=...]
    unnamed x3 -> x0, waiting for transfers between devices: 11.8 us -> none
    pallas_call x0 -> x3, Pallas kernels: none -> 10.7 us  [the longest x1 6.28 us: on_device(): pl.pallas_call(features_kernel, grid=(nb // step_blocks,), in_specs=[pl.B...]
    all_to_all x2 -> x1, starting transfers between devices: 13.4 us -> 7.52 us  [on_device(): lax.all_to_all(pieces, 'ex', split_axis=0, concat_axis=0, tiled=True)]
    dot_general x1 -> x0, local copies, waits for them, and re-layouts: 1.82 us -> none  [on_device(): jnp.dot(placement, partial_value, precision=highest)]
    reshape x2 -> x0, local copies, waits for them, and re-layouts: 1.63 us -> none  [the longest x1 0.98 us: on_device(): queries = query_grads.reshape(query_count, 2, R, R)]
  transfers between devices with their start and end apart: 4 -> 2, of which waited for: 2 -> 1; matrix products, arithmetic and copies ran while one was open for 23% -> 11% of each run, Pallas kernels for 0% -> 14%
where the time goes in v1:
time: 45.8 us; the launch traced here: 45.3 us
  blocking collectives  13.2 us (29%)
  Pallas kernels  10.7 us (23%)
  starting transfers between devices  7.93 us (17%)
  local copies, waits for them, and re-layouts  7.01 us (15%)
  matrix products  3.42 us (7%)
  waiting for transfers between devices  1.56 us (3%)
  other arithmetic  1.41 us (3%)
    all_to_all x1, blocking collectives, on_device(): lax.all_to_all(chunks, ('ex', 'tok'), split_axis=0, concat_axis=0, tiled=...  13.2 us
    all_to_all x1, starting transfers between devices, on_device(): lax.all_to_all(pieces, 'ex', split_axis=0, concat_axis=0, tiled=True)  7.52 us
    pallas_call x1, Pallas kernels, on_device(): pl.pallas_call(features_kernel, grid=(nb // step_blocks,), in_specs=[pl.B...  6.28 us
    unnamed x15, local copies, waits for them, and re-layouts  6.05 us
    dot_general x1, matrix products, on_device(): jnp.einsum('btlk,lkr->lbtr', out_grads, out_proj, preferred_element_type=...  3.42 us
    pallas_call x1, Pallas kernels, on_device(): pl.pallas_call(lambda *refs: scores_kernel(ex_count, tok_count, *refs), o...  3.07 us
    ppermute x1, waiting for transfers between devices, on_device(): other = lax.ppermute(theirs, 'ex', [(i, i ^ 1) for i in range(ex_count)])  1.56 us
    pallas_call x1, Pallas kernels, on_device(): pl.pallas_call(lambda *refs: total_kernel(1.0 / (r * size), *refs), out_s...  1.38 us
  transfers between devices with their start and end apart: 2, of which 1 were waited for; matrix products, arithmetic and copies ran while one was open for 11% of the time, Pallas kernels for 14%

profile of v1, /device:TPU:0, one launch (start us, length us, event | category | flops | bytes accessed | tf_op | source)
XLA Modules:
  0.0 45.3 jit_solution(12070485203694289574)
XLA Ops:
  0.0 0.0 copy-start
  0.0 0.9 %copy.34 = f32[1,2,64,128]{3,2,1,0:T(8,128)S(1)} copy(f32[1,2,64,128]{3,1,2,0:T(2,128)} %bitcast.27) | data formatting | bytes 131072
  0.9 0.9 %broadcast_in_dim.28 = f32[8,2,64,128]{3,2,1,0:T(8,128)} broadcast(f32[2,64,128]{2,1,0:T(8,128)S(1)} %bitcast.24), dimensions={1,2,3} | broadcast | bytes 589824 | tf_op jit(solution)/shard_map/broadcast_in_dim | solution.py:158
  1.8 0.0 copy-start.2
  1.8 0.0 copy-start.4
  1.8 7.5 %all-to-all-start = ((f32[16,64,128]{2,1,0:T(8,128)}), f32[16,64,128]{2,1,0:T(8,128)S(1)}, u32[]{:S(2)}, u32[]{:S(2)}) async-start(f32[16,64,128]{2,1,0:T(8,128)} %bitcast.2), calls=%async_computation | async-start | bytes 1048576 | tf_op jit(solution)/shard_map/all_to_all | solution.py:160
  9.3 0.7 %iota_compare_fusion = pred[32,32]{1,0:T(8,128)(4,1)S(1)} fusion(s32[32]{0:T(128)} %param.11), kind=kLoop, calls=%fused_computation.4 | loop fusion | flops 1024 | bytes 1152 | tf_op jit(solution)/shard_map/lt | solution.py:162
  10.0 0.7 %bitcast_add_fusion = s32[32,1]{0,1:T(1,128)S(1)} fusion(s32[32]{0:T(128)} %param.13, s32[32,1]{0,1:T(1,128)} %param.12), kind=kLoop, calls=%fused_computation.5 | loop fusion | flops 64 | bytes 384 | tf_op jit(solution)/shard_map/add | solution.py:165
  10.7 0.1 copy.31
  10.8 0.0 copy-done
  10.8 3.4 %fusion.2 = f32[2,32,32,64]{3,2,1,0:T(8,128)S(1)} fusion(bf16[32,32,2,1024]{3,2,1,0:T(2,128)(2,1)} %param.10, pred[32,32]{1,0:T(8,128)(4,1)S(1)} %iota_compare_fusion, bf16[2,1024,64]{1,2,0:T(8,128)(2,1)S(1)} %copy-done), kind=kOutput, calls=%fused_computation.2 | convolution fusion | flops 268566528 | bytes 4981760 | tf_op jit(solution)/shard_map/btlk,lkr->lbtr/dot_general | solution.py:163
  14.2 0.0 copy-done.2
  14.2 0.0 copy-done.4
  14.3 0.0 copy-start.1
  14.3 3.4 %copy-done.1 = bf16[32,32,4096]{2,1,0:T(8,128)(2,1)S(1)} copy-done((bf16[32,32,4096]{2,1,0:T(8,128)(2,1)S(1)}, bf16[32,32,4096]{2,1,0:T(8,128)(2,1)}, u32[]{:S(2)}) %copy-start.1) | copy-done | bytes 8388632
  17.6 6.3 %features.1 = (f32[33,32,128]{2,1,0:T(8,128)S(1)}, f32[33,32,128]{2,1,0:T(8,128)S(1)}) custom-call(s32[1]{0:T(128)} %bitcast.4.core_ref, bf16[32,32,4096]{2,1,0:T(8,128)(2,1)S(1)} %copy-done.1, f32[2,1024,64]{2,1,0:T(8,128)S(1)} %bitcast.22, bf16[4096,128]{1,0:T(8,128)(2,1)S(1)} %copy-done.2, f32[2,2,64,64]{3,2,1,0:T(8,128)S(1)} %copy-done.4, ...), custom_call_target="tpu_custom_call" | custom-call | flops 2147483648 | bytes 9437184 | tf_op jit(solution)/shard_map/features/pallas_call | solution.py:170
  23.9 0.0 copy-start.3
  23.9 0.8 %copy-done.3 = f32[33,32,128]{2,1,0:T(8,128)} copy-done((f32[33,32,128]{2,1,0:T(8,128)}, f32[33,32,128]{2,1,0:T(8,128)S(1)}, u32[]{:S(2)}) %copy-start.3) | copy-done | bytes 540696
  24.7 0.4 collective-permute-start
  25.1 1.6 %collective-permute-done.refs_2_ = f32[33,32,128]{2,1,0:T(8,128)S(1)} collective-permute-done((f32[33,32,128]{2,1,0:T(8,128)S(1)}, f32[33,32,128]{2,1,0:T(8,128)S(1)}, u32[]{:S(2)}, u32[]{:S(2)}) %collective-permute-start) | collective-permute-done | bytes 540704 | tf_op jit(solution)/shard_map/ppermute | solution.py:196
  26.7 0.0 copy-start.6
  26.7 0.0 all-to-all-done
  26.7 0.0 copy-start.5
  26.7 0.8 %copy-done.6 = f32[33,32,128]{2,1,0:T(8,128)} copy-done((f32[33,32,128]{2,1,0:T(8,128)}, f32[33,32,128]{2,1,0:T(8,128)S(1)}, u32[]{:S(2)}) %copy-start.6) | copy-done | bytes 540696
  27.5 0.2 copy-done.5
  27.7 3.1 %scores.1 = f32[32,64]{1,0:T(8,128)} custom-call(f32[1024,128]{1,0:T(8,128)} %bitcast.23, f32[33,32,128]{2,1,0:T(8,128)} %copy-done.3, f32[33,32,128]{2,1,0:T(8,128)} %copy-done.6), custom_call_target="tpu_custom_call" | custom-call | tf_op jit(solution)/shard_map/scores/pallas_call | solution.py:199
  30.8 13.2 %all_to_all.16 = f32[32,1,64]{2,1,0:T(1,128)} all-to-all(f32[32,1,64]{2,1,0:T(1,128)} %bitcast.26), channel_id=1, replica_groups=mesh['ex'=16,'tok'=2] {'ex','tok'}, dimensions={0} | all-to-all | bytes 16384 | tf_op jit(solution)/shard_map/all_to_all | solution.py:204
  43.9 1.4 %total.1 = f32[4,16]{1,0:T(4,128)} custom-call(f32[32,64]{1,0:T(8,128)} %bitcast.28), custom_call_target="tpu_custom_call" | custom-call | tf_op jit(solution)/shard_map/total/pallas_call | solution.py:205
  (2 shorter events, 0.0 us)
Async XLA Ops:
  0.0 10.8 %copy-start = (bf16[2,1024,64]{1,2,0:T(8,128)(2,1)S(1)}, bf16[2,1024,64]{1,2,0:T(8,128)(2,1)}, u32[]{:S(2)}) copy-start(bf16[2,1024,64]{1,2,0:T(8,128)(2,1)} %param.15) | copy-start | bytes 786436
  1.8 12.5 %copy-start.2 = (bf16[4096,128]{1,0:T(8,128)(2,1)S(1)}, bf16[4096,128]{1,0:T(8,128)(2,1)}, u32[]{:S(2)}) copy-start(bf16[4096,128]{1,0:T(8,128)(2,1)} %w_ref.1) | copy-start | bytes 3145732
  1.8 12.5 %copy-start.4 = (f32[2,2,64,64]{3,2,1,0:T(8,128)S(1)}, f32[2,2,64,64]{3,2,1,0:T(8,128)}, u32[]{:S(2)}) copy-start(f32[2,2,64,64]{3,2,1,0:T(8,128)} %precond_ref.1) | copy-start | bytes 196612
  1.8 24.9 %all-to-all-start = ((f32[16,64,128]{2,1,0:T(8,128)}), f32[16,64,128]{2,1,0:T(8,128)S(1)}, u32[]{:S(2)}, u32[]{:S(2)}) async-start(f32[16,64,128]{2,1,0:T(8,128)} %bitcast.2), calls=%async_computation | async-start | bytes 1048576 | tf_op jit(solution)/shard_map/all_to_all | solution.py:160
  14.3 3.4 %copy-start.1 = (bf16[32,32,4096]{2,1,0:T(8,128)(2,1)S(1)}, bf16[32,32,4096]{2,1,0:T(8,128)(2,1)}, u32[]{:S(2)}) copy-start(bf16[32,32,4096]{2,1,0:T(8,128)(2,1)} %act_ref.1) | copy-start | bytes 25165828
  23.9 0.8 %copy-start.3 = (f32[33,32,128]{2,1,0:T(8,128)}, f32[33,32,128]{2,1,0:T(8,128)S(1)}, u32[]{:S(2)}) copy-start(f32[33,32,128]{2,1,0:T(8,128)S(1)} %get-tuple-element.7.refs_1_) | copy-start | bytes 1622020
  24.7 2.0 %collective-permute-start = (f32[33,32,128]{2,1,0:T(8,128)S(1)}, f32[33,32,128]{2,1,0:T(8,128)S(1)}, u32[]{:S(2)}, u32[]{:S(2)}) collective-permute-start(f32[33,32,128]{2,1,0:T(8,128)S(1)} %get-tuple-element.8), channel_id=1, source_target_pairs={{0,2},{2,0},{4,6},{6,4},{8,10},{10,8},{12,14},{14,12},{16,18},{18,... | collective-permute-start | bytes 1622024 | tf_op jit(solution)/shard_map/ppermute | solution.py:196
  26.7 0.8 %copy-start.6 = (f32[33,32,128]{2,1,0:T(8,128)}, f32[33,32,128]{2,1,0:T(8,128)S(1)}, u32[]{:S(2)}) copy-start(f32[33,32,128]{2,1,0:T(8,128)S(1)} %collective-permute-done.refs_2_) | copy-start | bytes 1622020
  26.7 1.0 %copy-start.5 = (f32[16,64,128]{2,1,0:T(8,128)}, f32[16,64,128]{2,1,0:T(8,128)S(1)}, u32[]{:S(2)}) copy-start(f32[16,64,128]{2,1,0:T(8,128)S(1)} %all-to-all-done) | copy-start | bytes 1572868

commit v2 on v0

v2 whole, which is shorter than its diff:
```python
import jax
import jax.numpy as jnp
from jax import lax
from jax.experimental import pallas as pl
from jax.experimental.pallas import tpu as pltpu
from jax.sharding import PartitionSpec as P

EX_DEV = 4
SUB = 4
STEP = 8
WIDE = 16
HIGHEST = lax.Precision.HIGHEST
PLAIN = (((1,), (0,)), ((), ()))
NT = (((1,), (1,)), ((), ()))
TN = (((0,), (0,)), ((), ()))
VMEM = pl.BlockSpec(memory_space=pltpu.VMEM)
SMEM = pl.BlockSpec(memory_space=pltpu.SMEM)


def split(x):
    high = x.astype(jnp.bfloat16)
    return high, (x - high.astype(jnp.float32)).astype(jnp.bfloat16)


def mm(a, b, dims=PLAIN):
    return lax.dot_general(a, b, dims, preferred_element_type=jnp.float32)


def exact(a, b, dims=PLAIN):
    return lax.dot_general(a, b, dims, precision=HIGHEST, preferred_element_type=jnp.float32)


def iota(shape, axis):
    return lax.broadcasted_iota(jnp.int32, shape, axis)


def diagonal(parts):
    zero = jnp.zeros_like(parts[0])
    return jnp.concatenate(
        [
            jnp.concatenate([x if k == l else zero for k in range(len(parts))], axis=1)
            for l, x in enumerate(parts)
        ],
        axis=0,
    )


def factors_kernel(precond_ref, left_ref, right_ref):
    layers, r = precond_ref.shape[0], precond_ref.shape[-1]
    row, col = iota((r, r), 0), iota((r, r), 1)
    order = (col == 2 * (row % (r // 2)) + row // (r // 2)).astype(jnp.float32)
    eye = (col == row).astype(jnp.float32)
    left = diagonal([exact(order, precond_ref[l, 0], NT) for l in range(layers)])
    left_ref[...] = jnp.concatenate(split(left), axis=0)
    turned = [exact(eye, precond_ref[l, 1], NT) for l in range(layers)]
    high, low = split(diagonal([jnp.concatenate([x, x], axis=1) for x in turned]))
    right_ref[...] = jnp.concatenate([high, high, low], axis=0)


def outputs_kernel(len_ref, grad_ref, w_ref, left_ref, out_ref, raw_ref):
    nb, size, layers, depth = grad_ref.shape
    width = left_ref.shape[1]
    rows = STEP * size
    lane_layer = iota((rows, width), 1) // (width // layers)
    slot = iota((size, width), 0)

    def turn(i, carry):
        grads = grad_ref[pl.ds(i * STEP, STEP)].reshape(rows * layers, depth)
        raw_ref[...] = mm(grads, w_ref[...], NT)
        out = raw_ref[pl.ds(0, rows, stride=layers), :]
        for l in range(1, layers):
            out = jnp.where(lane_layer == l, raw_ref[pl.ds(l, rows, stride=layers), :], out)
        live = jnp.concatenate([slot < len_ref[i * STEP + j] for j in range(STEP)], axis=0)
        high, low = split(jnp.where(live, out, 0.0))
        both = mm(left_ref[...], high, NT)
        done = both[:width] + both[width:] + mm(left_ref[:width], low, NT)
        here = pl.ds(pl.multiple_of(i * rows, rows), rows)
        out_ref[0, :, here], out_ref[1, :, here] = split(done)
        return carry

    lax.fori_loop(0, nb // STEP, turn, 0)


def features_kernel(act_ref, out_ref, w_ref, right_ref, feat_ref, whole_ref, in_ref):
    nb, size, depth = act_ref.shape
    width = out_ref.shape[1]
    layers = right_ref.shape[1] // feat_ref.shape[2]
    r = width // layers
    half = r // 2
    rows = SUB * size
    low_lane = iota((half, 2 * r), 1) < r
    lane_block = iota((r, rows), 1) // size

    def finish(i):
        high, low = split(in_ref[i % 2])
        proj_in = mm(jnp.concatenate([high, low], axis=1), right_ref[: 2 * width])
        proj_in = proj_in + mm(high, right_ref[2 * width :])
        for s in range(WIDE // SUB):
            start = (i * WIDE + s * SUB) * size
            for l in range(layers):
                outs = [out_ref[k, l * r : (l + 1) * r, start : start + rows] for k in (0, 1)]
                ih, il = split(proj_in[s * rows : (s + 1) * rows, l * 2 * r : (l + 1) * 2 * r])
                lhs = jnp.concatenate(
                    [
                        jnp.concatenate(
                            [jnp.where(lane_block == j, o, jnp.zeros_like(o)) for o in outs], axis=1
                        )
                        for j in range(SUB)
                    ],
                    axis=0,
                )
                rhs = jnp.concatenate(
                    [
                        jnp.concatenate([ih, il], axis=1),
                        jnp.concatenate([ih, jnp.zeros_like(il)], axis=1),
                    ],
                    axis=0,
                )
                got = mm(lhs, rhs)
                got = got[:, : 2 * r] + got[:, 2 * r :]
                for j in range(SUB):
                    b = i * WIDE + s * SUB + j
                    whole_ref[pl.ds(l * half * nb + b, half, stride=nb), :] = jnp.where(
                        low_lane, got[j * r : j * r + half], got[j * r + half : (j + 1) * r]
                    )

    for i in range(nb // WIDE):
        acts = act_ref[pl.ds(i * WIDE, WIDE)].reshape(WIDE * size, depth)
        in_ref[i % 2] = mm(acts, w_ref[...])
        if i > 0:
            finish(i - 1)
    finish(nb // WIDE - 1)
    for g in range(layers * half):
        feat_ref[g, :nb], feat_ref[g, nb:] = split(whole_ref[g * nb : (g + 1) * nb, :])


def scores_kernel(ex_count, tok_count, own, masks, place_ref, id_ref, first_ref, second_ref, feat_ref, out_ref):
    groups, nb, lanes = feat_ref.shape
    nb = nb // 2
    count = own * len(masks)
    acc = jnp.zeros((2 * nb, 2 * count), jnp.float32)
    for g in range(0, groups, 2):
        here = slice(g * lanes, (g + 2) * lanes)
        parts = [split(ref[:, here]) for ref in (first_ref, second_ref)]
        q = jnp.concatenate([p[k] for k in (0, 1) for p in parts], axis=0)
        acc = acc + mm(jnp.concatenate([feat_ref[g], feat_ref[g + 1]], axis=1), q, NT)
    acc = acc[:nb] + acc[nb:]
    acc = acc[:, :count] + acc[:, count:]

    queries = own * ex_count
    piece = iota((count, queries), 0) // own
    mask = jnp.zeros((count, queries), jnp.int32)
    for k, m in enumerate(masks):
        mask = jnp.where(piece == k, m, mask)
    query = jnp.bitwise_xor(mask, place_ref[0]) * own + iota((count, queries), 0) % own
    order = (query == iota((count, queries), 1)).astype(jnp.bfloat16)
    high, low = split(acc)
    acc = mm(high, order) + mm(low, order)
    targets = ex_count * tok_count * EX_DEV
    lane = iota((nb, targets), 1)
    owner = lane // EX_DEV // tok_count * EX_DEV + lane % EX_DEV == id_ref[...]
    owner = owner.astype(jnp.float32).astype(jnp.bfloat16)
    high, low = split(acc)
    full = mm(owner, high, TN) + mm(owner, low, TN)
    each = queries // tok_count
    tok = iota((targets, each), 0) // EX_DEV % tok_count
    result = full[:, :each]
    for t in range(1, tok_count):
        result = jnp.where(tok == t, full[:, t * each : (t + 1) * each], result)
    out_ref[...] = result


def on_device(
    activations,
    out_grads,
    block_len,
    block_dest,
    block_slot,
    in_proj,
    out_proj,
    query_grads,
    precond,
):
    nb, size, depth = activations.shape
    layers, grad_depth, r = out_proj.shape
    half = r // 2
    ex_count, tok_count = lax.axis_size("ex"), lax.axis_size("tok")
    own = query_grads.shape[0]
    place = lax.axis_index("ex").astype(jnp.int32)

    def swapped(x, mask):
        return lax.ppermute(x, "ex", [(i, i ^ mask) for i in range(ex_count)])

    width = layers * r
    left, right = pl.pallas_call(
        factors_kernel,
        out_shape=[
            jax.ShapeDtypeStruct((2 * width, width), jnp.bfloat16),
            jax.ShapeDtypeStruct((3 * width, 2 * width), jnp.bfloat16),
        ],
        compiler_params=pltpu.CompilerParams(vmem_limit_bytes=4 * 1024 * 1024),
        cost_estimate=pl.CostEstimate(flops=10**10, bytes_accessed=2**20, transcendentals=0),
        name="factors",
    )(precond)
    outs = pl.pallas_call(
        outputs_kernel,
        in_specs=[SMEM, VMEM, pl.BlockSpec(), pl.BlockSpec()],
        out_shape=jax.ShapeDtypeStruct((2, width, nb * size), jnp.bfloat16),
        scratch_shapes=[pltpu.VMEM((STEP * size * layers, width), jnp.float32)],
        compiler_params=pltpu.CompilerParams(vmem_limit_bytes=8 * 1024 * 1024),
        cost_estimate=pl.CostEstimate(flops=10**10, bytes_accessed=2**20, transcendentals=0),
        name="outputs",
    )(block_len, out_grads, jnp.swapaxes(out_proj, 1, 2).reshape(width, grad_depth), left)

    held = [(0, query_grads)]
    bit = ex_count // 2
    while bit > 4:
        held = held + [(mask ^ bit, swapped(x, bit)) for mask, x in held]
        bit //= 2
    last = [bit] if bit == 2 else [4, 2, 6] if bit == 4 else []
    far = [(mask, lax.optimization_barrier((x, outs))[0]) for mask, x in held[1:]]
    held = held + [(m, swapped(query_grads, m)) for m in last]
    held = held + [(mask ^ m, swapped(x, m)) for mask, x in far for m in last]

    feats = pl.pallas_call(
        features_kernel,
        in_specs=[VMEM, pl.BlockSpec(), VMEM, pl.BlockSpec()],
        out_shape=jax.ShapeDtypeStruct((layers * half, 2 * nb, 2 * r), jnp.bfloat16),
        scratch_shapes=[
            pltpu.VMEM((layers * half * nb, 2 * r), jnp.float32),
            pltpu.VMEM((2, WIDE * size, width), jnp.float32),
        ],
        compiler_params=pltpu.CompilerParams(vmem_limit_bytes=12 * 1024 * 1024),
        cost_estimate=pl.CostEstimate(flops=10**10, bytes_accessed=2**20, transcendentals=0),
        name="features",
    )(activations, outs, in_proj, right)

    masks = [mask for mask, _ in held]
    first = jnp.concatenate([x for _, x in held], axis=0)
    first, feats = lax.optimization_barrier((first, feats))
    second = swapped(first, 1)
    masks = tuple(masks + [mask ^ 1 for mask in masks])

    each = own * ex_count // tok_count
    chunks = pl.pallas_call(
        lambda *refs: scores_kernel(ex_count, tok_count, own, masks, *refs),
        in_specs=[SMEM] + [pl.BlockSpec()] * 4,
        out_shape=jax.ShapeDtypeStruct((ex_count * tok_count * EX_DEV, each), jnp.float32),
        compiler_params=pltpu.CompilerParams(vmem_limit_bytes=12 * 1024 * 1024),
        name="scores",
    )(place[None], block_dest * EX_DEV + block_slot[:, None], first, second, feats)
    chunks = chunks.reshape(ex_count * tok_count, EX_DEV, each)
    arrived = lax.all_to_all(chunks, ("ex", "tok"), split_axis=0, concat_axis=0, tiled=True)
    return jnp.sum(arrived, axis=0).T * (1.0 / (r * size))


def solution(mesh):
    placed = (
        P(("ex", "tok"), None, None),
        P(("ex", "tok"), None, None, None),
        P(("ex", "tok")),
        P(("ex", "tok"), None),
        P(("ex", "tok")),
        P(),
        P(),
        P("ex", None),
        P(),
    )
    return jax.shard_map(
        on_device, mesh=mesh, in_specs=placed, out_specs=P("tok", "ex"), check_vma=False
    )
```

time: 94.1 us -> 35.9 us (0.38)
  waiting for transfers between devices: 37.1 us -> 2.36 us
  matrix products: 16.6 us -> 0 us
  between operations: 13.5 us -> 0.17 us
  blocking collectives: 0 us -> 10.7 us
  Pallas kernels: 0 us -> 9.13 us
  local copies, waits for them, and re-layouts: 9.68 us -> 1.65 us
  starting transfers between devices: 13.7 us -> 11.1 us
  other arithmetic: 3.06 us -> 0.63 us
    all_gather x1 -> x0, waiting for transfers between devices: 25.2 us -> none  [on_device(): lax.all_gather(conditioned, 'ex', axis=0, tiled=True)]
    dot_general x9 -> x0, matrix products: 16.6 us -> none  [the longest x1 5.03 us: on_device(): jnp.dot(activations.reshape(block_count * block_size, -1), in_proj, prefe...]
    all_to_all x2 -> x0, starting transfers between devices: 13.4 us -> none  [the longest x1 7.39 us: on_device(): lax.all_to_all(outgoing_hot, 'ex', split_axis=0, concat_axis=0, tiled=True)]
    unnamed x3 -> x0, waiting for transfers between devices: 11.8 us -> none
    ppermute x0 -> x8, starting transfers between devices: none -> 11.1 us  [swapped(): return lax.ppermute(x, 'ex', [(i, i ^ mask) for i in range(ex_count)])]
    all_to_all x0 -> x1, blocking collectives: none -> 10.7 us  [on_device(): lax.all_to_all(chunks, ('ex', 'tok'), split_axis=0, concat_axis=0, tiled=...]
    pallas_call x0 -> x4, Pallas kernels: none -> 9.13 us  [the longest x1 4.1 us: on_device(): pl.pallas_call(features_kernel, in_specs=[VMEM, pl.BlockSpec(), VMEM, pl....]
    unnamed x9 -> x20, local copies, waits for them, and re-layouts: 6.21 us -> 1.15 us
  transfers between devices with their start and end apart: 4 -> 8, of which waited for: 2 -> 2; matrix products, arithmetic and copies ran while one was open for 23% -> 0% of each run, Pallas kernels for 0% -> 23%
where the time goes in v2:
time: 35.9 us; the launch traced here: 35.8 us
  starting transfers between devices  11.1 us (31%)
  blocking collectives  10.7 us (30%)
  Pallas kernels  9.13 us (25%)
  waiting for transfers between devices  2.36 us (7%)
  local copies, waits for them, and re-layouts  1.65 us (5%)
  other arithmetic  0.63 us (2%)
    ppermute x8, starting transfers between devices, swapped(): return lax.ppermute(x, 'ex', [(i, i ^ mask) for i in range(ex_count)])  11.1 us
    all_to_all x1, blocking collectives, on_device(): lax.all_to_all(chunks, ('ex', 'tok'), split_axis=0, concat_axis=0, tiled=...  10.7 us
    pallas_call x1, Pallas kernels, on_device(): pl.pallas_call(features_kernel, in_specs=[VMEM, pl.BlockSpec(), VMEM, pl....  4.1 us
    pallas_call x1, Pallas kernels, on_device(): pl.pallas_call(outputs_kernel, in_specs=[SMEM, VMEM, pl.BlockSpec(), pl.B...  3.67 us
    ppermute x8, waiting for transfers between devices, swapped(): return lax.ppermute(x, 'ex', [(i, i ^ mask) for i in range(ex_count)])  2.36 us
    unnamed x20, local copies, waits for them, and re-layouts  1.15 us
    pallas_call x1, Pallas kernels, on_device(): pl.pallas_call(lambda *refs: scores_kernel(ex_count, tok_count, own, mask...  0.95 us
  transfers between devices with their start and end apart: 8, of which 2 were waited for; matrix products, arithmetic and copies ran while one was open for 0% of the time, Pallas kernels for 23%

profile of v2, /device:TPU:0, one launch (start us, length us, event | category | flops | bytes accessed | tf_op | source)
XLA Modules:
  0.0 35.8 jit_solution(11149963267687308825)
XLA Ops:
  0.0 0.0 copy-start.2
  0.0 0.0 copy-start
  0.0 4.0 %collective-permute-start = (f32[2,8192]{1,0:T(2,128)}, f32[2,8192]{1,0:T(2,128)S(1)}, u32[]{:S(2)}, u32[]{:S(2)}) collective-permute-start(f32[2,8192]{1,0:T(2,128)} %param.16), channel_id=1, source_target_pairs={{0,16},{2,18},{4,20},{6,22},{8,24},{10,26},{12,28},{14,30},{16,0},... | collective-permute-start | bytes 196616 | tf_op jit(solution)/shard_map/ppermute | solution.py:192
  4.0 1.6 %collective-permute-start.1 = (f32[2,8192]{1,0:T(2,128)}, f32[2,8192]{1,0:T(2,128)S(1)}, u32[]{:S(2)}, u32[]{:S(2)}) collective-permute-start(f32[2,8192]{1,0:T(2,128)} %param.16), channel_id=1, source_target_pairs={{0,8},{2,10},{4,12},{6,14},{8,0},{10,2},{12,4},{14,6},{16,24},{18,... | collective-permute-start | bytes 196616 | tf_op jit(solution)/shard_map/ppermute | solution.py:192
  5.6 1.5 %collective-permute-start.2 = (f32[2,8192]{1,0:T(2,128)}, f32[2,8192]{1,0:T(2,128)S(1)}, u32[]{:S(2)}, u32[]{:S(2)}) collective-permute-start(f32[2,8192]{1,0:T(2,128)} %param.16), channel_id=1, source_target_pairs={{0,4},{2,6},{4,0},{6,2},{8,12},{10,14},{12,8},{14,10},{16,20},{18,... | collective-permute-start | bytes 196616 | tf_op jit(solution)/shard_map/ppermute | solution.py:192
  7.1 0.4 %collective-permute-start.3 = (f32[2,8192]{1,0:T(2,128)}, f32[2,8192]{1,0:T(2,128)S(1)}, u32[]{:S(2)}, u32[]{:S(2)}) collective-permute-start(f32[2,8192]{1,0:T(2,128)} %param.16), channel_id=1, source_target_pairs={{0,12},{2,14},{4,8},{6,10},{8,4},{10,6},{12,0},{14,2},{16,28},{18,... | collective-permute-start | bytes 196616 | tf_op jit(solution)/shard_map/ppermute | solution.py:192
  7.5 0.0 copy-start.3
  7.5 0.9 %copy-done.3 = f32[2,2,64,64]{3,2,1,0:T(8,128)S(1)} copy-done((f32[2,2,64,64]{3,2,1,0:T(8,128)S(1)}, f32[2,2,64,64]{3,2,1,0:T(8,128)}, u32[]{:S(2)}) %copy-start.3) | copy-done | bytes 65560
  8.4 0.0 copy-start.4
  8.4 0.0 slice-start
  8.4 0.4 %factors.1 = (bf16[256,128]{1,0:T(8,128)(2,1)S(1)}, bf16[384,256]{1,0:T(8,128)(2,1)S(1)}) custom-call(f32[2,2,64,64]{3,2,1,0:T(8,128)S(1)} %copy-done.3), custom_call_target="tpu_custom_call" | custom-call | flops 10000000000 | bytes 1048576 | tf_op jit(solution)/shard_map/factors/pallas_call | solution.py:195
  8.9 0.0 slice-start.1
  8.9 0.0 copy-done.2
  8.9 0.0 copy-done
  8.9 0.2 copy-done.4
  9.1 0.0 copy-start.1
  9.1 3.7 %outputs.1.out_ref = bf16[2,128,1024]{2,1,0:T(8,128)(2,1)S(1)} custom-call(s32[32]{0:T(128)S(1)} %copy-done.4, bf16[32,32,2,1024]{3,2,1,0:T(2,128)(2,1)S(1)} %copy-done, bf16[128,1024]{1,0:T(8,128)(2,1)S(1)} %bitcast.12, bf16[256,128]{1,0:T(8,128)(2,1)S(1)} %get-tuple-element.10.left_ref), custom_call_target="tpu_custom_call" | custom-call | flops 10000000000 | bytes 1048576 | tf_op jit(solution)/shard_map/outputs/pallas_call | solution.py:205
  12.8 0.0 collective-permute-done
  12.8 1.6 %collective-permute-start.4 = (f32[2,8192]{1,0:T(2,128)S(1)}, f32[2,8192]{1,0:T(2,128)S(1)}, u32[]{:S(2)}, u32[]{:S(2)}) collective-permute-start(f32[2,8192]{1,0:T(2,128)S(1)} %collective-permute-done), channel_id=1, source_target_pairs={{0,8},{2,10},{4,12},{6,14},{8,0},{10,2},{12,4},{14,6},{16,24},{18,... | collective-permute-start | bytes 196616 | tf_op jit(solution)/shard_map/ppermute | solution.py:192
  14.4 1.5 %collective-permute-start.5 = (f32[2,8192]{1,0:T(2,128)S(1)}, f32[2,8192]{1,0:T(2,128)S(1)}, u32[]{:S(2)}, u32[]{:S(2)}) collective-permute-start(f32[2,8192]{1,0:T(2,128)S(1)} %collective-permute-done), channel_id=1, source_target_pairs={{0,4},{2,6},{4,0},{6,2},{8,12},{10,14},{12,8},{14,10},{16,20},{18,... | collective-permute-start | bytes 196616 | tf_op jit(solution)/shard_map/ppermute | solution.py:192
  15.9 0.0 collective-permute-done.1
  15.9 0.4 %collective-permute-start.6 = (f32[2,8192]{1,0:T(2,128)S(1)}, f32[2,8192]{1,0:T(2,128)S(1)}, u32[]{:S(2)}, u32[]{:S(2)}) collective-permute-start(f32[2,8192]{1,0:T(2,128)S(1)} %collective-permute-done), channel_id=1, source_target_pairs={{0,12},{2,14},{4,8},{6,10},{8,4},{10,6},{12,0},{14,2},{16,28},{18,... | collective-permute-start | bytes 196616 | tf_op jit(solution)/shard_map/ppermute | solution.py:192
  16.3 0.0 slice-done
  16.3 0.0 slice-done.1
  16.3 0.0 copy-done.1
  16.4 0.0 copy-start.5
  16.4 0.0 copy-start.6
  16.4 0.0 copy-start.7
  16.4 4.1 %features.1.refs_4_ = bf16[64,64,128]{2,1,0:T(8,128)(2,1)S(1)} custom-call(bf16[32,32,4096]{2,1,0:T(8,128)(2,1)S(1)} %bitcast.11, bf16[2,128,1024]{2,1,0:T(8,128)(2,1)S(1)} %outputs.1.out_ref, bf16[4096,128]{1,0:T(8,128)(2,1)S(1)} %copy-done.1, bf16[384,256]{1,0:T(8,128)(2,1)S(1)} %get-tuple-element.12.right_ref), custom_call_target="tpu_custom_call" | custom-call | flops 10000000000 | bytes 1048576 | tf_op jit(solution)/shard_map/features/pallas_call | solution.py:225
  20.5 0.0 collective-permute-done.2
  20.5 0.0 collective-permute-done.3
  20.5 0.0 collective-permute-done.4
  20.5 0.0 collective-permute-done.5
  20.5 0.6 %collective-permute-done.6 = f32[2,8192]{1,0:T(2,128)S(1)} collective-permute-done((f32[2,8192]{1,0:T(2,128)S(1)}, f32[2,8192]{1,0:T(2,128)S(1)}, u32[]{:S(2)}, u32[]{:S(2)}) %collective-permute-start.6) | collective-permute-done | bytes 65568 | tf_op jit(solution)/shard_map/ppermute | solution.py:192
  21.1 0.0 copy-done.5
  21.1 0.4 %concatenate.3.refs_2_ = f32[16,8192]{1,0:T(8,128)S(1)} concatenate(f32[2,8192]{1,0:T(2,128)S(1)} %copy-done.5, f32[2,8192]{1,0:T(2,128)S(1)} %collective-permute-done, f32[2,8192]{1,0:T(2,128)S(1)} %collective-permute-done.1, f32[2,8192]{1,0:T(2,128)S(1)} %collective-permute-done.2, f32[2,8192]{1,0:T(2,128)S(1)} %collective-permute-done.3, ...), dimensions={0} | concatenate | bytes 1048576 | tf_op jit(solution)/shard_map/concatenate | solution.py:239
  21.5 0.1 collective-permute-start.7
  21.6 0.0 copy-done.6
  21.6 0.0 copy-done.7
  21.6 0.1 copy.13.refs_1_
  21.7 1.8 %collective-permute-done.7.refs_3_ = f32[16,8192]{1,0:T(8,128)S(1)} collective-permute-done((f32[16,8192]{1,0:T(8,128)S(1)}, f32[16,8192]{1,0:T(8,128)S(1)}, u32[]{:S(2)}, u32[]{:S(2)}) %collective-permute-start.7) | collective-permute-done | bytes 524320 | tf_op jit(solution)/shard_map/ppermute | solution.py:192
  23.5 1.0 %scores.1 = f32[128,16]{1,0:T(8,128)S(1)} custom-call(s32[1]{0:T(128)} %bitcast.refs_0_, s32[32,1]{1,0:T(8,128)S(1)} %copy.13.refs_1_, f32[16,8192]{1,0:T(8,128)S(1)} %concatenate.3.refs_2_, f32[16,8192]{1,0:T(8,128)S(1)} %collective-permute-done.7.refs_3_, bf16[64,64,128]{2,1,0:T(8,128)(2,1)S(1)} %features.1.refs_4_), custom_call_target="tpu_custom_call" | custom-call | tf_op jit(solution)/shard_map/scores/pallas_call | solution.py:245
  24.5 10.7 %all_to_all.5 = f32[32,4,16]{2,1,0:T(4,128)S(1)} all-to-all(f32[32,4,16]{2,1,0:T(4,128)S(1)} %bitcast.9), channel_id=1, replica_groups=mesh['ex'=16,'tok'=2] {'ex','tok'}, dimensions={0} | all-to-all | bytes 16384 | tf_op jit(solution)/shard_map/all_to_all | solution.py:253
  35.2 0.6 %multiply_bitcast_fusion = f32[16,4]{0,1:T(4,128)} fusion(f32[4,16]{1,0:T(4,128)S(1)} %reduce_sum.9), kind=kLoop, calls=%fused_computation | loop fusion | flops 64 | bytes 512 | tf_op jit(solution)/shard_map/mul | solution.py:254
  (3 shorter events, 0.1 us)
Async XLA Ops:
  0.0 8.9 %copy-start.2 = (bf16[2,1024,64]{1,2,0:T(8,128)(2,1)S(1)}, bf16[2,1024,64]{1,2,0:T(8,128)(2,1)}, u32[]{:S(2)}) copy-start(bf16[2,1024,64]{1,2,0:T(8,128)(2,1)} %param.15) | copy-start | bytes 786436
  0.0 8.9 %copy-start = (bf16[32,32,2,1024]{3,2,1,0:T(2,128)(2,1)S(1)}, bf16[32,32,2,1024]{3,2,1,0:T(2,128)(2,1)}, u32[]{:S(2)}) copy-start(bf16[32,32,2,1024]{3,2,1,0:T(2,128)(2,1)} %grad_ref.1) | copy-start | bytes 12582916
  0.0 12.8 %collective-permute-start = (f32[2,8192]{1,0:T(2,128)}, f32[2,8192]{1,0:T(2,128)S(1)}, u32[]{:S(2)}, u32[]{:S(2)}) collective-permute-start(f32[2,8192]{1,0:T(2,128)} %param.16), channel_id=1, source_target_pairs={{0,16},{2,18},{4,20},{6,22},{8,24},{10,26},{12,28},{14,30},{16,0},... | collective-permute-start | bytes 196616 | tf_op jit(solution)/shard_map/ppermute | solution.py:192
  4.0 11.9 %collective-permute-start.1 = (f32[2,8192]{1,0:T(2,128)}, f32[2,8192]{1,0:T(2,128)S(1)}, u32[]{:S(2)}, u32[]{:S(2)}) collective-permute-start(f32[2,8192]{1,0:T(2,128)} %param.16), channel_id=1, source_target_pairs={{0,8},{2,10},{4,12},{6,14},{8,0},{10,2},{12,4},{14,6},{16,24},{18,... | collective-permute-start | bytes 196616 | tf_op jit(solution)/shard_map/ppermute | solution.py:192
  5.6 14.9 %collective-permute-start.2 = (f32[2,8192]{1,0:T(2,128)}, f32[2,8192]{1,0:T(2,128)S(1)}, u32[]{:S(2)}, u32[]{:S(2)}) collective-permute-start(f32[2,8192]{1,0:T(2,128)} %param.16), channel_id=1, source_target_pairs={{0,4},{2,6},{4,0},{6,2},{8,12},{10,14},{12,8},{14,10},{16,20},{18,... | collective-permute-start | bytes 196616 | tf_op jit(solution)/shard_map/ppermute | solution.py:192
  7.1 13.4 %collective-permute-start.3 = (f32[2,8192]{1,0:T(2,128)}, f32[2,8192]{1,0:T(2,128)S(1)}, u32[]{:S(2)}, u32[]{:S(2)}) collective-permute-start(f32[2,8192]{1,0:T(2,128)} %param.16), channel_id=1, source_target_pairs={{0,12},{2,14},{4,8},{6,10},{8,4},{10,6},{12,0},{14,2},{16,28},{18,... | collective-permute-start | bytes 196616 | tf_op jit(solution)/shard_map/ppermute | solution.py:192
  7.5 0.9 %copy-start.3 = (f32[2,2,64,64]{3,2,1,0:T(8,128)S(1)}, f32[2,2,64,64]{3,2,1,0:T(8,128)}, u32[]{:S(2)}) copy-start(f32[2,2,64,64]{3,2,1,0:T(8,128)} %precond_ref.1) | copy-start | bytes 196612
  8.4 0.7 %copy-start.4 = (s32[32]{0:T(128)S(1)}, s32[32]{0:T(128)}, u32[]{:S(2)}) copy-start(s32[32]{0:T(128)} %len_ref.1) | copy-start | bytes 388
  8.4 7.9 %slice-start = ((s8[8388608]{0:T(1024)(128)(4,1)}), s8[4194304]{0:T(1024)(128)(4,1)S(1)}, s32[]{:S(2)}) async-start(s8[8388608]{0:T(1024)(128)(4,1)} %bitcast.10), calls=%async_computation.1 | async-start | bytes 8388608
  8.9 7.5 %slice-start.1 = ((s8[8388608]{0:T(1024)(128)(4,1)}), s8[4194304]{0:T(1024)(128)(4,1)S(1)}, s32[]{:S(2)}) async-start(s8[8388608]{0:T(1024)(128)(4,1)} %bitcast.10), calls=%async_computation.2 | async-start | bytes 8388608
  9.1 7.3 %copy-start.1 = (bf16[4096,128]{1,0:T(8,128)(2,1)S(1)}, bf16[4096,128]{1,0:T(8,128)(2,1)}, u32[]{:S(2)}) copy-start(bf16[4096,128]{1,0:T(8,128)(2,1)} %w_ref.1) | copy-start | bytes 3145732
  12.8 7.7 %collective-permute-start.4 = (f32[2,8192]{1,0:T(2,128)S(1)}, f32[2,8192]{1,0:T(2,128)S(1)}, u32[]{:S(2)}, u32[]{:S(2)}) collective-permute-start(f32[2,8192]{1,0:T(2,128)S(1)} %collective-permute-done), channel_id=1, source_target_pairs={{0,8},{2,10},{4,12},{6,14},{8,0},{10,2},{12,4},{14,6},{16,24},{18,... | collective-permute-start | bytes 196616 | tf_op jit(solution)/shard_map/ppermute | solution.py:192
  14.4 6.1 %collective-permute-start.5 = (f32[2,8192]{1,0:T(2,128)S(1)}, f32[2,8192]{1,0:T(2,128)S(1)}, u32[]{:S(2)}, u32[]{:S(2)}) collective-permute-start(f32[2,8192]{1,0:T(2,128)S(1)} %collective-permute-done), channel_id=1, source_target_pairs={{0,4},{2,6},{4,0},{6,2},{8,12},{10,14},{12,8},{14,10},{16,20},{18,... | collective-permute-start | bytes 196616 | tf_op jit(solution)/shard_map/ppermute | solution.py:192
  15.9 5.2 %collective-permute-start.6 = (f32[2,8192]{1,0:T(2,128)S(1)}, f32[2,8192]{1,0:T(2,128)S(1)}, u32[]{:S(2)}, u32[]{:S(2)}) collective-permute-start(f32[2,8192]{1,0:T(2,128)S(1)} %collective-permute-done), channel_id=1, source_target_pairs={{0,12},{2,14},{4,8},{6,10},{8,4},{10,6},{12,0},{14,2},{16,28},{18,... | collective-permute-start | bytes 196616 | tf_op jit(solution)/shard_map/ppermute | solution.py:192
  16.4 4.8 %copy-start.5 = (f32[2,8192]{1,0:T(2,128)S(1)}, f32[2,8192]{1,0:T(2,128)}, u32[]{:S(2)}) copy-start(f32[2,8192]{1,0:T(2,128)} %param.16) | copy-start | bytes 196612
  16.4 5.2 %copy-start.6 = (s32[32]{0:T(128)S(1)}, s32[32]{0:T(128)}, u32[]{:S(2)}) copy-start(s32[32]{0:T(128)} %param.13) | copy-start | bytes 388
  16.4 5.2 %copy-start.7 = (s32[32,1]{0,1:T(1,128)S(1)}, s32[32,1]{0,1:T(1,128)}, u32[]{:S(2)}) copy-start(s32[32,1]{0,1:T(1,128)} %param.12) | copy-start | bytes 388
  21.5 2.0 %collective-permute-start.7 = (f32[16,8192]{1,0:T(8,128)S(1)}, f32[16,8192]{1,0:T(8,128)S(1)}, u32[]{:S(2)}, u32[]{:S(2)}) collective-permute-start(f32[16,8192]{1,0:T(8,128)S(1)} %concatenate.3.refs_2_), channel_id=1, source_target_pairs={{0,2},{2,0},{4,6},{6,4},{8,10},{10,8},{12,14},{14,12},{16,18},{18,... | collective-permute-start | bytes 1572872 | tf_op jit(solution)/shard_map/ppermute | solution.py:192

commit v3 on v2

--- a/solution.py
+++ b/solution.py
@@ -81,10 +81,10 @@
     lax.fori_loop(0, nb // STEP, turn, 0)
 
 
-def features_kernel(act_ref, out_ref, w_ref, right_ref, feat_ref, whole_ref, in_ref):
+def features_kernel(dest_ref, slot_ref, act_ref, out_ref, w_ref, right_ref, feat_ref, in_ref):
     nb, size, depth = act_ref.shape
     width = out_ref.shape[1]
-    layers = right_ref.shape[1] // feat_ref.shape[2]
+    layers = right_ref.shape[1] // feat_ref.shape[1]
     r = width // layers
     half = r // 2
     rows = SUB * size
@@ -120,7 +120,7 @@
                 got = got[:, : 2 * r] + got[:, 2 * r :]
                 for j in range(SUB):
                     b = i * WIDE + s * SUB + j
-                    whole_ref[pl.ds(l * half * nb + b, half, stride=nb), :] = jnp.where(
+                    feat_ref[pl.ds(l * half * nb + b, half, stride=nb), :] = jnp.where(
                         low_lane, got[j * r : j * r + half], got[j * r + half : (j + 1) * r]
                     )
 
@@ -130,22 +130,36 @@
         if i > 0:
             finish(i - 1)
     finish(nb // WIDE - 1)
-    for g in range(layers * half):
-        feat_ref[g, :nb], feat_ref[g, nb:] = split(whole_ref[g * nb : (g + 1) * nb, :])
-
-
-def scores_kernel(ex_count, tok_count, own, masks, place_ref, id_ref, first_ref, second_ref, feat_ref, out_ref):
-    groups, nb, lanes = feat_ref.shape
-    nb = nb // 2
-    count = own * len(masks)
+    for b in range(nb):
+        example = (dest_ref[b] * EX_DEV + slot_ref[b]).astype(jnp.float32)
+        feat_ref[pl.ds(layers * half * nb + b, 1), :] = jnp.full((1, 2 * r), example)
+
+
+def products(pieces, feat_ref):
+    lanes = feat_ref.shape[1]
+    groups = pieces[0].shape[1] // lanes
+    nb = feat_ref.shape[0] // (groups + 1)
+    count = sum(ref.shape[0] for ref in pieces)
     acc = jnp.zeros((2 * nb, 2 * count), jnp.float32)
     for g in range(0, groups, 2):
-        here = slice(g * lanes, (g + 2) * lanes)
-        parts = [split(ref[:, here]) for ref in (first_ref, second_ref)]
-        q = jnp.concatenate([p[k] for k in (0, 1) for p in parts], axis=0)
-        acc = acc + mm(jnp.concatenate([feat_ref[g], feat_ref[g + 1]], axis=1), q, NT)
+        q = jnp.concatenate([ref[:, g * lanes : (g + 2) * lanes] for ref in pieces], axis=0)
+        f = [feat_ref[(g + d) * nb : (g + d + 1) * nb, :] for d in (0, 1)]
+        f = jnp.concatenate(f, axis=1)
+        q, f = [jnp.concatenate(split(x), axis=0) for x in (q, f)]
+        acc = acc + mm(f, q, NT)
     acc = acc[:nb] + acc[nb:]
-    acc = acc[:, :count] + acc[:, count:]
+    return acc[:, :count] + acc[:, count:]
+
+
+def own_scores_kernel(*refs):
+    *pieces, mine_ref, out_ref = refs
+    out_ref[...] = products(pieces, mine_ref)
+
+
+def scores_kernel(ex_count, tok_count, own, masks, place_ref, *refs):
+    *pieces, own_ref, dest_ref, other_ref, out_ref = refs
+    acc = jnp.concatenate([own_ref[...], products(pieces, other_ref)], axis=0)
+    blocks, count = acc.shape
 
     queries = own * ex_count
     piece = iota((count, queries), 0) // own
@@ -153,12 +167,14 @@
     for k, m in enumerate(masks):
         mask = jnp.where(piece == k, m, mask)
     query = jnp.bitwise_xor(mask, place_ref[0]) * own + iota((count, queries), 0) % own
-    order = (query == iota((count, queries), 1)).astype(jnp.bfloat16)
+    order = (query == iota((count, queries), 1)).astype(jnp.float32).astype(jnp.bfloat16)
     high, low = split(acc)
     acc = mm(high, order) + mm(low, order)
     targets = ex_count * tok_count * EX_DEV
-    lane = iota((nb, targets), 1)
-    owner = lane // EX_DEV // tok_count * EX_DEV + lane % EX_DEV == id_ref[...]
+    lane = iota((blocks, targets), 1)
+    ids = [ref[ref.shape[0] - blocks // 2 :, :1] for ref in (dest_ref, other_ref)]
+    ids = jnp.concatenate(ids, axis=0).astype(jnp.int32)
+    owner = lane // EX_DEV // tok_count * EX_DEV + lane % EX_DEV == ids
     owner = owner.astype(jnp.float32).astype(jnp.bfloat16)
     high, low = split(acc)
     full = mm(owner, high, TN) + mm(owner, low, TN)
@@ -212,43 +228,44 @@
         name="outputs",
     )(block_len, out_grads, jnp.swapaxes(out_proj, 1, 2).reshape(width, grad_depth), left)
 
-    held = [(0, query_grads)]
+    held, masks = query_grads, [0]
     bit = ex_count // 2
     while bit > 4:
-        held = held + [(mask ^ bit, swapped(x, bit)) for mask, x in held]
+        held = jnp.concatenate([held, swapped(held, bit)], axis=0)
+        masks = masks + [mask ^ bit for mask in masks]
         bit //= 2
-    last = [bit] if bit == 2 else [4, 2, 6] if bit == 4 else []
-    far = [(mask, lax.optimization_barrier((x, outs))[0]) for mask, x in held[1:]]
-    held = held + [(m, swapped(query_grads, m)) for m in last]
-    held = held + [(mask ^ m, swapped(x, m)) for mask, x in far for m in last]
-
-    feats = pl.pallas_call(
+    last = [bit] if bit == 2 else [2, 4, 6] if bit == 4 else []
+    held, outs = lax.optimization_barrier((held, outs))
+    pieces = [held] + [swapped(held, m) for m in last]
+    masks = tuple(mask ^ m for m in [0] + last for mask in masks)
+
+    mine = pl.pallas_call(
         features_kernel,
-        in_specs=[VMEM, pl.BlockSpec(), VMEM, pl.BlockSpec()],
-        out_shape=jax.ShapeDtypeStruct((layers * half, 2 * nb, 2 * r), jnp.bfloat16),
-        scratch_shapes=[
-            pltpu.VMEM((layers * half * nb, 2 * r), jnp.float32),
-            pltpu.VMEM((2, WIDE * size, width), jnp.float32),
-        ],
+        in_specs=[SMEM, SMEM, VMEM, pl.BlockSpec(), VMEM, pl.BlockSpec()],
+        out_shape=jax.ShapeDtypeStruct(((layers * half + 1) * nb, 2 * r), jnp.float32),
+        scratch_shapes=[pltpu.VMEM((2, WIDE * size, width), jnp.float32)],
         compiler_params=pltpu.CompilerParams(vmem_limit_bytes=12 * 1024 * 1024),
         cost_estimate=pl.CostEstimate(flops=10**10, bytes_accessed=2**20, transcendentals=0),
         name="features",
-    )(activations, outs, in_proj, right)
-
-    masks = [mask for mask, _ in held]
-    first = jnp.concatenate([x for _, x in held], axis=0)
-    first, feats = lax.optimization_barrier((first, feats))
-    second = swapped(first, 1)
-    masks = tuple(masks + [mask ^ 1 for mask in masks])
+    )(block_dest[:, 0], block_slot, activations, outs, in_proj, right)
+
+    other = swapped(mine, 1)
 
     each = own * ex_count // tok_count
+    own_scores = pl.pallas_call(
+        own_scores_kernel,
+        out_shape=jax.ShapeDtypeStruct((nb, own * len(masks)), jnp.float32),
+        compiler_params=pltpu.CompilerParams(vmem_limit_bytes=8 * 1024 * 1024),
+        cost_estimate=pl.CostEstimate(flops=10**10, bytes_accessed=2**20, transcendentals=0),
+        name="own_scores",
+    )(*pieces, mine)
     chunks = pl.pallas_call(
         lambda *refs: scores_kernel(ex_count, tok_count, own, masks, *refs),
-        in_specs=[SMEM] + [pl.BlockSpec()] * 4,
+        in_specs=[SMEM] + [pl.BlockSpec()] * (len(pieces) + 3),
         out_shape=jax.ShapeDtypeStruct((ex_count * tok_count * EX_DEV, each), jnp.float32),
-        compiler_params=pltpu.CompilerParams(vmem_limit_bytes=12 * 1024 * 1024),
+        compiler_params=pltpu.CompilerParams(vmem_limit_bytes=8 * 1024 * 1024),
         name="scores",
-    )(place[None], block_dest * EX_DEV + block_slot[:, None], first, second, feats)
+    )(place[None], *pieces, own_scores, mine[layers * half * nb :], other)
     chunks = chunks.reshape(ex_count * tok_count, EX_DEV, each)
     arrived = lax.all_to_all(chunks, ("ex", "tok"), split_axis=0, concat_axis=0, tiled=True)
     return jnp.sum(arrived, axis=0).T * (1.0 / (r * size))

time: 35.9 us -> 33.7 us (0.939)
  starting transfers between devices: 11.1 us -> 7.66 us
  Pallas kernels: 9.13 us -> 10.1 us
  blocking collectives: 10.7 us -> 11.6 us
  local copies, waits for them, and re-layouts: 1.65 us -> 1.16 us
    ppermute x8 -> x5, starting transfers between devices: 11.1 us -> 7.66 us  [swapped(): return lax.ppermute(x, 'ex', [(i, i ^ mask) for i in range(ex_count)])]
    pallas_call x1 -> x2, Pallas kernels: 4.1 us -> 5.07 us  [the longest x1 4.61 us: on_device(): pl.pallas_call(features_kernel, in_specs=[SMEM, SMEM, VMEM, pl.BlockSpec(...]
    all_to_all x1, blocking collectives: 10.7 us -> 11.6 us  [on_device(): lax.all_to_all(chunks, ('ex', 'tok'), split_axis=0, concat_axis=0, tiled=...]
    concatenate x1 -> x0, local copies, waits for them, and re-layouts: 0.41 us -> none  [on_device(): first = jnp.concatenate([x for _, x in held], axis=0)]
    ppermute x8 -> x5, waiting for transfers between devices: 2.36 us -> 2.18 us  [swapped(): return lax.ppermute(x, 'ex', [(i, i ^ mask) for i in range(ex_count)])]
  transfers between devices with their start and end apart: 8 -> 5, of which waited for: 2 -> 2; matrix products, arithmetic and copies ran while one was open for 0% -> 0% of each run, Pallas kernels for 23% -> 27%
where the time goes in v3:
time: 33.7 us; the launch traced here: 33.6 us
  blocking collectives  11.6 us (34%)
  Pallas kernels  10.1 us (30%)
  starting transfers between devices  7.66 us (23%)
  waiting for transfers between devices  2.18 us (6%)
  local copies, waits for them, and re-layouts  1.16 us (3%)
  other arithmetic  0.69 us (2%)
    all_to_all x1, blocking collectives, on_device(): lax.all_to_all(chunks, ('ex', 'tok'), split_axis=0, concat_axis=0, tiled=...  11.6 us
    ppermute x5, starting transfers between devices, swapped(): return lax.ppermute(x, 'ex', [(i, i ^ mask) for i in range(ex_count)])  7.66 us
    pallas_call x1, Pallas kernels, on_device(): pl.pallas_call(features_kernel, in_specs=[SMEM, SMEM, VMEM, pl.BlockSpec(...  4.61 us
    pallas_call x1, Pallas kernels, on_device(): pl.pallas_call(outputs_kernel, in_specs=[SMEM, VMEM, pl.BlockSpec(), pl.B...  3.68 us
    ppermute x5, waiting for transfers between devices, swapped(): return lax.ppermute(x, 'ex', [(i, i ^ mask) for i in range(ex_count)])  2.18 us
    unnamed x20, local copies, waits for them, and re-layouts  1.16 us
    pallas_call x1, Pallas kernels, on_device(): pl.pallas_call(lambda *refs: scores_kernel(ex_count, tok_count, own, mask...  0.95 us
  transfers between devices with their start and end apart: 5, of which 2 were waited for; matrix products, arithmetic and copies ran while one was open for 0% of the time, Pallas kernels for 27%

profile of v3, /device:TPU:0, one launch (start us, length us, event | category | flops | bytes accessed | tf_op | source)
XLA Modules:
  0.0 33.6 jit_solution(13150810955330726146)
XLA Ops:
  0.0 0.0 copy-start.2
  0.0 0.0 copy-start
  0.0 4.0 %collective-permute-start = (f32[2,8192]{1,0:T(2,128)}, f32[2,8192]{1,0:T(2,128)S(1)}, u32[]{:S(2)}, u32[]{:S(2)}) collective-permute-start(f32[2,8192]{1,0:T(2,128)} %param.16), channel_id=1, source_target_pairs={{0,16},{2,18},{4,20},{6,22},{8,24},{10,26},{12,28},{14,30},{16,0},... | collective-permute-start | bytes 196616 | tf_op jit(solution)/shard_map/ppermute | solution.py:208
  4.0 0.0 copy-start.3
  4.0 0.9 %copy-done.3 = f32[2,2,64,64]{3,2,1,0:T(8,128)S(1)} copy-done((f32[2,2,64,64]{3,2,1,0:T(8,128)S(1)}, f32[2,2,64,64]{3,2,1,0:T(8,128)}, u32[]{:S(2)}) %copy-start.3) | copy-done | bytes 65560
  4.9 0.0 copy-start.4
  4.9 0.0 slice-start
  5.0 0.4 %factors.1 = (bf16[256,128]{1,0:T(8,128)(2,1)S(1)}, bf16[384,256]{1,0:T(8,128)(2,1)S(1)}) custom-call(f32[2,2,64,64]{3,2,1,0:T(8,128)S(1)} %copy-done.3), custom_call_target="tpu_custom_call" | custom-call | flops 10000000000 | bytes 1048576 | tf_op jit(solution)/shard_map/factors/pallas_call | solution.py:211
  5.4 0.0 copy-done.2
  5.4 0.0 copy-done
  5.4 0.2 copy-done.4
  5.6 0.0 copy-start.7
  5.6 0.0 slice-start.1
  5.6 0.0 copy-start.1
  5.6 0.0 copy-start.5
  5.6 0.0 copy-start.6
  5.6 3.7 %outputs.1.out_ref = bf16[2,128,1024]{2,1,0:T(8,128)(2,1)S(1)} custom-call(s32[32]{0:T(128)S(1)} %copy-done.4, bf16[32,32,2,1024]{3,2,1,0:T(2,128)(2,1)S(1)} %copy-done, bf16[128,1024]{1,0:T(8,128)(2,1)S(1)} %bitcast.11, bf16[256,128]{1,0:T(8,128)(2,1)S(1)} %get-tuple-element.9.left_ref), custom_call_target="tpu_custom_call" | custom-call | flops 10000000000 | bytes 1048576 | tf_op jit(solution)/shard_map/outputs/pallas_call | solution.py:221
  9.3 0.0 collective-permute-done
  9.3 0.0 copy-done.7
  9.3 0.1 pad_maximum_fusion.refs_0_.refs_1_
  9.4 1.6 %collective-permute-start.1 = (f32[4,8192]{1,0:T(4,128)S(1)}, f32[4,8192]{1,0:T(4,128)S(1)}, u32[]{:S(2)}, u32[]{:S(2)}) collective-permute-start(f32[4,8192]{1,0:T(4,128)S(1)} %pad_maximum_fusion.refs_0_.refs_1_), channel_id=1, source_target_pairs={{0,4},{2,6},{4,0},{6,2},{8,12},{10,14},{12,8},{14,10},{16,20},{18,... | collective-permute-start | bytes 393224 | tf_op jit(solution)/shard_map/ppermute | solution.py:208
  11.0 1.6 %collective-permute-start.2 = (f32[4,8192]{1,0:T(4,128)S(1)}, f32[4,8192]{1,0:T(4,128)S(1)}, u32[]{:S(2)}, u32[]{:S(2)}) collective-permute-start(f32[4,8192]{1,0:T(4,128)S(1)} %pad_maximum_fusion.refs_0_.refs_1_), channel_id=1, source_target_pairs={{0,8},{2,10},{4,12},{6,14},{8,0},{10,2},{12,4},{14,6},{16,24},{18,... | collective-permute-start | bytes 393224 | tf_op jit(solution)/shard_map/ppermute | solution.py:208
  12.6 0.4 %collective-permute-start.3 = (f32[4,8192]{1,0:T(4,128)S(1)}, f32[4,8192]{1,0:T(4,128)S(1)}, u32[]{:S(2)}, u32[]{:S(2)}) collective-permute-start(f32[4,8192]{1,0:T(4,128)S(1)} %pad_maximum_fusion.refs_0_.refs_1_), channel_id=1, source_target_pairs={{0,12},{2,14},{4,8},{6,10},{8,4},{10,6},{12,0},{14,2},{16,28},{18,... | collective-permute-start | bytes 393224 | tf_op jit(solution)/shard_map/ppermute | solution.py:208
  13.0 0.0 slice-done
  13.0 0.0 slice-done.1
  13.0 0.0 copy-done.1
  13.0 0.0 copy-done.5
  13.0 0.0 copy-done.6
  13.0 4.6 %features.1.refs_4_ = f32[2080,128]{1,0:T(8,128)S(1)} custom-call(s32[32]{0:T(128)S(1)} %bitcast.12, s32[32]{0:T(128)S(1)} %copy-done.6, bf16[32,32,4096]{2,1,0:T(8,128)(2,1)S(1)} %bitcast.10, bf16[2,128,1024]{2,1,0:T(8,128)(2,1)S(1)} %outputs.1.out_ref, bf16[4096,128]{1,0:T(8,128)(2,1)S(1)} %copy-done.1, bf16[384,256]{1,0:T(8,128)(2,1)S(1)} %get-tuple-element.12.right_ref), custom_call_target="tpu_custom_call" | custom-call | flops 10000000000 | bytes 1048576 | tf_op jit(solution)/shard_map/features/pallas_call | solution.py:242
  17.6 0.1 collective-permute-start.4
  17.7 0.0 collective-permute-done.1.refs_1_.refs_2_
  17.7 0.0 collective-permute-done.2.refs_2_.refs_3_
  17.7 1.0 %collective-permute-done.3.refs_3_.refs_4_ = f32[4,8192]{1,0:T(4,128)S(1)} collective-permute-done((f32[4,8192]{1,0:T(4,128)S(1)}, f32[4,8192]{1,0:T(4,128)S(1)}, u32[]{:S(2)}, u32[]{:S(2)}) %collective-permute-start.3) | collective-permute-done | bytes 131104 | tf_op jit(solution)/shard_map/ppermute | solution.py:208
  18.7 0.5 %own_scores.1.refs_5_ = f32[32,16]{1,0:T(8,128)S(1)} custom-call(f32[4,8192]{1,0:T(4,128)S(1)} %pad_maximum_fusion.refs_0_.refs_1_, f32[4,8192]{1,0:T(4,128)S(1)} %collective-permute-done.1.refs_1_.refs_2_, f32[4,8192]{1,0:T(4,128)S(1)} %collective-permute-done.2.refs_2_.refs_3_, f32[4,8192]{1,0:T(4,128)S(1)} %collective-permute-done.3.refs_3_.refs_4_, ...), custom_call_target="tpu_custom_call" | custom-call | flops 10000000000 | bytes 1048576 | tf_op jit(solution)/shard_map/own_scores/pallas_call | solution.py:255
  19.2 1.2 %collective-permute-done.4.refs_7_ = f32[2080,128]{1,0:T(8,128)S(1)} collective-permute-done((f32[2080,128]{1,0:T(8,128)S(1)}, f32[2080,128]{1,0:T(8,128)S(1)}, u32[]{:S(2)}, u32[]{:S(2)}) %collective-permute-start.4) | collective-permute-done | bytes 1064992 | tf_op jit(solution)/shard_map/ppermute | solution.py:208
  20.4 0.9 %scores.1 = f32[128,16]{1,0:T(8,128)S(1)} custom-call(s32[1]{0:T(128)} %bitcast.refs_0_, f32[4,8192]{1,0:T(4,128)S(1)} %pad_maximum_fusion.refs_0_.refs_1_, f32[4,8192]{1,0:T(4,128)S(1)} %collective-permute-done.1.refs_1_.refs_2_, f32[4,8192]{1,0:T(4,128)S(1)} %collective-permute-done.2.refs_2_.refs_3_, ...), custom_call_target="tpu_custom_call" | custom-call | tf_op jit(solution)/shard_map/scores/pallas_call | solution.py:262
  21.3 11.6 %all_to_all.5 = f32[32,4,16]{2,1,0:T(4,128)S(1)} all-to-all(f32[32,4,16]{2,1,0:T(4,128)S(1)} %bitcast.8), channel_id=1, replica_groups=mesh['ex'=16,'tok'=2] {'ex','tok'}, dimensions={0} | all-to-all | bytes 16384 | tf_op jit(solution)/shard_map/all_to_all | solution.py:270
  33.0 0.6 %multiply_bitcast_fusion = f32[16,4]{0,1:T(4,128)} fusion(f32[4,16]{1,0:T(4,128)S(1)} %reduce_sum.9), kind=kLoop, calls=%fused_computation.1 | loop fusion | flops 64 | bytes 512 | tf_op jit(solution)/shard_map/mul | solution.py:271
  (3 shorter events, 0.0 us)
Async XLA Ops:
  0.0 5.4 %copy-start.2 = (bf16[2,1024,64]{1,2,0:T(8,128)(2,1)S(1)}, bf16[2,1024,64]{1,2,0:T(8,128)(2,1)}, u32[]{:S(2)}) copy-start(bf16[2,1024,64]{1,2,0:T(8,128)(2,1)} %param.15) | copy-start | bytes 786436
  0.0 5.4 %copy-start = (bf16[32,32,2,1024]{3,2,1,0:T(2,128)(2,1)S(1)}, bf16[32,32,2,1024]{3,2,1,0:T(2,128)(2,1)}, u32[]{:S(2)}) copy-start(bf16[32,32,2,1024]{3,2,1,0:T(2,128)(2,1)} %grad_ref.1) | copy-start | bytes 12582916
  0.0 9.3 %collective-permute-start = (f32[2,8192]{1,0:T(2,128)}, f32[2,8192]{1,0:T(2,128)S(1)}, u32[]{:S(2)}, u32[]{:S(2)}) collective-permute-start(f32[2,8192]{1,0:T(2,128)} %param.16), channel_id=1, source_target_pairs={{0,16},{2,18},{4,20},{6,22},{8,24},{10,26},{12,28},{14,30},{16,0},... | collective-permute-start | bytes 196616 | tf_op jit(solution)/shard_map/ppermute | solution.py:208
  4.0 0.9 %copy-start.3 = (f32[2,2,64,64]{3,2,1,0:T(8,128)S(1)}, f32[2,2,64,64]{3,2,1,0:T(8,128)}, u32[]{:S(2)}) copy-start(f32[2,2,64,64]{3,2,1,0:T(8,128)} %precond_ref.1) | copy-start | bytes 196612
  4.9 0.7 %copy-start.4 = (s32[32]{0:T(128)S(1)}, s32[32]{0:T(128)}, u32[]{:S(2)}) copy-start(s32[32]{0:T(128)} %len_ref.1) | copy-start | bytes 388
  4.9 8.0 %slice-start = ((s8[8388608]{0:T(1024)(128)(4,1)}), s8[4194304]{0:T(1024)(128)(4,1)S(1)}, s32[]{:S(2)}) async-start(s8[8388608]{0:T(1024)(128)(4,1)} %bitcast.9), calls=%async_computation.1 | async-start | bytes 8388608
  5.6 3.7 %copy-start.7 = (f32[2,8192]{1,0:T(2,128)S(1)}, f32[2,8192]{1,0:T(2,128)}, u32[]{:S(2)}) copy-start(f32[2,8192]{1,0:T(2,128)} %param.16) | copy-start | bytes 196612
  5.6 7.4 %slice-start.1 = ((s8[8388608]{0:T(1024)(128)(4,1)}), s8[4194304]{0:T(1024)(128)(4,1)S(1)}, s32[]{:S(2)}) async-start(s8[8388608]{0:T(1024)(128)(4,1)} %bitcast.9), calls=%async_computation.2 | async-start | bytes 8388608
  5.6 7.4 %copy-start.1 = (bf16[4096,128]{1,0:T(8,128)(2,1)S(1)}, bf16[4096,128]{1,0:T(8,128)(2,1)}, u32[]{:S(2)}) copy-start(bf16[4096,128]{1,0:T(8,128)(2,1)} %w_ref.1) | copy-start | bytes 3145732
  5.6 7.4 %copy-start.5 = (s32[32,1]{0,1:T(1,128)S(1)}, s32[32,1]{0,1:T(1,128)}, u32[]{:S(2)}) copy-start(s32[32,1]{0,1:T(1,128)} %param.12) | copy-start | bytes 388
  5.6 7.4 %copy-start.6 = (s32[32]{0:T(128)S(1)}, s32[32]{0:T(128)}, u32[]{:S(2)}) copy-start(s32[32]{0:T(128)} %slot_ref.1) | copy-start | bytes 388
  9.4 8.3 %collective-permute-start.1 = (f32[4,8192]{1,0:T(4,128)S(1)}, f32[4,8192]{1,0:T(4,128)S(1)}, u32[]{:S(2)}, u32[]{:S(2)}) collective-permute-start(f32[4,8192]{1,0:T(4,128)S(1)} %pad_maximum_fusion.refs_0_.refs_1_), channel_id=1, source_target_pairs={{0,4},{2,6},{4,0},{6,2},{8,12},{10,14},{12,8},{14,10},{16,20},{18,... | collective-permute-start | bytes 393224 | tf_op jit(solution)/shard_map/ppermute | solution.py:208
  11.0 6.7 %collective-permute-start.2 = (f32[4,8192]{1,0:T(4,128)S(1)}, f32[4,8192]{1,0:T(4,128)S(1)}, u32[]{:S(2)}, u32[]{:S(2)}) collective-permute-start(f32[4,8192]{1,0:T(4,128)S(1)} %pad_maximum_fusion.refs_0_.refs_1_), channel_id=1, source_target_pairs={{0,8},{2,10},{4,12},{6,14},{8,0},{10,2},{12,4},{14,6},{16,24},{18,... | collective-permute-start | bytes 393224 | tf_op jit(solution)/shard_map/ppermute | solution.py:208
  12.6 6.1 %collective-permute-start.3 = (f32[4,8192]{1,0:T(4,128)S(1)}, f32[4,8192]{1,0:T(4,128)S(1)}, u32[]{:S(2)}, u32[]{:S(2)}) collective-permute-start(f32[4,8192]{1,0:T(4,128)S(1)} %pad_maximum_fusion.refs_0_.refs_1_), channel_id=1, source_target_pairs={{0,12},{2,14},{4,8},{6,10},{8,4},{10,6},{12,0},{14,2},{16,28},{18,... | collective-permute-start | bytes 393224 | tf_op jit(solution)/shard_map/ppermute | solution.py:208
  17.6 2.7 %collective-permute-start.4 = (f32[2080,128]{1,0:T(8,128)S(1)}, f32[2080,128]{1,0:T(8,128)S(1)}, u32[]{:S(2)}, u32[]{:S(2)}) collective-permute-start(f32[2080,128]{1,0:T(8,128)S(1)} %features.1.refs_4_), channel_id=1, source_target_pairs={{0,2},{2,0},{4,6},{6,4},{8,10},{10,8},{12,14},{14,12},{16,18},{18,... | collective-permute-start | bytes 3194888 | tf_op jit(solution)/shard_map/ppermute | solution.py:208

commit v4 on v3

--- a/solution.py
+++ b/solution.py
@@ -120,7 +120,8 @@
                 got = got[:, : 2 * r] + got[:, 2 * r :]
                 for j in range(SUB):
                     b = i * WIDE + s * SUB + j
-                    feat_ref[pl.ds(l * half * nb + b, half, stride=nb), :] = jnp.where(
+                    here = (b * layers + l) * half
+                    feat_ref[here : here + half] = jnp.where(
                         low_lane, got[j * r : j * r + half], got[j * r + half : (j + 1) * r]
                     )
 
@@ -143,7 +144,7 @@
     acc = jnp.zeros((2 * nb, 2 * count), jnp.float32)
     for g in range(0, groups, 2):
         q = jnp.concatenate([ref[:, g * lanes : (g + 2) * lanes] for ref in pieces], axis=0)
-        f = [feat_ref[(g + d) * nb : (g + d + 1) * nb, :] for d in (0, 1)]
+        f = [feat_ref[pl.ds(g + d, nb, stride=groups), :] for d in (0, 1)]
         f = jnp.concatenate(f, axis=1)
         q, f = [jnp.concatenate(split(x), axis=0) for x in (q, f)]
         acc = acc + mm(f, q, NT)
@@ -170,20 +171,22 @@
     order = (query == iota((count, queries), 1)).astype(jnp.float32).astype(jnp.bfloat16)
     high, low = split(acc)
     acc = mm(high, order) + mm(low, order)
-    targets = ex_count * tok_count * EX_DEV
-    lane = iota((blocks, targets), 1)
+    targets = ex_count * tok_count
+    lane = iota((blocks, targets * EX_DEV), 1)
     ids = [ref[ref.shape[0] - blocks // 2 :, :1] for ref in (dest_ref, other_ref)]
     ids = jnp.concatenate(ids, axis=0).astype(jnp.int32)
-    owner = lane // EX_DEV // tok_count * EX_DEV + lane % EX_DEV == ids
+    owner = lane % targets // tok_count * EX_DEV + lane // targets == ids
     owner = owner.astype(jnp.float32).astype(jnp.bfloat16)
     high, low = split(acc)
     full = mm(owner, high, TN) + mm(owner, low, TN)
     each = queries // tok_count
-    tok = iota((targets, each), 0) // EX_DEV % tok_count
+    tok = iota((targets * EX_DEV, each), 0) % tok_count
     result = full[:, :each]
     for t in range(1, tok_count):
         result = jnp.where(tok == t, full[:, t * each : (t + 1) * each], result)
-    out_ref[...] = result
+    out_ref[...] = jnp.concatenate(
+        [result[k * targets : (k + 1) * targets] for k in range(EX_DEV)], axis=1
+    )
 
 
 def on_device(
@@ -234,7 +237,7 @@
         held = jnp.concatenate([held, swapped(held, bit)], axis=0)
         masks = masks + [mask ^ bit for mask in masks]
         bit //= 2
-    last = [bit] if bit == 2 else [2, 4, 6] if bit == 4 else []
+    last = [bit] if bit == 2 else [6, 2, 4] if bit == 4 else []
     held, outs = lax.optimization_barrier((held, outs))
     pieces = [held] + [swapped(held, m) for m in last]
     masks = tuple(mask ^ m for m in [0] + last for mask in masks)
@@ -262,13 +265,13 @@
     chunks = pl.pallas_call(
         lambda *refs: scores_kernel(ex_count, tok_count, own, masks, *refs),
         in_specs=[SMEM] + [pl.BlockSpec()] * (len(pieces) + 3),
-        out_shape=jax.ShapeDtypeStruct((ex_count * tok_count * EX_DEV, each), jnp.float32),
+        out_shape=jax.ShapeDtypeStruct((ex_count * tok_count, EX_DEV * each), jnp.float32),
         compiler_params=pltpu.CompilerParams(vmem_limit_bytes=8 * 1024 * 1024),
         name="scores",
     )(place[None], *pieces, own_scores, mine[layers * half * nb :], other)
-    chunks = chunks.reshape(ex_count * tok_count, EX_DEV, each)
     arrived = lax.all_to_all(chunks, ("ex", "tok"), split_axis=0, concat_axis=0, tiled=True)
-    return jnp.sum(arrived, axis=0).T * (1.0 / (r * size))
+    total = jnp.sum(arrived, axis=0) * (1.0 / (r * size))
+    return total.reshape(EX_DEV, each).T
 
 
 def solution(mesh):

time: 33.7 us -> 33.2 us (0.985)
  local copies, waits for them, and re-layouts: 1.16 us -> 1.82 us
  other arithmetic: 0.69 us -> 0.12 us
  blocking collectives: 11.6 us -> 11.2 us
  waiting for transfers between devices: 2.18 us -> 1.79 us
    mul x0 -> x1, local copies, waits for them, and re-layouts: none -> 0.66 us  [on_device(): total = jnp.sum(arrived, axis=0) * (1.0 / (r * size))]
    mul x1, other arithmetic: 0.58 us -> 0.01 us  [on_device(): total = jnp.sum(arrived, axis=0) * (1.0 / (r * size))]
    pallas_call x1, Pallas kernels: 4.61 us -> 4.11 us  [on_device(): pl.pallas_call(features_kernel, in_specs=[SMEM, SMEM, VMEM, pl.BlockSpec(...]
    all_to_all x1, blocking collectives: 11.6 us -> 11.2 us  [on_device(): lax.all_to_all(chunks, ('ex', 'tok'), split_axis=0, concat_axis=0, tiled=...]
    pallas_call x1, Pallas kernels: 0.46 us -> 0.86 us  [on_device(): pl.pallas_call(own_scores_kernel, out_shape=jax.ShapeDtypeStruct((nb, own...]
    ppermute x5, waiting for transfers between devices: 2.18 us -> 1.79 us  [swapped(): return lax.ppermute(x, 'ex', [(i, i ^ mask) for i in range(ex_count)])]
  transfers between devices with their start and end apart: 5 -> 5, of which waited for: 2 -> 3; matrix products, arithmetic and copies ran while one was open for 0% -> 0% of each run, Pallas kernels for 27% -> 27%
where the time goes in v4:
time: 33.2 us; the launch traced here: 33 us
  blocking collectives  11.2 us (34%)
  Pallas kernels  10.3 us (31%)
  starting transfers between devices  7.66 us (23%)
  local copies, waits for them, and re-layouts  1.82 us (5%)
  waiting for transfers between devices  1.79 us (5%)
    all_to_all x1, blocking collectives, on_device(): lax.all_to_all(chunks, ('ex', 'tok'), split_axis=0, concat_axis=0, tiled=...  11.2 us
    ppermute x5, starting transfers between devices, swapped(): return lax.ppermute(x, 'ex', [(i, i ^ mask) for i in range(ex_count)])  7.66 us
    pallas_call x1, Pallas kernels, on_device(): pl.pallas_call(features_kernel, in_specs=[SMEM, SMEM, VMEM, pl.BlockSpec(...  4.11 us
    pallas_call x1, Pallas kernels, on_device(): pl.pallas_call(outputs_kernel, in_specs=[SMEM, VMEM, pl.BlockSpec(), pl.B...  3.68 us
    ppermute x5, waiting for transfers between devices, swapped(): return lax.ppermute(x, 'ex', [(i, i ^ mask) for i in range(ex_count)])  1.79 us
    pallas_call x1, Pallas kernels, on_device(): pl.pallas_call(lambda *refs: scores_kernel(ex_count, tok_count, own, mask...  1.2 us
    unnamed x20, local copies, waits for them, and re-layouts  1.16 us
    pallas_call x1, Pallas kernels, on_device(): pl.pallas_call(own_scores_kernel, out_shape=jax.ShapeDtypeStruct((nb, own...  0.86 us
  transfers between devices with their start and end apart: 5, of which 3 were waited for; matrix products, arithmetic and copies ran while one was open for 0% of the time, Pallas kernels for 27%

profile of v4, /device:TPU:0, one launch (start us, length us, event | category | flops | bytes accessed | tf_op | source)
XLA Modules:
  0.0 33.0 jit_solution(12258583344152154594)
XLA Ops:
  0.0 0.0 copy-start.2
  0.0 0.0 copy-start
  0.0 4.0 %collective-permute-start = (f32[2,8192]{1,0:T(2,128)}, f32[2,8192]{1,0:T(2,128)S(1)}, u32[]{:S(2)}, u32[]{:S(2)}) collective-permute-start(f32[2,8192]{1,0:T(2,128)} %param.16), channel_id=1, source_target_pairs={{0,16},{2,18},{4,20},{6,22},{8,24},{10,26},{12,28},{14,30},{16,0},... | collective-permute-start | bytes 196616 | tf_op jit(solution)/shard_map/ppermute | solution.py:211
  4.0 0.0 copy-start.3
  4.0 0.9 %copy-done.3 = f32[2,2,64,64]{3,2,1,0:T(8,128)S(1)} copy-done((f32[2,2,64,64]{3,2,1,0:T(8,128)S(1)}, f32[2,2,64,64]{3,2,1,0:T(8,128)}, u32[]{:S(2)}) %copy-start.3) | copy-done | bytes 65560
  4.9 0.0 copy-start.4
  4.9 0.0 slice-start
  5.0 0.4 %factors.1 = (bf16[256,128]{1,0:T(8,128)(2,1)S(1)}, bf16[384,256]{1,0:T(8,128)(2,1)S(1)}) custom-call(f32[2,2,64,64]{3,2,1,0:T(8,128)S(1)} %copy-done.3), custom_call_target="tpu_custom_call" | custom-call | flops 10000000000 | bytes 1048576 | tf_op jit(solution)/shard_map/factors/pallas_call | solution.py:214
  5.4 0.0 copy-done.2
  5.4 0.0 copy-done
  5.4 0.2 copy-done.4
  5.6 0.0 copy-start.7
  5.6 0.0 slice-start.1
  5.6 0.0 copy-start.1
  5.6 0.0 copy-start.5
  5.6 0.0 copy-start.6
  5.6 3.7 %outputs.1.out_ref = bf16[2,128,1024]{2,1,0:T(8,128)(2,1)S(1)} custom-call(s32[32]{0:T(128)S(1)} %copy-done.4, bf16[32,32,2,1024]{3,2,1,0:T(2,128)(2,1)S(1)} %copy-done, bf16[128,1024]{1,0:T(8,128)(2,1)S(1)} %bitcast.12, bf16[256,128]{1,0:T(8,128)(2,1)S(1)} %get-tuple-element.9.left_ref), custom_call_target="tpu_custom_call" | custom-call | flops 10000000000 | bytes 1048576 | tf_op jit(solution)/shard_map/outputs/pallas_call | solution.py:224
  9.3 0.0 collective-permute-done
  9.3 0.0 copy-done.7
  9.3 0.1 pad_maximum_fusion.refs_0_.refs_1_
  9.4 2.6 %collective-permute-start.1 = (f32[4,8192]{1,0:T(4,128)S(1)}, f32[4,8192]{1,0:T(4,128)S(1)}, u32[]{:S(2)}, u32[]{:S(2)}) collective-permute-start(f32[4,8192]{1,0:T(4,128)S(1)} %pad_maximum_fusion.refs_0_.refs_1_), channel_id=1, source_target_pairs={{0,12},{2,14},{4,8},{6,10},{8,4},{10,6},{12,0},{14,2},{16,28},{18,... | collective-permute-start | bytes 393224 | tf_op jit(solution)/shard_map/ppermute | solution.py:211
  12.0 0.5 %collective-permute-start.2 = (f32[4,8192]{1,0:T(4,128)S(1)}, f32[4,8192]{1,0:T(4,128)S(1)}, u32[]{:S(2)}, u32[]{:S(2)}) collective-permute-start(f32[4,8192]{1,0:T(4,128)S(1)} %pad_maximum_fusion.refs_0_.refs_1_), channel_id=1, source_target_pairs={{0,4},{2,6},{4,0},{6,2},{8,12},{10,14},{12,8},{14,10},{16,20},{18,... | collective-permute-start | bytes 393224 | tf_op jit(solution)/shard_map/ppermute | solution.py:211
  12.5 0.4 %collective-permute-start.3 = (f32[4,8192]{1,0:T(4,128)S(1)}, f32[4,8192]{1,0:T(4,128)S(1)}, u32[]{:S(2)}, u32[]{:S(2)}) collective-permute-start(f32[4,8192]{1,0:T(4,128)S(1)} %pad_maximum_fusion.refs_0_.refs_1_), channel_id=1, source_target_pairs={{0,8},{2,10},{4,12},{6,14},{8,0},{10,2},{12,4},{14,6},{16,24},{18,... | collective-permute-start | bytes 393224 | tf_op jit(solution)/shard_map/ppermute | solution.py:211
  13.0 0.0 slice-done
  13.0 0.0 slice-done.1
  13.0 0.0 copy-done.1
  13.0 0.0 copy-done.5
  13.0 0.0 copy-done.6
  13.0 4.1 %features.1.refs_4_ = f32[2080,128]{1,0:T(8,128)S(1)} custom-call(s32[32]{0:T(128)S(1)} %bitcast.13, s32[32]{0:T(128)S(1)} %copy-done.6, bf16[32,32,4096]{2,1,0:T(8,128)(2,1)S(1)} %bitcast.11, bf16[2,128,1024]{2,1,0:T(8,128)(2,1)S(1)} %outputs.1.out_ref, bf16[4096,128]{1,0:T(8,128)(2,1)S(1)} %copy-done.1, bf16[384,256]{1,0:T(8,128)(2,1)S(1)} %get-tuple-element.12.right_ref), custom_call_target="tpu_custom_call" | custom-call | flops 10000000000 | bytes 1048576 | tf_op jit(solution)/shard_map/features/pallas_call | solution.py:245
  17.1 0.1 collective-permute-start.4
  17.2 0.0 collective-permute-done.1.refs_1_.refs_2_
  17.2 0.9 %collective-permute-done.2.refs_2_.refs_3_ = f32[4,8192]{1,0:T(4,128)S(1)} collective-permute-done((f32[4,8192]{1,0:T(4,128)S(1)}, f32[4,8192]{1,0:T(4,128)S(1)}, u32[]{:S(2)}, u32[]{:S(2)}) %collective-permute-start.2) | collective-permute-done | bytes 131104 | tf_op jit(solution)/shard_map/ppermute | solution.py:211
  18.1 0.1 collective-permute-done.3.refs_3_.refs_4_
  18.2 0.9 %own_scores.1.refs_5_ = f32[32,16]{1,0:T(8,128)S(1)} custom-call(f32[4,8192]{1,0:T(4,128)S(1)} %pad_maximum_fusion.refs_0_.refs_1_, f32[4,8192]{1,0:T(4,128)S(1)} %collective-permute-done.1.refs_1_.refs_2_, f32[4,8192]{1,0:T(4,128)S(1)} %collective-permute-done.2.refs_2_.refs_3_, f32[4,8192]{1,0:T(4,128)S(1)} %collective-permute-done.3.refs_3_.refs_4_, ...), custom_call_target="tpu_custom_call" | custom-call | flops 10000000000 | bytes 1048576 | tf_op jit(solution)/shard_map/own_scores/pallas_call | solution.py:258
  19.1 0.8 %collective-permute-done.4.refs_7_ = f32[2080,128]{1,0:T(8,128)S(1)} collective-permute-done((f32[2080,128]{1,0:T(8,128)S(1)}, f32[2080,128]{1,0:T(8,128)S(1)}, u32[]{:S(2)}, u32[]{:S(2)}) %collective-permute-start.4) | collective-permute-done | bytes 1064992 | tf_op jit(solution)/shard_map/ppermute | solution.py:211
  19.9 1.2 %scores.1 = f32[32,64]{1,0:T(8,128)S(1)} custom-call(s32[1]{0:T(128)} %bitcast.refs_0_, f32[4,8192]{1,0:T(4,128)S(1)} %pad_maximum_fusion.refs_0_.refs_1_, f32[4,8192]{1,0:T(4,128)S(1)} %collective-permute-done.1.refs_1_.refs_2_, f32[4,8192]{1,0:T(4,128)S(1)} %collective-permute-done.2.refs_2_.refs_3_, f32[4,8192]{1,0:T(4,128)S(1)} %collective-permute-done.3.refs_3_.refs_4_, ...), custom_call_target="tpu_custom_call" | custom-call | tf_op jit(solution)/shard_map/scores/pallas_call | solution.py:265
  21.1 11.2 %all_to_all.9 = f32[32,1,64]{2,1,0:T(1,128)S(1)} all-to-all(f32[32,1,64]{2,1,0:T(1,128)S(1)} %bitcast.9), channel_id=1, replica_groups=mesh['ex'=16,'tok'=2] {'ex','tok'}, dimensions={0} | all-to-all | bytes 16384 | tf_op jit(solution)/shard_map/all_to_all | solution.py:272
  32.3 0.1 reduce_sum.9
  32.3 0.7 %mul.12 = f32[4,16]{1,0:T(4,128)} reshape(f32[64]{0:T(128)S(1)} %broadcast_multiply_fusion) | data formatting | bytes 512 | tf_op jit(solution)/shard_map/mul | solution.py:273
  (3 shorter events, 0.0 us)
Async XLA Ops:
  0.0 5.4 %copy-start.2 = (bf16[2,1024,64]{1,2,0:T(8,128)(2,1)S(1)}, bf16[2,1024,64]{1,2,0:T(8,128)(2,1)}, u32[]{:S(2)}) copy-start(bf16[2,1024,64]{1,2,0:T(8,128)(2,1)} %param.15) | copy-start | bytes 786436
  0.0 5.4 %copy-start = (bf16[32,32,2,1024]{3,2,1,0:T(2,128)(2,1)S(1)}, bf16[32,32,2,1024]{3,2,1,0:T(2,128)(2,1)}, u32[]{:S(2)}) copy-start(bf16[32,32,2,1024]{3,2,1,0:T(2,128)(2,1)} %grad_ref.1) | copy-start | bytes 12582916
  0.0 9.3 %collective-permute-start = (f32[2,8192]{1,0:T(2,128)}, f32[2,8192]{1,0:T(2,128)S(1)}, u32[]{:S(2)}, u32[]{:S(2)}) collective-permute-start(f32[2,8192]{1,0:T(2,128)} %param.16), channel_id=1, source_target_pairs={{0,16},{2,18},{4,20},{6,22},{8,24},{10,26},{12,28},{14,30},{16,0},... | collective-permute-start | bytes 196616 | tf_op jit(solution)/shard_map/ppermute | solution.py:211
  4.0 0.9 %copy-start.3 = (f32[2,2,64,64]{3,2,1,0:T(8,128)S(1)}, f32[2,2,64,64]{3,2,1,0:T(8,128)}, u32[]{:S(2)}) copy-start(f32[2,2,64,64]{3,2,1,0:T(8,128)} %precond_ref.1) | copy-start | bytes 196612
  4.9 0.7 %copy-start.4 = (s32[32]{0:T(128)S(1)}, s32[32]{0:T(128)}, u32[]{:S(2)}) copy-start(s32[32]{0:T(128)} %len_ref.1) | copy-start | bytes 388
  4.9 8.0 %slice-start = ((s8[8388608]{0:T(1024)(128)(4,1)}), s8[4194304]{0:T(1024)(128)(4,1)S(1)}, s32[]{:S(2)}) async-start(s8[8388608]{0:T(1024)(128)(4,1)} %bitcast.10), calls=%async_computation.1 | async-start | bytes 8388608
  5.6 3.7 %copy-start.7 = (f32[2,8192]{1,0:T(2,128)S(1)}, f32[2,8192]{1,0:T(2,128)}, u32[]{:S(2)}) copy-start(f32[2,8192]{1,0:T(2,128)} %param.16) | copy-start | bytes 196612
  5.6 7.4 %slice-start.1 = ((s8[8388608]{0:T(1024)(128)(4,1)}), s8[4194304]{0:T(1024)(128)(4,1)S(1)}, s32[]{:S(2)}) async-start(s8[8388608]{0:T(1024)(128)(4,1)} %bitcast.10), calls=%async_computation.2 | async-start | bytes 8388608
  5.6 7.4 %copy-start.1 = (bf16[4096,128]{1,0:T(8,128)(2,1)S(1)}, bf16[4096,128]{1,0:T(8,128)(2,1)}, u32[]{:S(2)}) copy-start(bf16[4096,128]{1,0:T(8,128)(2,1)} %w_ref.1) | copy-start | bytes 3145732
  5.6 7.4 %copy-start.5 = (s32[32,1]{0,1:T(1,128)S(1)}, s32[32,1]{0,1:T(1,128)}, u32[]{:S(2)}) copy-start(s32[32,1]{0,1:T(1,128)} %param.12) | copy-start | bytes 388
  5.6 7.4 %copy-start.6 = (s32[32]{0:T(128)S(1)}, s32[32]{0:T(128)}, u32[]{:S(2)}) copy-start(s32[32]{0:T(128)} %slot_ref.1) | copy-start | bytes 388
  9.4 7.8 %collective-permute-start.1 = (f32[4,8192]{1,0:T(4,128)S(1)}, f32[4,8192]{1,0:T(4,128)S(1)}, u32[]{:S(2)}, u32[]{:S(2)}) collective-permute-start(f32[4,8192]{1,0:T(4,128)S(1)} %pad_maximum_fusion.refs_0_.refs_1_), channel_id=1, source_target_pairs={{0,12},{2,14},{4,8},{6,10},{8,4},{10,6},{12,0},{14,2},{16,28},{18,... | collective-permute-start | bytes 393224 | tf_op jit(solution)/shard_map/ppermute | solution.py:211
  12.0 6.1 %collective-permute-start.2 = (f32[4,8192]{1,0:T(4,128)S(1)}, f32[4,8192]{1,0:T(4,128)S(1)}, u32[]{:S(2)}, u32[]{:S(2)}) collective-permute-start(f32[4,8192]{1,0:T(4,128)S(1)} %pad_maximum_fusion.refs_0_.refs_1_), channel_id=1, source_target_pairs={{0,4},{2,6},{4,0},{6,2},{8,12},{10,14},{12,8},{14,10},{16,20},{18,... | collective-permute-start | bytes 393224 | tf_op jit(solution)/shard_map/ppermute | solution.py:211
  12.5 5.7 %collective-permute-start.3 = (f32[4,8192]{1,0:T(4,128)S(1)}, f32[4,8192]{1,0:T(4,128)S(1)}, u32[]{:S(2)}, u32[]{:S(2)}) collective-permute-start(f32[4,8192]{1,0:T(4,128)S(1)} %pad_maximum_fusion.refs_0_.refs_1_), channel_id=1, source_target_pairs={{0,8},{2,10},{4,12},{6,14},{8,0},{10,2},{12,4},{14,6},{16,24},{18,... | collective-permute-start | bytes 393224 | tf_op jit(solution)/shard_map/ppermute | solution.py:211
  17.1 2.7 %collective-permute-start.4 = (f32[2080,128]{1,0:T(8,128)S(1)}, f32[2080,128]{1,0:T(8,128)S(1)}, u32[]{:S(2)}, u32[]{:S(2)}) collective-permute-start(f32[2080,128]{1,0:T(8,128)S(1)} %features.1.refs_4_), channel_id=1, source_target_pairs={{0,2},{2,0},{4,6},{6,4},{8,10},{10,8},{12,14},{14,12},{16,18},{18,... | collective-permute-start | bytes 3194888 | tf_op jit(solution)/shard_map/ppermute | solution.py:211

commit v5 on v4

--- a/solution.py
+++ b/solution.py
@@ -14,7 +14,6 @@
 NT = (((1,), (1,)), ((), ()))
 TN = (((0,), (0,)), ((), ()))
 VMEM = pl.BlockSpec(memory_space=pltpu.VMEM)
-SMEM = pl.BlockSpec(memory_space=pltpu.SMEM)
 
 
 def split(x):
@@ -70,7 +69,8 @@
         out = raw_ref[pl.ds(0, rows, stride=layers), :]
         for l in range(1, layers):
             out = jnp.where(lane_layer == l, raw_ref[pl.ds(l, rows, stride=layers), :], out)
-        live = jnp.concatenate([slot < len_ref[i * STEP + j] for j in range(STEP)], axis=0)
+        lens = [len_ref[pl.ds(i * STEP + j, 1), :] for j in range(STEP)]
+        live = jnp.concatenate([slot < x for x in lens], axis=0)
         high, low = split(jnp.where(live, out, 0.0))
         both = mm(left_ref[...], high, NT)
         done = both[:width] + both[width:] + mm(left_ref[:width], low, NT)
@@ -81,7 +81,7 @@
     lax.fori_loop(0, nb // STEP, turn, 0)
 
 
-def features_kernel(dest_ref, slot_ref, act_ref, out_ref, w_ref, right_ref, feat_ref, in_ref):
+def features_kernel(id_ref, act_ref, out_ref, w_ref, right_ref, feat_ref, in_ref):
     nb, size, depth = act_ref.shape
     width = out_ref.shape[1]
     layers = right_ref.shape[1] // feat_ref.shape[1]
@@ -131,9 +131,7 @@
         if i > 0:
             finish(i - 1)
     finish(nb // WIDE - 1)
-    for b in range(nb):
-        example = (dest_ref[b] * EX_DEV + slot_ref[b]).astype(jnp.float32)
-        feat_ref[pl.ds(layers * half * nb + b, 1), :] = jnp.full((1, 2 * r), example)
+    feat_ref[layers * half * nb :] = id_ref[...]
 
 
 def products(pieces, feat_ref):
@@ -167,7 +165,7 @@
     mask = jnp.zeros((count, queries), jnp.int32)
     for k, m in enumerate(masks):
         mask = jnp.where(piece == k, m, mask)
-    query = jnp.bitwise_xor(mask, place_ref[0]) * own + iota((count, queries), 0) % own
+    query = jnp.bitwise_xor(mask, place_ref[:, :1]) * own + iota((count, queries), 0) % own
     order = (query == iota((count, queries), 1)).astype(jnp.float32).astype(jnp.bfloat16)
     high, low = split(acc)
     acc = mm(high, order) + mm(low, order)
@@ -221,15 +219,16 @@
         cost_estimate=pl.CostEstimate(flops=10**10, bytes_accessed=2**20, transcendentals=0),
         name="factors",
     )(precond)
+    lens = jnp.broadcast_to(block_len[:, None], (nb, width))
     outs = pl.pallas_call(
         outputs_kernel,
-        in_specs=[SMEM, VMEM, pl.BlockSpec(), pl.BlockSpec()],
+        in_specs=[pl.BlockSpec(), VMEM, pl.BlockSpec(), pl.BlockSpec()],
         out_shape=jax.ShapeDtypeStruct((2, width, nb * size), jnp.bfloat16),
         scratch_shapes=[pltpu.VMEM((STEP * size * layers, width), jnp.float32)],
         compiler_params=pltpu.CompilerParams(vmem_limit_bytes=8 * 1024 * 1024),
         cost_estimate=pl.CostEstimate(flops=10**10, bytes_accessed=2**20, transcendentals=0),
         name="outputs",
-    )(block_len, out_grads, jnp.swapaxes(out_proj, 1, 2).reshape(width, grad_depth), left)
+    )(lens, out_grads, jnp.swapaxes(out_proj, 1, 2).reshape(width, grad_depth), left)
 
     held, masks = query_grads, [0]
     bit = ex_count // 2
@@ -242,15 +241,17 @@
     pieces = [held] + [swapped(held, m) for m in last]
     masks = tuple(mask ^ m for m in [0] + last for mask in masks)
 
+    ids = (block_dest * EX_DEV + block_slot[:, None]).astype(jnp.float32)
+    ids = jnp.broadcast_to(ids, (nb, 2 * r))
     mine = pl.pallas_call(
         features_kernel,
-        in_specs=[SMEM, SMEM, VMEM, pl.BlockSpec(), VMEM, pl.BlockSpec()],
+        in_specs=[pl.BlockSpec(), VMEM, pl.BlockSpec(), VMEM, pl.BlockSpec()],
         out_shape=jax.ShapeDtypeStruct(((layers * half + 1) * nb, 2 * r), jnp.float32),
         scratch_shapes=[pltpu.VMEM((2, WIDE * size, width), jnp.float32)],
         compiler_params=pltpu.CompilerParams(vmem_limit_bytes=12 * 1024 * 1024),
         cost_estimate=pl.CostEstimate(flops=10**10, bytes_accessed=2**20, transcendentals=0),
         name="features",
-    )(block_dest[:, 0], block_slot, activations, outs, in_proj, right)
+    )(ids, activations, outs, in_proj, right)
 
     other = swapped(mine, 1)
 
@@ -264,11 +265,10 @@
     )(*pieces, mine)
     chunks = pl.pallas_call(
         lambda *refs: scores_kernel(ex_count, tok_count, own, masks, *refs),
-        in_specs=[SMEM] + [pl.BlockSpec()] * (len(pieces) + 3),
         out_shape=jax.ShapeDtypeStruct((ex_count * tok_count, EX_DEV * each), jnp.float32),
         compiler_params=pltpu.CompilerParams(vmem_limit_bytes=8 * 1024 * 1024),
         name="scores",
-    )(place[None], *pieces, own_scores, mine[layers * half * nb :], other)
+    )(jnp.full((1, 2 * r), place), *pieces, own_scores, ids, other)
     arrived = lax.all_to_all(chunks, ("ex", "tok"), split_axis=0, concat_axis=0, tiled=True)
     total = jnp.sum(arrived, axis=0) * (1.0 / (r * size))
     return total.reshape(EX_DEV, each).T

time: 33.2 us -> 32.7 us (0.985)
  Pallas kernels: 10.3 us -> 9.16 us
  blocking collectives: 11.2 us -> 11.6 us
    pallas_call x2, Pallas kernels: 7.79 us -> 6.7 us  [the longest x1 3.56 us: on_device(): pl.pallas_call(features_kernel, in_specs=[pl.BlockSpec(), VMEM, pl.BlockS...]
    all_to_all x1, blocking collectives: 11.2 us -> 11.6 us  [on_device(): lax.all_to_all(chunks, ('ex', 'tok'), split_axis=0, concat_axis=0, tiled=...]
  transfers between devices with their start and end apart: 5 -> 5, of which waited for: 3 -> 3; matrix products, arithmetic and copies ran while one was open for 0% -> 0% of each run, Pallas kernels for 27% -> 24%
where the time goes in v5:
time: 32.7 us; the launch traced here: 32.5 us
  blocking collectives  11.6 us (35%)
  Pallas kernels  9.16 us (28%)
  starting transfers between devices  7.66 us (23%)
  local copies, waits for them, and re-layouts  1.99 us (6%)
  waiting for transfers between devices  1.8 us (6%)
    all_to_all x1, blocking collectives, on_device(): lax.all_to_all(chunks, ('ex', 'tok'), split_axis=0, concat_axis=0, tiled=...  11.6 us
    ppermute x5, starting transfers between devices, swapped(): return lax.ppermute(x, 'ex', [(i, i ^ mask) for i in range(ex_count)])  7.66 us
    pallas_call x1, Pallas kernels, on_device(): pl.pallas_call(features_kernel, in_specs=[pl.BlockSpec(), VMEM, pl.BlockS...  3.56 us
    pallas_call x1, Pallas kernels, on_device(): pl.pallas_call(outputs_kernel, in_specs=[pl.BlockSpec(), VMEM, pl.BlockSp...  3.14 us
    ppermute x5, waiting for transfers between devices, swapped(): return lax.ppermute(x, 'ex', [(i, i ^ mask) for i in range(ex_count)])  1.8 us
    pallas_call x1, Pallas kernels, on_device(): pl.pallas_call(lambda *refs: scores_kernel(ex_count, tok_count, own, mask...  1.2 us
    unnamed x20, local copies, waits for them, and re-layouts  1.18 us
    pallas_call x1, Pallas kernels, on_device(): pl.pallas_call(own_scores_kernel, out_shape=jax.ShapeDtypeStruct((nb, own...  0.86 us
  transfers between devices with their start and end apart: 5, of which 3 were waited for; matrix products, arithmetic and copies ran while one was open for 0% of the time, Pallas kernels for 24%

profile of v5, /device:TPU:0, one launch (start us, length us, event | category | flops | bytes accessed | tf_op | source)
XLA Modules:
  0.0 32.5 jit_solution(12874654057900912680)
XLA Ops:
  0.0 0.0 copy-start.2
  0.0 0.0 copy-start
  0.0 4.0 %collective-permute-start = (f32[2,8192]{1,0:T(2,128)}, f32[2,8192]{1,0:T(2,128)S(1)}, u32[]{:S(2)}, u32[]{:S(2)}) collective-permute-start(f32[2,8192]{1,0:T(2,128)} %param.16), channel_id=1, source_target_pairs={{0,16},{2,18},{4,20},{6,22},{8,24},{10,26},{12,28},{14,30},{16,0},... | collective-permute-start | bytes 196616 | tf_op jit(solution)/shard_map/ppermute | solution.py:209
  4.0 0.0 copy-start.3
  4.0 0.9 %copy-done.3 = f32[2,2,64,64]{3,2,1,0:T(8,128)S(1)} copy-done((f32[2,2,64,64]{3,2,1,0:T(8,128)S(1)}, f32[2,2,64,64]{3,2,1,0:T(8,128)}, u32[]{:S(2)}) %copy-start.3) | copy-done | bytes 65560
  4.9 0.0 copy-start.5
  4.9 0.0 slice-start
  5.0 0.4 %factors.1 = (bf16[256,128]{1,0:T(8,128)(2,1)S(1)}, bf16[384,256]{1,0:T(8,128)(2,1)S(1)}) custom-call(f32[2,2,64,64]{3,2,1,0:T(8,128)S(1)} %copy-done.3), custom_call_target="tpu_custom_call" | custom-call | flops 10000000000 | bytes 1048576 | tf_op jit(solution)/shard_map/factors/pallas_call | solution.py:212
  5.4 0.2 copy-done.5
  5.6 0.1 broadcast_in_dim.20.len_ref
  5.7 0.0 copy-done.2
  5.7 0.0 copy-done
  5.7 0.0 copy-start.6
  5.7 0.0 copy-start.7
  5.7 0.0 copy-start.4
  5.7 0.0 slice-start.1
  5.7 0.0 copy-start.1
  5.7 3.1 %outputs.1.out_ref = bf16[2,128,1024]{2,1,0:T(8,128)(2,1)S(1)} custom-call(s32[32,128]{1,0:T(8,128)S(1)} %broadcast_in_dim.20.len_ref, bf16[32,32,2,1024]{3,2,1,0:T(2,128)(2,1)S(1)} %copy-done, bf16[128,1024]{1,0:T(8,128)(2,1)S(1)} %bitcast.18, bf16[256,128]{1,0:T(8,128)(2,1)S(1)} %get-tuple-element.9.left_ref), custom_call_target="tpu_custom_call" | custom-call | flops 10000000000 | bytes 1048576 | tf_op jit(solution)/shard_map/outputs/pallas_call | solution.py:223
  8.9 0.0 copy-done.6
  8.9 0.0 copy-done.7
  8.9 0.0 collective-permute-done
  8.9 0.0 copy-done.4
  8.9 0.1 pad_maximum_fusion.refs_0_.refs_1_
  9.0 2.6 %collective-permute-start.1 = (f32[4,8192]{1,0:T(4,128)S(1)}, f32[4,8192]{1,0:T(4,128)S(1)}, u32[]{:S(2)}, u32[]{:S(2)}) collective-permute-start(f32[4,8192]{1,0:T(4,128)S(1)} %pad_maximum_fusion.refs_0_.refs_1_), channel_id=1, source_target_pairs={{0,12},{2,14},{4,8},{6,10},{8,4},{10,6},{12,0},{14,2},{16,28},{18,... | collective-permute-start | bytes 393224 | tf_op jit(solution)/shard_map/ppermute | solution.py:209
  11.6 0.5 %collective-permute-start.2 = (f32[4,8192]{1,0:T(4,128)S(1)}, f32[4,8192]{1,0:T(4,128)S(1)}, u32[]{:S(2)}, u32[]{:S(2)}) collective-permute-start(f32[4,8192]{1,0:T(4,128)S(1)} %pad_maximum_fusion.refs_0_.refs_1_), channel_id=1, source_target_pairs={{0,4},{2,6},{4,0},{6,2},{8,12},{10,14},{12,8},{14,10},{16,20},{18,... | collective-permute-start | bytes 393224 | tf_op jit(solution)/shard_map/ppermute | solution.py:209
  12.1 0.4 %collective-permute-start.3 = (f32[4,8192]{1,0:T(4,128)S(1)}, f32[4,8192]{1,0:T(4,128)S(1)}, u32[]{:S(2)}, u32[]{:S(2)}) collective-permute-start(f32[4,8192]{1,0:T(4,128)S(1)} %pad_maximum_fusion.refs_0_.refs_1_), channel_id=1, source_target_pairs={{0,8},{2,10},{4,12},{6,14},{8,0},{10,2},{12,4},{14,6},{16,24},{18,... | collective-permute-start | bytes 393224 | tf_op jit(solution)/shard_map/ppermute | solution.py:209
  12.5 0.1 broadcast_in_dim.23.id_ref.refs_6_
  12.6 0.0 slice-done
  12.6 0.0 slice-done.1
  12.6 0.0 copy-done.1
  12.6 3.6 %features.1.refs_4_ = f32[2080,128]{1,0:T(8,128)S(1)} custom-call(f32[32,128]{1,0:T(8,128)S(1)} %broadcast_in_dim.23.id_ref.refs_6_, bf16[32,32,4096]{2,1,0:T(8,128)(2,1)S(1)} %bitcast.17, bf16[2,128,1024]{2,1,0:T(8,128)(2,1)S(1)} %outputs.1.out_ref, bf16[4096,128]{1,0:T(8,128)(2,1)S(1)} %copy-done.1, bf16[384,256]{1,0:T(8,128)(2,1)S(1)} %get-tuple-element.12.right_ref), custom_call_target="tpu_custom_call" | custom-call | flops 10000000000 | bytes 1048576 | tf_op jit(solution)/shard_map/features/pallas_call | solution.py:246
  16.2 0.1 collective-permute-start.4
  16.3 0.0 collective-permute-done.1.refs_1_.refs_2_
  16.3 1.4 %collective-permute-done.2.refs_2_.refs_3_ = f32[4,8192]{1,0:T(4,128)S(1)} collective-permute-done((f32[4,8192]{1,0:T(4,128)S(1)}, f32[4,8192]{1,0:T(4,128)S(1)}, u32[]{:S(2)}, u32[]{:S(2)}) %collective-permute-start.2) | collective-permute-done | bytes 131104 | tf_op jit(solution)/shard_map/ppermute | solution.py:209
  17.7 0.1 collective-permute-done.3.refs_3_.refs_4_
  17.8 0.9 %own_scores.1.refs_5_ = f32[32,16]{1,0:T(8,128)S(1)} custom-call(f32[4,8192]{1,0:T(4,128)S(1)} %pad_maximum_fusion.refs_0_.refs_1_, f32[4,8192]{1,0:T(4,128)S(1)} %collective-permute-done.1.refs_1_.refs_2_, f32[4,8192]{1,0:T(4,128)S(1)} %collective-permute-done.2.refs_2_.refs_3_, f32[4,8192]{1,0:T(4,128)S(1)} %collective-permute-done.3.refs_3_.refs_4_, ...), custom_call_target="tpu_custom_call" | custom-call | flops 10000000000 | bytes 1048576 | tf_op jit(solution)/shard_map/own_scores/pallas_call | solution.py:259
  18.6 0.3 collective-permute-done.4.refs_7_
  19.0 1.2 %scores.1 = f32[32,64]{1,0:T(8,128)S(1)} custom-call(s32[1,128]{1,0:T(1,128)S(1)} %broadcast_in_dim.19.refs_0_, f32[4,8192]{1,0:T(4,128)S(1)} %pad_maximum_fusion.refs_0_.refs_1_, f32[4,8192]{1,0:T(4,128)S(1)} %collective-permute-done.1.refs_1_.refs_2_, f32[4,8192]{1,0:T(4,128)S(1)} %collective-permute-done.2.refs_2_.refs_3_, ...), custom_call_target="tpu_custom_call" | custom-call | tf_op jit(solution)/shard_map/scores/pallas_call | solution.py:266
  20.2 11.6 %all_to_all.9 = f32[32,1,64]{2,1,0:T(1,128)S(1)} all-to-all(f32[32,1,64]{2,1,0:T(1,128)S(1)} %bitcast.15), channel_id=1, replica_groups=mesh['ex'=16,'tok'=2] {'ex','tok'}, dimensions={0} | all-to-all | bytes 16384 | tf_op jit(solution)/shard_map/all_to_all | solution.py:272
  31.8 0.1 reduce_sum.9
  31.8 0.7 %mul.20 = f32[4,16]{1,0:T(4,128)} reshape(f32[64]{0:T(128)S(1)} %broadcast_multiply_fusion) | data formatting | bytes 512 | tf_op jit(solution)/shard_map/mul | solution.py:273
  (4 shorter events, 0.0 us)
Async XLA Ops:
  0.0 5.7 %copy-start.2 = (bf16[2,1024,64]{1,2,0:T(8,128)(2,1)S(1)}, bf16[2,1024,64]{1,2,0:T(8,128)(2,1)}, u32[]{:S(2)}) copy-start(bf16[2,1024,64]{1,2,0:T(8,128)(2,1)} %param.15) | copy-start | bytes 786436
  0.0 5.7 %copy-start = (bf16[32,32,2,1024]{3,2,1,0:T(2,128)(2,1)S(1)}, bf16[32,32,2,1024]{3,2,1,0:T(2,128)(2,1)}, u32[]{:S(2)}) copy-start(bf16[32,32,2,1024]{3,2,1,0:T(2,128)(2,1)} %grad_ref.1) | copy-start | bytes 12582916
  0.0 8.9 %collective-permute-start = (f32[2,8192]{1,0:T(2,128)}, f32[2,8192]{1,0:T(2,128)S(1)}, u32[]{:S(2)}, u32[]{:S(2)}) collective-permute-start(f32[2,8192]{1,0:T(2,128)} %param.16), channel_id=1, source_target_pairs={{0,16},{2,18},{4,20},{6,22},{8,24},{10,26},{12,28},{14,30},{16,0},... | collective-permute-start | bytes 196616 | tf_op jit(solution)/shard_map/ppermute | solution.py:209
  4.0 0.9 %copy-start.3 = (f32[2,2,64,64]{3,2,1,0:T(8,128)S(1)}, f32[2,2,64,64]{3,2,1,0:T(8,128)}, u32[]{:S(2)}) copy-start(f32[2,2,64,64]{3,2,1,0:T(8,128)} %precond_ref.1) | copy-start | bytes 196612
  4.9 0.7 %copy-start.5 = (s32[32]{0:T(128)S(1)}, s32[32]{0:T(128)}, u32[]{:S(2)}) copy-start(s32[32]{0:T(128)} %param.11) | copy-start | bytes 388
  4.9 7.7 %slice-start = ((s8[8388608]{0:T(1024)(128)(4,1)}), s8[4194304]{0:T(1024)(128)(4,1)S(1)}, s32[]{:S(2)}) async-start(s8[8388608]{0:T(1024)(128)(4,1)} %bitcast.16), calls=%async_computation.1 | async-start | bytes 8388608
  5.7 3.2 %copy-start.6 = (s32[32]{0:T(128)S(1)}, s32[32]{0:T(128)}, u32[]{:S(2)}) copy-start(s32[32]{0:T(128)} %param.13) | copy-start | bytes 388
  5.7 3.2 %copy-start.7 = (s32[32,1]{0,1:T(1,128)S(1)}, s32[32,1]{0,1:T(1,128)}, u32[]{:S(2)}) copy-start(s32[32,1]{0,1:T(1,128)} %param.12) | copy-start | bytes 388
  5.7 3.2 %copy-start.4 = (f32[2,8192]{1,0:T(2,128)S(1)}, f32[2,8192]{1,0:T(2,128)}, u32[]{:S(2)}) copy-start(f32[2,8192]{1,0:T(2,128)} %param.16) | copy-start | bytes 196612
  5.7 6.9 %slice-start.1 = ((s8[8388608]{0:T(1024)(128)(4,1)}), s8[4194304]{0:T(1024)(128)(4,1)S(1)}, s32[]{:S(2)}) async-start(s8[8388608]{0:T(1024)(128)(4,1)} %bitcast.16), calls=%async_computation.2 | async-start | bytes 8388608
  5.7 6.9 %copy-start.1 = (bf16[4096,128]{1,0:T(8,128)(2,1)S(1)}, bf16[4096,128]{1,0:T(8,128)(2,1)}, u32[]{:S(2)}) copy-start(bf16[4096,128]{1,0:T(8,128)(2,1)} %w_ref.1) | copy-start | bytes 3145732
  9.0 7.3 %collective-permute-start.1 = (f32[4,8192]{1,0:T(4,128)S(1)}, f32[4,8192]{1,0:T(4,128)S(1)}, u32[]{:S(2)}, u32[]{:S(2)}) collective-permute-start(f32[4,8192]{1,0:T(4,128)S(1)} %pad_maximum_fusion.refs_0_.refs_1_), channel_id=1, source_target_pairs={{0,12},{2,14},{4,8},{6,10},{8,4},{10,6},{12,0},{14,2},{16,28},{18,... | collective-permute-start | bytes 393224 | tf_op jit(solution)/shard_map/ppermute | solution.py:209
  11.6 6.1 %collective-permute-start.2 = (f32[4,8192]{1,0:T(4,128)S(1)}, f32[4,8192]{1,0:T(4,128)S(1)}, u32[]{:S(2)}, u32[]{:S(2)}) collective-permute-start(f32[4,8192]{1,0:T(4,128)S(1)} %pad_maximum_fusion.refs_0_.refs_1_), channel_id=1, source_target_pairs={{0,4},{2,6},{4,0},{6,2},{8,12},{10,14},{12,8},{14,10},{16,20},{18,... | collective-permute-start | bytes 393224 | tf_op jit(solution)/shard_map/ppermute | solution.py:209
  12.1 5.7 %collective-permute-start.3 = (f32[4,8192]{1,0:T(4,128)S(1)}, f32[4,8192]{1,0:T(4,128)S(1)}, u32[]{:S(2)}, u32[]{:S(2)}) collective-permute-start(f32[4,8192]{1,0:T(4,128)S(1)} %pad_maximum_fusion.refs_0_.refs_1_), channel_id=1, source_target_pairs={{0,8},{2,10},{4,12},{6,14},{8,0},{10,2},{12,4},{14,6},{16,24},{18,... | collective-permute-start | bytes 393224 | tf_op jit(solution)/shard_map/ppermute | solution.py:209
  16.2 2.7 %collective-permute-start.4 = (f32[2080,128]{1,0:T(8,128)S(1)}, f32[2080,128]{1,0:T(8,128)S(1)}, u32[]{:S(2)}, u32[]{:S(2)}) collective-permute-start(f32[2080,128]{1,0:T(8,128)S(1)} %features.1.refs_4_), channel_id=1, source_target_pairs={{0,2},{2,0},{4,6},{6,4},{8,10},{10,8},{12,14},{14,12},{16,18},{18,... | collective-permute-start | bytes 3194888 | tf_op jit(solution)/shard_map/ppermute | solution.py:209

commit v6 on v5

--- a/solution.py
+++ b/solution.py
@@ -1,3 +1,5 @@
+import functools
+
 import jax
 import jax.numpy as jnp
 from jax import lax
@@ -48,12 +50,14 @@
     layers, r = precond_ref.shape[0], precond_ref.shape[-1]
     row, col = iota((r, r), 0), iota((r, r), 1)
     order = (col == 2 * (row % (r // 2)) + row // (r // 2)).astype(jnp.float32)
-    eye = (col == row).astype(jnp.float32)
     left = diagonal([exact(order, precond_ref[l, 0], NT) for l in range(layers)])
     left_ref[...] = jnp.concatenate(split(left), axis=0)
-    turned = [exact(eye, precond_ref[l, 1], NT) for l in range(layers)]
-    high, low = split(diagonal([jnp.concatenate([x, x], axis=1) for x in turned]))
-    right_ref[...] = jnp.concatenate([high, high, low], axis=0)
+    for l in range(layers):
+        high, low = split(diagonal([precond_ref[l, 1]] * 2))
+        zero = jnp.zeros_like(high)
+        right_ref[l] = jnp.concatenate(
+            [jnp.concatenate([high, low], axis=1), jnp.concatenate([high, zero], axis=1)], axis=0
+        )
 
 
 def outputs_kernel(len_ref, grad_ref, w_ref, left_ref, out_ref, raw_ref):
@@ -81,25 +85,23 @@
     lax.fori_loop(0, nb // STEP, turn, 0)
 
 
-def features_kernel(id_ref, act_ref, out_ref, w_ref, right_ref, feat_ref, in_ref):
+def features_kernel(id_ref, act_ref, out_ref, w_ref, feat_ref, in_ref):
     nb, size, depth = act_ref.shape
     width = out_ref.shape[1]
-    layers = right_ref.shape[1] // feat_ref.shape[1]
-    r = width // layers
-    half = r // 2
+    r = feat_ref.shape[1] // 2
+    layers, half = width // r, r // 2
     rows = SUB * size
     low_lane = iota((half, 2 * r), 1) < r
     lane_block = iota((r, rows), 1) // size
 
     def finish(i):
-        high, low = split(in_ref[i % 2])
-        proj_in = mm(jnp.concatenate([high, low], axis=1), right_ref[: 2 * width])
-        proj_in = proj_in + mm(high, right_ref[2 * width :])
+        proj_in = in_ref[i % 2]
         for s in range(WIDE // SUB):
             start = (i * WIDE + s * SUB) * size
             for l in range(layers):
                 outs = [out_ref[k, l * r : (l + 1) * r, start : start + rows] for k in (0, 1)]
-                ih, il = split(proj_in[s * rows : (s + 1) * rows, l * 2 * r : (l + 1) * 2 * r])
+                x = proj_in[s * rows : (s + 1) * rows, l * r : (l + 1) * r]
+                ih, il = split(jnp.concatenate([x, x], axis=1))
                 lhs = jnp.concatenate(
                     [
                         jnp.concatenate(
@@ -134,30 +136,38 @@
     feat_ref[layers * half * nb :] = id_ref[...]
 
 
-def products(pieces, feat_ref):
+def products(q_ref, feat_ref):
     lanes = feat_ref.shape[1]
-    groups = pieces[0].shape[1] // lanes
-    nb = feat_ref.shape[0] // (groups + 1)
-    count = sum(ref.shape[0] for ref in pieces)
+    groups = q_ref.shape[1] // lanes
+    nb = feat_ref.shape[0] // groups
+    count = q_ref.shape[0] // 2
     acc = jnp.zeros((2 * nb, 2 * count), jnp.float32)
     for g in range(0, groups, 2):
-        q = jnp.concatenate([ref[:, g * lanes : (g + 2) * lanes] for ref in pieces], axis=0)
         f = [feat_ref[pl.ds(g + d, nb, stride=groups), :] for d in (0, 1)]
-        f = jnp.concatenate(f, axis=1)
-        q, f = [jnp.concatenate(split(x), axis=0) for x in (q, f)]
-        acc = acc + mm(f, q, NT)
+        f = jnp.concatenate(split(jnp.concatenate(f, axis=1)), axis=0)
+        acc = acc + mm(f, q_ref[:, g * lanes : (g + 2) * lanes], NT)
     acc = acc[:nb] + acc[nb:]
     return acc[:, :count] + acc[:, count:]
 
 
 def own_scores_kernel(*refs):
-    *pieces, mine_ref, out_ref = refs
-    out_ref[...] = products(pieces, mine_ref)
-
-
-def scores_kernel(ex_count, tok_count, own, masks, place_ref, *refs):
-    *pieces, own_ref, dest_ref, other_ref, out_ref = refs
-    acc = jnp.concatenate([own_ref[...], products(pieces, other_ref)], axis=0)
+    *pieces, right_ref, mine_ref, score_ref, q_ref = refs
+    layers, lanes = right_ref.shape[0], mine_ref.shape[1]
+    groups = q_ref.shape[1] // lanes
+    count, some = q_ref.shape[0] // 2, groups // layers // 4
+    for begin in range(0, groups, some):
+        here = [slice(g * lanes, (g + 1) * lanes) for g in range(begin, begin + some)]
+        q = jnp.concatenate([ref[:, x] for x in here for ref in pieces], axis=0)
+        q = mm(jnp.concatenate(split(q), axis=1), right_ref[begin * layers // groups])
+        high, low = split(q[:, :lanes] + q[:, lanes:])
+        for k, x in enumerate(here):
+            rows = slice(k * count, (k + 1) * count)
+            q_ref[:, x] = jnp.concatenate([high[rows], low[rows]], axis=0)
+    score_ref[...] = products(q_ref, mine_ref)
+
+
+def scores_kernel(ex_count, tok_count, own, masks, place_ref, q_ref, own_ref, id_ref, other_ref, out_ref):
+    acc = jnp.concatenate([own_ref[...], products(q_ref, other_ref)], axis=0)
     blocks, count = acc.shape
 
     queries = own * ex_count
@@ -169,14 +179,15 @@
     order = (query == iota((count, queries), 1)).astype(jnp.float32).astype(jnp.bfloat16)
     high, low = split(acc)
     acc = mm(high, order) + mm(low, order)
-    targets = ex_count * tok_count
-    lane = iota((blocks, targets * EX_DEV), 1)
-    ids = [ref[ref.shape[0] - blocks // 2 :, :1] for ref in (dest_ref, other_ref)]
-    ids = jnp.concatenate(ids, axis=0).astype(jnp.int32)
-    owner = lane % targets // tok_count * EX_DEV + lane // targets == ids
+    targets = out_ref.shape[0]
+    last = other_ref.shape[0] - id_ref.shape[0]
+    ids = [ref[start : start + 1, : blocks // 2] for ref, start in ((id_ref, 0), (other_ref, last))]
+    ids = jnp.concatenate(ids, axis=1).astype(jnp.int32)
+    row = iota((targets * EX_DEV, blocks), 0)
+    owner = row % targets // tok_count * EX_DEV + row // targets == ids
     owner = owner.astype(jnp.float32).astype(jnp.bfloat16)
     high, low = split(acc)
-    full = mm(owner, high, TN) + mm(owner, low, TN)
+    full = mm(owner, high) + mm(owner, low)
     each = queries // tok_count
     tok = iota((targets * EX_DEV, each), 0) % tok_count
     result = full[:, :each]
@@ -213,7 +224,7 @@
         factors_kernel,
         out_shape=[
             jax.ShapeDtypeStruct((2 * width, width), jnp.bfloat16),
-            jax.ShapeDtypeStruct((3 * width, 2 * width), jnp.bfloat16),
+            jax.ShapeDtypeStruct((layers, 4 * r, 4 * r), jnp.bfloat16),
         ],
         compiler_params=pltpu.CompilerParams(vmem_limit_bytes=4 * 1024 * 1024),
         cost_estimate=pl.CostEstimate(flops=10**10, bytes_accessed=2**20, transcendentals=0),
@@ -241,34 +252,37 @@
     pieces = [held] + [swapped(held, m) for m in last]
     masks = tuple(mask ^ m for m in [0] + last for mask in masks)
 
-    ids = (block_dest * EX_DEV + block_slot[:, None]).astype(jnp.float32)
-    ids = jnp.broadcast_to(ids, (nb, 2 * r))
+    ids = (block_dest[:, 0] * EX_DEV + block_slot).astype(jnp.float32)
+    ids = jnp.broadcast_to(jnp.pad(ids, (0, 2 * r - nb))[None], (8, 2 * r))
     mine = pl.pallas_call(
         features_kernel,
-        in_specs=[pl.BlockSpec(), VMEM, pl.BlockSpec(), VMEM, pl.BlockSpec()],
-        out_shape=jax.ShapeDtypeStruct(((layers * half + 1) * nb, 2 * r), jnp.float32),
+        in_specs=[pl.BlockSpec(), VMEM, pl.BlockSpec(), VMEM],
+        out_shape=jax.ShapeDtypeStruct((layers * half * nb + 8, 2 * r), jnp.float32),
         scratch_shapes=[pltpu.VMEM((2, WIDE * size, width), jnp.float32)],
         compiler_params=pltpu.CompilerParams(vmem_limit_bytes=12 * 1024 * 1024),
         cost_estimate=pl.CostEstimate(flops=10**10, bytes_accessed=2**20, transcendentals=0),
         name="features",
-    )(ids, activations, outs, in_proj, right)
+    )(ids, activations, outs, in_proj)
 
     other = swapped(mine, 1)
 
     each = own * ex_count // tok_count
-    own_scores = pl.pallas_call(
+    own_scores, split_queries = pl.pallas_call(
         own_scores_kernel,
-        out_shape=jax.ShapeDtypeStruct((nb, own * len(masks)), jnp.float32),
+        out_shape=[
+            jax.ShapeDtypeStruct((nb, own * len(masks)), jnp.float32),
+            jax.ShapeDtypeStruct((2 * own * len(masks), query_grads.shape[1]), jnp.bfloat16),
+        ],
         compiler_params=pltpu.CompilerParams(vmem_limit_bytes=8 * 1024 * 1024),
         cost_estimate=pl.CostEstimate(flops=10**10, bytes_accessed=2**20, transcendentals=0),
         name="own_scores",
-    )(*pieces, mine)
+    )(*pieces, right, mine)
     chunks = pl.pallas_call(
-        lambda *refs: scores_kernel(ex_count, tok_count, own, masks, *refs),
+        functools.partial(scores_kernel, ex_count, tok_count, own, masks),
         out_shape=jax.ShapeDtypeStruct((ex_count * tok_count, EX_DEV * each), jnp.float32),
         compiler_params=pltpu.CompilerParams(vmem_limit_bytes=8 * 1024 * 1024),
         name="scores",
-    )(jnp.full((1, 2 * r), place), *pieces, own_scores, ids, other)
+    )(jnp.full((1, 2 * r), place), split_queries, own_scores, ids, other)
     arrived = lax.all_to_all(chunks, ("ex", "tok"), split_axis=0, concat_axis=0, tiled=True)
     total = jnp.sum(arrived, axis=0) * (1.0 / (r * size))
     return total.reshape(EX_DEV, each).T

time: 32.7 us -> 32.1 us (0.982)
  blocking collectives: 11.6 us -> 11.1 us
  Pallas kernels: 9.16 us -> 8.78 us
    all_to_all x1, blocking collectives: 11.6 us -> 11.1 us  [on_device(): lax.all_to_all(chunks, ('ex', 'tok'), split_axis=0, concat_axis=0, tiled=...]
    pallas_call x1, Pallas kernels: 3.56 us -> 3.06 us  [on_device(): pl.pallas_call(features_kernel, in_specs=[pl.BlockSpec(), VMEM, pl.BlockS...]
  transfers between devices with their start and end apart: 5 -> 5, of which waited for: 3 -> 2; matrix products, arithmetic and copies ran while one was open for 0% -> 0% of each run, Pallas kernels for 24% -> 24%
where the time goes in v6:
time: 32.1 us; the launch traced here: 31.9 us
  blocking collectives  11.1 us (35%)
  Pallas kernels  8.78 us (27%)
  starting transfers between devices  7.66 us (24%)
  waiting for transfers between devices  2.06 us (6%)
  local copies, waits for them, and re-layouts  2.03 us (6%)
    all_to_all x1, blocking collectives, on_device(): lax.all_to_all(chunks, ('ex', 'tok'), split_axis=0, concat_axis=0, tiled=...  11.1 us
    ppermute x5, starting transfers between devices, swapped(): return lax.ppermute(x, 'ex', [(i, i ^ mask) for i in range(ex_count)])  7.66 us
    pallas_call x1, Pallas kernels, on_device(): pl.pallas_call(outputs_kernel, in_specs=[pl.BlockSpec(), VMEM, pl.BlockSp...  3.14 us
    pallas_call x1, Pallas kernels, on_device(): pl.pallas_call(features_kernel, in_specs=[pl.BlockSpec(), VMEM, pl.BlockS...  3.06 us
    ppermute x5, waiting for transfers between devices, swapped(): return lax.ppermute(x, 'ex', [(i, i ^ mask) for i in range(ex_count)])  2.06 us
    unnamed x20, local copies, waits for them, and re-layouts  1.29 us
    pallas_call x1, Pallas kernels, on_device(): pl.pallas_call(functools.partial(scores_kernel, ex_count, tok_count, own,...  1.21 us
    pallas_call x1, Pallas kernels, on_device(): pl.pallas_call(own_scores_kernel, out_shape=[jax.ShapeDtypeStruct((nb, ow...  1.07 us
  transfers between devices with their start and end apart: 5, of which 2 were waited for; matrix products, arithmetic and copies ran while one was open for 0% of the time, Pallas kernels for 24%

profile of v6, /device:TPU:0, one launch (start us, length us, event | category | flops | bytes accessed | tf_op | source)
XLA Modules:
  0.0 31.9 jit_solution(650070046860210407)
XLA Ops:
  0.0 0.0 copy-start.2
  0.0 0.0 copy-start
  0.0 4.0 %collective-permute-start = (f32[2,8192]{1,0:T(2,128)}, f32[2,8192]{1,0:T(2,128)S(1)}, u32[]{:S(2)}, u32[]{:S(2)}) collective-permute-start(f32[2,8192]{1,0:T(2,128)} %param.16), channel_id=1, source_target_pairs={{0,16},{2,18},{4,20},{6,22},{8,24},{10,26},{12,28},{14,30},{16,0},... | collective-permute-start | bytes 196616 | tf_op jit(solution)/shard_map/ppermute | solution.py:220
  4.0 0.0 copy-start.3
  4.0 0.9 %copy-done.3 = f32[2,2,64,64]{3,2,1,0:T(8,128)S(1)} copy-done((f32[2,2,64,64]{3,2,1,0:T(8,128)S(1)}, f32[2,2,64,64]{3,2,1,0:T(8,128)}, u32[]{:S(2)}) %copy-start.3) | copy-done | bytes 65560
  4.9 0.0 copy-start.5
  4.9 0.0 slice-start
  5.0 0.3 factors.1
  5.3 0.3 %copy-done.5 = s32[32]{0:T(128)S(1)} copy-done((s32[32]{0:T(128)S(1)}, s32[32]{0:T(128)}, u32[]{:S(2)}) %copy-start.5) | copy-done | bytes 152
  5.6 0.1 broadcast_in_dim.7.len_ref
  5.7 0.0 copy-done.2
  5.7 0.0 copy-done
  5.7 0.0 copy-start.6
  5.7 0.0 copy-start.7
  5.7 0.0 copy-start.4
  5.7 0.0 slice-start.1
  5.7 0.0 copy-start.1
  5.7 3.1 %outputs.1.out_ref = bf16[2,128,1024]{2,1,0:T(8,128)(2,1)S(1)} custom-call(s32[32,128]{1,0:T(8,128)S(1)} %broadcast_in_dim.7.len_ref, bf16[32,32,2,1024]{3,2,1,0:T(2,128)(2,1)S(1)} %copy-done, bf16[128,1024]{1,0:T(8,128)(2,1)S(1)} %bitcast.14, bf16[256,128]{1,0:T(8,128)(2,1)S(1)} %get-tuple-element.11.left_ref), custom_call_target="tpu_custom_call" | custom-call | flops 10000000000 | bytes 1048576 | tf_op jit(solution)/shard_map/outputs/pallas_call | solution.py:234
  8.9 0.0 copy-done.6
  8.9 0.0 copy-done.7
  8.9 0.0 collective-permute-done
  8.9 0.0 copy-done.4
  8.9 0.1 pad_maximum_fusion.refs_0_
  9.0 2.6 %collective-permute-start.1 = (f32[4,8192]{1,0:T(4,128)S(1)}, f32[4,8192]{1,0:T(4,128)S(1)}, u32[]{:S(2)}, u32[]{:S(2)}) collective-permute-start(f32[4,8192]{1,0:T(4,128)S(1)} %pad_maximum_fusion.refs_0_), channel_id=1, source_target_pairs={{0,12},{2,14},{4,8},{6,10},{8,4},{10,6},{12,0},{14,2},{16,28},{18,... | collective-permute-start | bytes 393224 | tf_op jit(solution)/shard_map/ppermute | solution.py:220
  11.6 0.5 %collective-permute-start.2 = (f32[4,8192]{1,0:T(4,128)S(1)}, f32[4,8192]{1,0:T(4,128)S(1)}, u32[]{:S(2)}, u32[]{:S(2)}) collective-permute-start(f32[4,8192]{1,0:T(4,128)S(1)} %pad_maximum_fusion.refs_0_), channel_id=1, source_target_pairs={{0,4},{2,6},{4,0},{6,2},{8,12},{10,14},{12,8},{14,10},{16,20},{18,... | collective-permute-start | bytes 393224 | tf_op jit(solution)/shard_map/ppermute | solution.py:220
  12.1 0.4 %collective-permute-start.3 = (f32[4,8192]{1,0:T(4,128)S(1)}, f32[4,8192]{1,0:T(4,128)S(1)}, u32[]{:S(2)}, u32[]{:S(2)}) collective-permute-start(f32[4,8192]{1,0:T(4,128)S(1)} %pad_maximum_fusion.refs_0_), channel_id=1, source_target_pairs={{0,8},{2,10},{4,12},{6,14},{8,0},{10,2},{12,4},{14,6},{16,24},{18,... | collective-permute-start | bytes 393224 | tf_op jit(solution)/shard_map/ppermute | solution.py:220
  12.6 0.0 slice-done
  12.6 0.0 slice-done.1
  12.6 0.0 copy-done.1
  12.6 3.1 %features.1.refs_5_ = f32[2056,128]{1,0:T(8,128)S(1)} custom-call(f32[8,128]{1,0:T(8,128)S(1)} %broadcast_in_dim.8.id_ref, bf16[32,32,4096]{2,1,0:T(8,128)(2,1)S(1)} %bitcast.13, bf16[2,128,1024]{2,1,0:T(8,128)(2,1)S(1)} %outputs.1.out_ref, bf16[4096,128]{1,0:T(8,128)(2,1)S(1)} %copy-done.1), custom_call_target="tpu_custom_call" | custom-call | flops 10000000000 | bytes 1048576 | tf_op jit(solution)/shard_map/features/pallas_call | solution.py:257
  15.7 0.1 collective-permute-start.4
  15.7 0.0 collective-permute-done.1.refs_1_
  15.7 2.0 %collective-permute-done.2.refs_2_ = f32[4,8192]{1,0:T(4,128)S(1)} collective-permute-done((f32[4,8192]{1,0:T(4,128)S(1)}, f32[4,8192]{1,0:T(4,128)S(1)}, u32[]{:S(2)}, u32[]{:S(2)}) %collective-permute-start.2) | collective-permute-done | bytes 131104 | tf_op jit(solution)/shard_map/ppermute | solution.py:220
  17.7 0.1 collective-permute-done.3.refs_3_
  17.8 1.1 %own_scores.1 = (f32[32,16]{1,0:T(8,128)S(1)}, bf16[32,8192]{1,0:T(8,128)(2,1)S(1)}) custom-call(f32[4,8192]{1,0:T(4,128)S(1)} %pad_maximum_fusion.refs_0_, f32[4,8192]{1,0:T(4,128)S(1)} %collective-permute-done.1.refs_1_, f32[4,8192]{1,0:T(4,128)S(1)} %collective-permute-done.2.refs_2_, f32[4,8192]{1,0:T(4,128)S(1)} %collective-permute-done.3.refs_3_, ...), custom_call_target="tpu_custom_call" | custom-call | flops 10000000000 | bytes 1048576 | tf_op jit(solution)/shard_map/own_scores/pallas_call | solution.py:270
  18.9 0.0 collective-permute-done.4.other_ref
  18.9 1.2 %scores.1 = f32[32,64]{1,0:T(8,128)S(1)} custom-call(s32[1,128]{1,0:T(1,128)S(1)} %broadcast_in_dim.6.place_ref, bf16[32,8192]{1,0:T(8,128)(2,1)S(1)} %get-tuple-element.15.q_ref, f32[32,16]{1,0:T(8,128)S(1)} %get-tuple-element.16.own_ref, f32[8,128]{1,0:T(8,128)S(1)} %broadcast_in_dim.8.id_ref, f32[2056,128]{1,0:T(8,128)S(1)} %collective-permute-done.4.other_ref), custom_call_target="tpu_custom_call" | custom-call | tf_op jit(solution)/shard_map/scores/pallas_call | solution.py:280
  20.1 11.1 %all_to_all.9 = f32[32,1,64]{2,1,0:T(1,128)S(1)} all-to-all(f32[32,1,64]{2,1,0:T(1,128)S(1)} %bitcast.11), channel_id=1, replica_groups=mesh['ex'=16,'tok'=2] {'ex','tok'}, dimensions={0} | all-to-all | bytes 16384 | tf_op jit(solution)/shard_map/all_to_all | solution.py:286
  31.2 0.1 reduce_sum.9
  31.3 0.7 %mul.24 = f32[4,16]{1,0:T(4,128)} reshape(f32[64]{0:T(128)S(1)} %broadcast_multiply_fusion) | data formatting | bytes 512 | tf_op jit(solution)/shard_map/mul | solution.py:287
  (6 shorter events, 0.0 us)
Async XLA Ops:
  0.0 5.7 %copy-start.2 = (bf16[2,1024,64]{1,2,0:T(8,128)(2,1)S(1)}, bf16[2,1024,64]{1,2,0:T(8,128)(2,1)}, u32[]{:S(2)}) copy-start(bf16[2,1024,64]{1,2,0:T(8,128)(2,1)} %param.15) | copy-start | bytes 786436
  0.0 5.7 %copy-start = (bf16[32,32,2,1024]{3,2,1,0:T(2,128)(2,1)S(1)}, bf16[32,32,2,1024]{3,2,1,0:T(2,128)(2,1)}, u32[]{:S(2)}) copy-start(bf16[32,32,2,1024]{3,2,1,0:T(2,128)(2,1)} %grad_ref.1) | copy-start | bytes 12582916
  0.0 8.9 %collective-permute-start = (f32[2,8192]{1,0:T(2,128)}, f32[2,8192]{1,0:T(2,128)S(1)}, u32[]{:S(2)}, u32[]{:S(2)}) collective-permute-start(f32[2,8192]{1,0:T(2,128)} %param.16), channel_id=1, source_target_pairs={{0,16},{2,18},{4,20},{6,22},{8,24},{10,26},{12,28},{14,30},{16,0},... | collective-permute-start | bytes 196616 | tf_op jit(solution)/shard_map/ppermute | solution.py:220
  4.0 0.9 %copy-start.3 = (f32[2,2,64,64]{3,2,1,0:T(8,128)S(1)}, f32[2,2,64,64]{3,2,1,0:T(8,128)}, u32[]{:S(2)}) copy-start(f32[2,2,64,64]{3,2,1,0:T(8,128)} %precond_ref.1) | copy-start | bytes 196612
  4.9 0.7 %copy-start.5 = (s32[32]{0:T(128)S(1)}, s32[32]{0:T(128)}, u32[]{:S(2)}) copy-start(s32[32]{0:T(128)} %param.11) | copy-start | bytes 388
  4.9 7.6 %slice-start = ((s8[8388608]{0:T(1024)(128)(4,1)}), s8[4194304]{0:T(1024)(128)(4,1)S(1)}, s32[]{:S(2)}) async-start(s8[8388608]{0:T(1024)(128)(4,1)} %bitcast.12), calls=%async_computation.1 | async-start | bytes 8388608
  5.7 3.2 %copy-start.6 = (s32[32]{0:T(128)S(1)}, s32[32]{0:T(128)}, u32[]{:S(2)}) copy-start(s32[32]{0:T(128)} %param.13) | copy-start | bytes 388
  5.7 3.2 %copy-start.7 = (s32[32,1]{0,1:T(1,128)S(1)}, s32[32,1]{0,1:T(1,128)}, u32[]{:S(2)}) copy-start(s32[32,1]{0,1:T(1,128)} %param.12) | copy-start | bytes 388
  5.7 3.2 %copy-start.4 = (f32[2,8192]{1,0:T(2,128)S(1)}, f32[2,8192]{1,0:T(2,128)}, u32[]{:S(2)}) copy-start(f32[2,8192]{1,0:T(2,128)} %param.16) | copy-start | bytes 196612
  5.7 6.9 %slice-start.1 = ((s8[8388608]{0:T(1024)(128)(4,1)}), s8[4194304]{0:T(1024)(128)(4,1)S(1)}, s32[]{:S(2)}) async-start(s8[8388608]{0:T(1024)(128)(4,1)} %bitcast.12), calls=%async_computation.2 | async-start | bytes 8388608
  5.7 6.9 %copy-start.1 = (bf16[4096,128]{1,0:T(8,128)(2,1)S(1)}, bf16[4096,128]{1,0:T(8,128)(2,1)}, u32[]{:S(2)}) copy-start(bf16[4096,128]{1,0:T(8,128)(2,1)} %w_ref.1) | copy-start | bytes 3145732
  9.0 6.7 %collective-permute-start.1 = (f32[4,8192]{1,0:T(4,128)S(1)}, f32[4,8192]{1,0:T(4,128)S(1)}, u32[]{:S(2)}, u32[]{:S(2)}) collective-permute-start(f32[4,8192]{1,0:T(4,128)S(1)} %pad_maximum_fusion.refs_0_), channel_id=1, source_target_pairs={{0,12},{2,14},{4,8},{6,10},{8,4},{10,6},{12,0},{14,2},{16,28},{18,... | collective-permute-start | bytes 393224 | tf_op jit(solution)/shard_map/ppermute | solution.py:220
  11.6 6.1 %collective-permute-start.2 = (f32[4,8192]{1,0:T(4,128)S(1)}, f32[4,8192]{1,0:T(4,128)S(1)}, u32[]{:S(2)}, u32[]{:S(2)}) collective-permute-start(f32[4,8192]{1,0:T(4,128)S(1)} %pad_maximum_fusion.refs_0_), channel_id=1, source_target_pairs={{0,4},{2,6},{4,0},{6,2},{8,12},{10,14},{12,8},{14,10},{16,20},{18,... | collective-permute-start | bytes 393224 | tf_op jit(solution)/shard_map/ppermute | solution.py:220
  12.1 5.7 %collective-permute-start.3 = (f32[4,8192]{1,0:T(4,128)S(1)}, f32[4,8192]{1,0:T(4,128)S(1)}, u32[]{:S(2)}, u32[]{:S(2)}) collective-permute-start(f32[4,8192]{1,0:T(4,128)S(1)} %pad_maximum_fusion.refs_0_), channel_id=1, source_target_pairs={{0,8},{2,10},{4,12},{6,14},{8,0},{10,2},{12,4},{14,6},{16,24},{18,... | collective-permute-start | bytes 393224 | tf_op jit(solution)/shard_map/ppermute | solution.py:220
  15.7 3.2 %collective-permute-start.4 = (f32[2056,128]{1,0:T(8,128)S(1)}, f32[2056,128]{1,0:T(8,128)S(1)}, u32[]{:S(2)}, u32[]{:S(2)}) collective-permute-start(f32[2056,128]{1,0:T(8,128)S(1)} %features.1.refs_5_), channel_id=1, source_target_pairs={{0,2},{2,0},{4,6},{6,4},{8,10},{10,8},{12,14},{14,12},{16,18},{18,... | collective-permute-start | bytes 3158024 | tf_op jit(solution)/shard_map/ppermute | solution.py:220

commit v7 on v6

--- a/solution.py
+++ b/solution.py
@@ -10,7 +10,7 @@
 EX_DEV = 4
 SUB = 4
 STEP = 8
-WIDE = 16
+WIDE = 8
 HIGHEST = lax.Precision.HIGHEST
 PLAIN = (((1,), (0,)), ((), ()))
 NT = (((1,), (1,)), ((), ()))
@@ -154,7 +154,7 @@
     *pieces, right_ref, mine_ref, score_ref, q_ref = refs
     layers, lanes = right_ref.shape[0], mine_ref.shape[1]
     groups = q_ref.shape[1] // lanes
-    count, some = q_ref.shape[0] // 2, groups // layers // 4
+    count, some = q_ref.shape[0] // 2, groups // layers // 2
     for begin in range(0, groups, some):
         here = [slice(g * lanes, (g + 1) * lanes) for g in range(begin, begin + some)]
         q = jnp.concatenate([ref[:, x] for x in here for ref in pieces], axis=0)

time: 32.1 us -> 32 us (level)
  no operation moved by 1% of the time
where the time goes in v7:
time: 32 us; the launch traced here: 31.8 us
  blocking collectives  11 us (34%)
  Pallas kernels  8.7 us (27%)
  starting transfers between devices  7.66 us (24%)
  waiting for transfers between devices  2.14 us (7%)
  local copies, waits for them, and re-layouts  2.03 us (6%)
    all_to_all x1, blocking collectives, on_device(): lax.all_to_all(chunks, ('ex', 'tok'), split_axis=0, concat_axis=0, tiled=...  11 us
    ppermute x5, starting transfers between devices, swapped(): return lax.ppermute(x, 'ex', [(i, i ^ mask) for i in range(ex_count)])  7.66 us
    pallas_call x1, Pallas kernels, on_device(): pl.pallas_call(outputs_kernel, in_specs=[pl.BlockSpec(), VMEM, pl.BlockSp...  3.14 us
    pallas_call x1, Pallas kernels, on_device(): pl.pallas_call(features_kernel, in_specs=[pl.BlockSpec(), VMEM, pl.BlockS...  2.99 us
    ppermute x5, waiting for transfers between devices, swapped(): return lax.ppermute(x, 'ex', [(i, i ^ mask) for i in range(ex_count)])  2.14 us
    unnamed x20, local copies, waits for them, and re-layouts  1.29 us
    pallas_call x1, Pallas kernels, on_device(): pl.pallas_call(functools.partial(scores_kernel, ex_count, tok_count, own,...  1.21 us
    pallas_call x1, Pallas kernels, on_device(): pl.pallas_call(own_scores_kernel, out_shape=[jax.ShapeDtypeStruct((nb, ow...  1.07 us
  transfers between devices with their start and end apart: 5, of which 2 were waited for; matrix products, arithmetic and copies ran while one was open for 0% of the time, Pallas kernels for 24%

profile of v7, /device:TPU:0, one launch (start us, length us, event | category | flops | bytes accessed | tf_op | source)
XLA Modules:
  0.0 31.8 jit_solution(5068593008331088124)
XLA Ops:
  0.0 0.0 copy-start.2
  0.0 0.0 copy-start
  0.0 4.0 %collective-permute-start = (f32[2,8192]{1,0:T(2,128)}, f32[2,8192]{1,0:T(2,128)S(1)}, u32[]{:S(2)}, u32[]{:S(2)}) collective-permute-start(f32[2,8192]{1,0:T(2,128)} %param.16), channel_id=1, source_target_pairs={{0,16},{2,18},{4,20},{6,22},{8,24},{10,26},{12,28},{14,30},{16,0},... | collective-permute-start | bytes 196616 | tf_op jit(solution)/shard_map/ppermute | solution.py:220
  4.0 0.0 copy-start.3
  4.0 0.9 %copy-done.3 = f32[2,2,64,64]{3,2,1,0:T(8,128)S(1)} copy-done((f32[2,2,64,64]{3,2,1,0:T(8,128)S(1)}, f32[2,2,64,64]{3,2,1,0:T(8,128)}, u32[]{:S(2)}) %copy-start.3) | copy-done | bytes 65560
  4.9 0.0 copy-start.5
  4.9 0.0 slice-start
  5.0 0.3 factors.1
  5.3 0.3 %copy-done.5 = s32[32]{0:T(128)S(1)} copy-done((s32[32]{0:T(128)S(1)}, s32[32]{0:T(128)}, u32[]{:S(2)}) %copy-start.5) | copy-done | bytes 152
  5.6 0.1 broadcast_in_dim.7.len_ref
  5.7 0.0 copy-done.2
  5.7 0.0 copy-done
  5.7 0.0 copy-start.6
  5.7 0.0 copy-start.7
  5.7 0.0 copy-start.4
  5.7 0.0 slice-start.1
  5.7 0.0 copy-start.1
  5.7 3.1 %outputs.1.out_ref = bf16[2,128,1024]{2,1,0:T(8,128)(2,1)S(1)} custom-call(s32[32,128]{1,0:T(8,128)S(1)} %broadcast_in_dim.7.len_ref, bf16[32,32,2,1024]{3,2,1,0:T(2,128)(2,1)S(1)} %copy-done, bf16[128,1024]{1,0:T(8,128)(2,1)S(1)} %bitcast.14, bf16[256,128]{1,0:T(8,128)(2,1)S(1)} %get-tuple-element.11.left_ref), custom_call_target="tpu_custom_call" | custom-call | flops 10000000000 | bytes 1048576 | tf_op jit(solution)/shard_map/outputs/pallas_call | solution.py:234
  8.9 0.0 copy-done.6
  8.9 0.0 copy-done.7
  8.9 0.0 collective-permute-done
  8.9 0.0 copy-done.4
  8.9 0.1 pad_maximum_fusion.refs_0_
  9.0 2.6 %collective-permute-start.1 = (f32[4,8192]{1,0:T(4,128)S(1)}, f32[4,8192]{1,0:T(4,128)S(1)}, u32[]{:S(2)}, u32[]{:S(2)}) collective-permute-start(f32[4,8192]{1,0:T(4,128)S(1)} %pad_maximum_fusion.refs_0_), channel_id=1, source_target_pairs={{0,12},{2,14},{4,8},{6,10},{8,4},{10,6},{12,0},{14,2},{16,28},{18,... | collective-permute-start | bytes 393224 | tf_op jit(solution)/shard_map/ppermute | solution.py:220
  11.6 0.5 %collective-permute-start.2 = (f32[4,8192]{1,0:T(4,128)S(1)}, f32[4,8192]{1,0:T(4,128)S(1)}, u32[]{:S(2)}, u32[]{:S(2)}) collective-permute-start(f32[4,8192]{1,0:T(4,128)S(1)} %pad_maximum_fusion.refs_0_), channel_id=1, source_target_pairs={{0,4},{2,6},{4,0},{6,2},{8,12},{10,14},{12,8},{14,10},{16,20},{18,... | collective-permute-start | bytes 393224 | tf_op jit(solution)/shard_map/ppermute | solution.py:220
  12.1 0.4 %collective-permute-start.3 = (f32[4,8192]{1,0:T(4,128)S(1)}, f32[4,8192]{1,0:T(4,128)S(1)}, u32[]{:S(2)}, u32[]{:S(2)}) collective-permute-start(f32[4,8192]{1,0:T(4,128)S(1)} %pad_maximum_fusion.refs_0_), channel_id=1, source_target_pairs={{0,8},{2,10},{4,12},{6,14},{8,0},{10,2},{12,4},{14,6},{16,24},{18,... | collective-permute-start | bytes 393224 | tf_op jit(solution)/shard_map/ppermute | solution.py:220
  12.6 0.0 slice-done
  12.6 0.0 slice-done.1
  12.6 0.0 copy-done.1
  12.6 3.0 %features.1.refs_5_ = f32[2056,128]{1,0:T(8,128)S(1)} custom-call(f32[8,128]{1,0:T(8,128)S(1)} %broadcast_in_dim.8.id_ref, bf16[32,32,4096]{2,1,0:T(8,128)(2,1)S(1)} %bitcast.13, bf16[2,128,1024]{2,1,0:T(8,128)(2,1)S(1)} %outputs.1.out_ref, bf16[4096,128]{1,0:T(8,128)(2,1)S(1)} %copy-done.1), custom_call_target="tpu_custom_call" | custom-call | flops 10000000000 | bytes 1048576 | tf_op jit(solution)/shard_map/features/pallas_call | solution.py:257
  15.6 0.1 collective-permute-start.4
  15.7 0.0 collective-permute-done.1.refs_1_
  15.7 2.1 %collective-permute-done.2.refs_2_ = f32[4,8192]{1,0:T(4,128)S(1)} collective-permute-done((f32[4,8192]{1,0:T(4,128)S(1)}, f32[4,8192]{1,0:T(4,128)S(1)}, u32[]{:S(2)}, u32[]{:S(2)}) %collective-permute-start.2) | collective-permute-done | bytes 131104 | tf_op jit(solution)/shard_map/ppermute | solution.py:220
  17.7 0.1 collective-permute-done.3.refs_3_
  17.8 1.1 %own_scores.1 = (f32[32,16]{1,0:T(8,128)S(1)}, bf16[32,8192]{1,0:T(8,128)(2,1)S(1)}) custom-call(f32[4,8192]{1,0:T(4,128)S(1)} %pad_maximum_fusion.refs_0_, f32[4,8192]{1,0:T(4,128)S(1)} %collective-permute-done.1.refs_1_, f32[4,8192]{1,0:T(4,128)S(1)} %collective-permute-done.2.refs_2_, f32[4,8192]{1,0:T(4,128)S(1)} %collective-permute-done.3.refs_3_, ...), custom_call_target="tpu_custom_call" | custom-call | flops 10000000000 | bytes 1048576 | tf_op jit(solution)/shard_map/own_scores/pallas_call | solution.py:270
  18.9 0.0 collective-permute-done.4.other_ref
  18.9 1.2 %scores.1 = f32[32,64]{1,0:T(8,128)S(1)} custom-call(s32[1,128]{1,0:T(1,128)S(1)} %broadcast_in_dim.6.place_ref, bf16[32,8192]{1,0:T(8,128)(2,1)S(1)} %get-tuple-element.15.q_ref, f32[32,16]{1,0:T(8,128)S(1)} %get-tuple-element.16.own_ref, f32[8,128]{1,0:T(8,128)S(1)} %broadcast_in_dim.8.id_ref, f32[2056,128]{1,0:T(8,128)S(1)} %collective-permute-done.4.other_ref), custom_call_target="tpu_custom_call" | custom-call | tf_op jit(solution)/shard_map/scores/pallas_call | solution.py:280
  20.1 11.0 %all_to_all.9 = f32[32,1,64]{2,1,0:T(1,128)S(1)} all-to-all(f32[32,1,64]{2,1,0:T(1,128)S(1)} %bitcast.11), channel_id=1, replica_groups=mesh['ex'=16,'tok'=2] {'ex','tok'}, dimensions={0} | all-to-all | bytes 16384 | tf_op jit(solution)/shard_map/all_to_all | solution.py:286
  31.1 0.1 reduce_sum.9
  31.2 0.7 %mul.24 = f32[4,16]{1,0:T(4,128)} reshape(f32[64]{0:T(128)S(1)} %broadcast_multiply_fusion) | data formatting | bytes 512 | tf_op jit(solution)/shard_map/mul | solution.py:287
  (6 shorter events, 0.0 us)
Async XLA Ops:
  0.0 5.7 %copy-start.2 = (bf16[2,1024,64]{1,2,0:T(8,128)(2,1)S(1)}, bf16[2,1024,64]{1,2,0:T(8,128)(2,1)}, u32[]{:S(2)}) copy-start(bf16[2,1024,64]{1,2,0:T(8,128)(2,1)} %param.15) | copy-start | bytes 786436
  0.0 5.7 %copy-start = (bf16[32,32,2,1024]{3,2,1,0:T(2,128)(2,1)S(1)}, bf16[32,32,2,1024]{3,2,1,0:T(2,128)(2,1)}, u32[]{:S(2)}) copy-start(bf16[32,32,2,1024]{3,2,1,0:T(2,128)(2,1)} %grad_ref.1) | copy-start | bytes 12582916
  0.0 8.9 %collective-permute-start = (f32[2,8192]{1,0:T(2,128)}, f32[2,8192]{1,0:T(2,128)S(1)}, u32[]{:S(2)}, u32[]{:S(2)}) collective-permute-start(f32[2,8192]{1,0:T(2,128)} %param.16), channel_id=1, source_target_pairs={{0,16},{2,18},{4,20},{6,22},{8,24},{10,26},{12,28},{14,30},{16,0},... | collective-permute-start | bytes 196616 | tf_op jit(solution)/shard_map/ppermute | solution.py:220
  4.0 0.9 %copy-start.3 = (f32[2,2,64,64]{3,2,1,0:T(8,128)S(1)}, f32[2,2,64,64]{3,2,1,0:T(8,128)}, u32[]{:S(2)}) copy-start(f32[2,2,64,64]{3,2,1,0:T(8,128)} %precond_ref.1) | copy-start | bytes 196612
  4.9 0.7 %copy-start.5 = (s32[32]{0:T(128)S(1)}, s32[32]{0:T(128)}, u32[]{:S(2)}) copy-start(s32[32]{0:T(128)} %param.11) | copy-start | bytes 388
  4.9 7.6 %slice-start = ((s8[8388608]{0:T(1024)(128)(4,1)}), s8[4194304]{0:T(1024)(128)(4,1)S(1)}, s32[]{:S(2)}) async-start(s8[8388608]{0:T(1024)(128)(4,1)} %bitcast.12), calls=%async_computation.1 | async-start | bytes 8388608
  5.7 3.2 %copy-start.6 = (s32[32]{0:T(128)S(1)}, s32[32]{0:T(128)}, u32[]{:S(2)}) copy-start(s32[32]{0:T(128)} %param.13) | copy-start | bytes 388
  5.7 3.2 %copy-start.7 = (s32[32,1]{0,1:T(1,128)S(1)}, s32[32,1]{0,1:T(1,128)}, u32[]{:S(2)}) copy-start(s32[32,1]{0,1:T(1,128)} %param.12) | copy-start | bytes 388
  5.7 3.2 %copy-start.4 = (f32[2,8192]{1,0:T(2,128)S(1)}, f32[2,8192]{1,0:T(2,128)}, u32[]{:S(2)}) copy-start(f32[2,8192]{1,0:T(2,128)} %param.16) | copy-start | bytes 196612
  5.7 6.9 %slice-start.1 = ((s8[8388608]{0:T(1024)(128)(4,1)}), s8[4194304]{0:T(1024)(128)(4,1)S(1)}, s32[]{:S(2)}) async-start(s8[8388608]{0:T(1024)(128)(4,1)} %bitcast.12), calls=%async_computation.2 | async-start | bytes 8388608
  5.7 6.9 %copy-start.1 = (bf16[4096,128]{1,0:T(8,128)(2,1)S(1)}, bf16[4096,128]{1,0:T(8,128)(2,1)}, u32[]{:S(2)}) copy-start(bf16[4096,128]{1,0:T(8,128)(2,1)} %w_ref.1) | copy-start | bytes 3145732
  9.0 6.7 %collective-permute-start.1 = (f32[4,8192]{1,0:T(4,128)S(1)}, f32[4,8192]{1,0:T(4,128)S(1)}, u32[]{:S(2)}, u32[]{:S(2)}) collective-permute-start(f32[4,8192]{1,0:T(4,128)S(1)} %pad_maximum_fusion.refs_0_), channel_id=1, source_target_pairs={{0,12},{2,14},{4,8},{6,10},{8,4},{10,6},{12,0},{14,2},{16,28},{18,... | collective-permute-start | bytes 393224 | tf_op jit(solution)/shard_map/ppermute | solution.py:220
  11.6 6.1 %collective-permute-start.2 = (f32[4,8192]{1,0:T(4,128)S(1)}, f32[4,8192]{1,0:T(4,128)S(1)}, u32[]{:S(2)}, u32[]{:S(2)}) collective-permute-start(f32[4,8192]{1,0:T(4,128)S(1)} %pad_maximum_fusion.refs_0_), channel_id=1, source_target_pairs={{0,4},{2,6},{4,0},{6,2},{8,12},{10,14},{12,8},{14,10},{16,20},{18,... | collective-permute-start | bytes 393224 | tf_op jit(solution)/shard_map/ppermute | solution.py:220
  12.1 5.7 %collective-permute-start.3 = (f32[4,8192]{1,0:T(4,128)S(1)}, f32[4,8192]{1,0:T(4,128)S(1)}, u32[]{:S(2)}, u32[]{:S(2)}) collective-permute-start(f32[4,8192]{1,0:T(4,128)S(1)} %pad_maximum_fusion.refs_0_), channel_id=1, source_target_pairs={{0,8},{2,10},{4,12},{6,14},{8,0},{10,2},{12,4},{14,6},{16,24},{18,... | collective-permute-start | bytes 393224 | tf_op jit(solution)/shard_map/ppermute | solution.py:220
  15.6 3.3 %collective-permute-start.4 = (f32[2056,128]{1,0:T(8,128)S(1)}, f32[2056,128]{1,0:T(8,128)S(1)}, u32[]{:S(2)}, u32[]{:S(2)}) collective-permute-start(f32[2056,128]{1,0:T(8,128)S(1)} %features.1.refs_5_), channel_id=1, source_target_pairs={{0,2},{2,0},{4,6},{6,4},{8,10},{10,8},{12,14},{14,12},{16,18},{18,... | collective-permute-start | bytes 3158024 | tf_op jit(solution)/shard_map/ppermute | solution.py:220

commit v8 on v7

--- a/solution.py
+++ b/solution.py
@@ -136,15 +136,29 @@
     feat_ref[layers * half * nb :] = id_ref[...]
 
 
+def pair(feat_ref, nb, groups, g):
+    f = [feat_ref[pl.ds(g + d, nb, stride=groups), :] for d in (0, 1)]
+    return jnp.concatenate(split(jnp.concatenate(f, axis=1)), axis=0)
+
+
+def pairs_kernel(feat_ref, out_ref):
+    nb = out_ref.shape[1] // 2
+    groups = 2 * out_ref.shape[0]
+    for g in range(0, groups, 2):
+        out_ref[g // 2] = pair(feat_ref, nb, groups, g)
+
+
 def products(q_ref, feat_ref):
-    lanes = feat_ref.shape[1]
+    count = q_ref.shape[0] // 2
+    if len(feat_ref.shape) == 3:
+        nb, lanes = feat_ref.shape[1] // 2, feat_ref.shape[2] // 2
+    else:
+        lanes = feat_ref.shape[1]
+        nb = feat_ref.shape[0] // (q_ref.shape[1] // lanes)
     groups = q_ref.shape[1] // lanes
-    nb = feat_ref.shape[0] // groups
-    count = q_ref.shape[0] // 2
     acc = jnp.zeros((2 * nb, 2 * count), jnp.float32)
     for g in range(0, groups, 2):
-        f = [feat_ref[pl.ds(g + d, nb, stride=groups), :] for d in (0, 1)]
-        f = jnp.concatenate(split(jnp.concatenate(f, axis=1)), axis=0)
+        f = feat_ref[g // 2] if len(feat_ref.shape) == 3 else pair(feat_ref, nb, groups, g)
         acc = acc + mm(f, q_ref[:, g * lanes : (g + 2) * lanes], NT)
     acc = acc[:nb] + acc[nb:]
     return acc[:, :count] + acc[:, count:]
@@ -152,7 +166,7 @@
 
 def own_scores_kernel(*refs):
     *pieces, right_ref, mine_ref, score_ref, q_ref = refs
-    layers, lanes = right_ref.shape[0], mine_ref.shape[1]
+    layers, lanes = right_ref.shape[0], mine_ref.shape[2] // 2
     groups = q_ref.shape[1] // lanes
     count, some = q_ref.shape[0] // 2, groups // layers // 2
     for begin in range(0, groups, some):
@@ -267,6 +281,13 @@
     other = swapped(mine, 1)
 
     each = own * ex_count // tok_count
+    pairs = pl.pallas_call(
+        pairs_kernel,
+        out_shape=jax.ShapeDtypeStruct((layers * half // 2, 2 * nb, 4 * r), jnp.bfloat16),
+        compiler_params=pltpu.CompilerParams(vmem_limit_bytes=8 * 1024 * 1024),
+        cost_estimate=pl.CostEstimate(flops=0, bytes_accessed=0, transcendentals=0),
+        name="pairs",
+    )(mine)
     own_scores, split_queries = pl.pallas_call(
         own_scores_kernel,
         out_shape=[
@@ -276,7 +297,7 @@
         compiler_params=pltpu.CompilerParams(vmem_limit_bytes=8 * 1024 * 1024),
         cost_estimate=pl.CostEstimate(flops=10**10, bytes_accessed=2**20, transcendentals=0),
         name="own_scores",
-    )(*pieces, right, mine)
+    )(*pieces, right, pairs)
     chunks = pl.pallas_call(
         functools.partial(scores_kernel, ex_count, tok_count, own, masks),
         out_shape=jax.ShapeDtypeStruct((ex_count * tok_count, EX_DEV * each), jnp.float32),

time: 32 us -> 32 us (level)
  waiting for transfers between devices: 2.14 us -> 1.54 us
  Pallas kernels: 8.7 us -> 9.08 us
    ppermute x5, waiting for transfers between devices: 2.14 us -> 1.54 us  [swapped(): return lax.ppermute(x, 'ex', [(i, i ^ mask) for i in range(ex_count)])]
    pallas_call x0 -> x1, Pallas kernels: none -> 0.6 us  [on_device(): pl.pallas_call(pairs_kernel, out_shape=jax.ShapeDtypeStruct((layers * hal...]
  transfers between devices with their start and end apart: 5 -> 5, of which waited for: 2 -> 2; matrix products, arithmetic and copies ran while one was open for 0% -> 0% of each run, Pallas kernels for 24% -> 25%
where the time goes in v8:
time: 32 us; the launch traced here: 31.8 us
  blocking collectives  11.2 us (35%)
  Pallas kernels  9.08 us (28%)
  starting transfers between devices  7.66 us (24%)
  local copies, waits for them, and re-layouts  2.03 us (6%)
  waiting for transfers between devices  1.54 us (5%)
    all_to_all x1, blocking collectives, on_device(): lax.all_to_all(chunks, ('ex', 'tok'), split_axis=0, concat_axis=0, tiled=...  11.2 us
    ppermute x5, starting transfers between devices, swapped(): return lax.ppermute(x, 'ex', [(i, i ^ mask) for i in range(ex_count)])  7.66 us
    pallas_call x1, Pallas kernels, on_device(): pl.pallas_call(outputs_kernel, in_specs=[pl.BlockSpec(), VMEM, pl.BlockSp...  3.14 us
    pallas_call x1, Pallas kernels, on_device(): pl.pallas_call(features_kernel, in_specs=[pl.BlockSpec(), VMEM, pl.BlockS...  2.98 us
    ppermute x5, waiting for transfers between devices, swapped(): return lax.ppermute(x, 'ex', [(i, i ^ mask) for i in range(ex_count)])  1.54 us
    unnamed x20, local copies, waits for them, and re-layouts  1.29 us
    pallas_call x1, Pallas kernels, on_device(): pl.pallas_call(functools.partial(scores_kernel, ex_count, tok_count, own,...  1.21 us
    pallas_call x1, Pallas kernels, on_device(): pl.pallas_call(own_scores_kernel, out_shape=[jax.ShapeDtypeStruct((nb, ow...  0.86 us
  transfers between devices with their start and end apart: 5, of which 2 were waited for; matrix products, arithmetic and copies ran while one was open for 0% of the time, Pallas kernels for 25%

profile of v8, /device:TPU:0, one launch (start us, length us, event | category | flops | bytes accessed | tf_op | source)
XLA Modules:
  0.0 31.8 jit_solution(6324833199939282139)
XLA Ops:
  0.0 0.0 copy-start.2
  0.0 0.0 copy-start
  0.0 4.0 %collective-permute-start = (f32[2,8192]{1,0:T(2,128)}, f32[2,8192]{1,0:T(2,128)S(1)}, u32[]{:S(2)}, u32[]{:S(2)}) collective-permute-start(f32[2,8192]{1,0:T(2,128)} %param.16), channel_id=1, source_target_pairs={{0,16},{2,18},{4,20},{6,22},{8,24},{10,26},{12,28},{14,30},{16,0},... | collective-permute-start | bytes 196616 | tf_op jit(solution)/shard_map/ppermute | solution.py:234
  4.0 0.0 copy-start.3
  4.0 0.9 %copy-done.3 = f32[2,2,64,64]{3,2,1,0:T(8,128)S(1)} copy-done((f32[2,2,64,64]{3,2,1,0:T(8,128)S(1)}, f32[2,2,64,64]{3,2,1,0:T(8,128)}, u32[]{:S(2)}) %copy-start.3) | copy-done | bytes 65560
  4.9 0.0 copy-start.5
  4.9 0.0 slice-start
  5.0 0.3 factors.1
  5.3 0.3 %copy-done.5 = s32[32]{0:T(128)S(1)} copy-done((s32[32]{0:T(128)S(1)}, s32[32]{0:T(128)}, u32[]{:S(2)}) %copy-start.5) | copy-done | bytes 152
  5.6 0.1 broadcast_in_dim.7.len_ref
  5.7 0.0 copy-done.2
  5.7 0.0 copy-done
  5.7 0.0 copy-start.6
  5.7 0.0 copy-start.7
  5.7 0.0 copy-start.4
  5.7 0.0 slice-start.1
  5.7 0.0 copy-start.1
  5.7 3.1 %outputs.1.out_ref = bf16[2,128,1024]{2,1,0:T(8,128)(2,1)S(1)} custom-call(s32[32,128]{1,0:T(8,128)S(1)} %broadcast_in_dim.7.len_ref, bf16[32,32,2,1024]{3,2,1,0:T(2,128)(2,1)S(1)} %copy-done, bf16[128,1024]{1,0:T(8,128)(2,1)S(1)} %bitcast.14, bf16[256,128]{1,0:T(8,128)(2,1)S(1)} %get-tuple-element.11.left_ref), custom_call_target="tpu_custom_call" | custom-call | flops 10000000000 | bytes 1048576 | tf_op jit(solution)/shard_map/outputs/pallas_call | solution.py:248
  8.9 0.0 copy-done.6
  8.9 0.0 copy-done.7
  8.9 0.0 collective-permute-done
  8.9 0.0 copy-done.4
  8.9 0.1 pad_maximum_fusion.refs_0_
  9.0 2.6 %collective-permute-start.1 = (f32[4,8192]{1,0:T(4,128)S(1)}, f32[4,8192]{1,0:T(4,128)S(1)}, u32[]{:S(2)}, u32[]{:S(2)}) collective-permute-start(f32[4,8192]{1,0:T(4,128)S(1)} %pad_maximum_fusion.refs_0_), channel_id=1, source_target_pairs={{0,12},{2,14},{4,8},{6,10},{8,4},{10,6},{12,0},{14,2},{16,28},{18,... | collective-permute-start | bytes 393224 | tf_op jit(solution)/shard_map/ppermute | solution.py:234
  11.6 0.5 %collective-permute-start.2 = (f32[4,8192]{1,0:T(4,128)S(1)}, f32[4,8192]{1,0:T(4,128)S(1)}, u32[]{:S(2)}, u32[]{:S(2)}) collective-permute-start(f32[4,8192]{1,0:T(4,128)S(1)} %pad_maximum_fusion.refs_0_), channel_id=1, source_target_pairs={{0,4},{2,6},{4,0},{6,2},{8,12},{10,14},{12,8},{14,10},{16,20},{18,... | collective-permute-start | bytes 393224 | tf_op jit(solution)/shard_map/ppermute | solution.py:234
  12.1 0.4 %collective-permute-start.3 = (f32[4,8192]{1,0:T(4,128)S(1)}, f32[4,8192]{1,0:T(4,128)S(1)}, u32[]{:S(2)}, u32[]{:S(2)}) collective-permute-start(f32[4,8192]{1,0:T(4,128)S(1)} %pad_maximum_fusion.refs_0_), channel_id=1, source_target_pairs={{0,8},{2,10},{4,12},{6,14},{8,0},{10,2},{12,4},{14,6},{16,24},{18,... | collective-permute-start | bytes 393224 | tf_op jit(solution)/shard_map/ppermute | solution.py:234
  12.6 0.0 slice-done
  12.6 0.0 slice-done.1
  12.6 0.0 copy-done.1
  12.6 3.0 %features.1.feat_ref = f32[2056,128]{1,0:T(8,128)S(1)} custom-call(f32[8,128]{1,0:T(8,128)S(1)} %broadcast_in_dim.8.id_ref, bf16[32,32,4096]{2,1,0:T(8,128)(2,1)S(1)} %bitcast.13, bf16[2,128,1024]{2,1,0:T(8,128)(2,1)S(1)} %outputs.1.out_ref, bf16[4096,128]{1,0:T(8,128)(2,1)S(1)} %copy-done.1), custom_call_target="tpu_custom_call" | custom-call | flops 10000000000 | bytes 1048576 | tf_op jit(solution)/shard_map/features/pallas_call | solution.py:271
  15.6 0.1 collective-permute-start.4
  15.7 0.6 %pairs.1.refs_5_ = bf16[32,64,256]{2,1,0:T(8,128)(2,1)S(1)} custom-call(f32[2056,128]{1,0:T(8,128)S(1)} %features.1.feat_ref), custom_call_target="tpu_custom_call" | custom-call | tf_op jit(solution)/shard_map/pairs/pallas_call | solution.py:284
  16.3 0.0 collective-permute-done.1.refs_1_
  16.3 1.5 %collective-permute-done.2.refs_2_ = f32[4,8192]{1,0:T(4,128)S(1)} collective-permute-done((f32[4,8192]{1,0:T(4,128)S(1)}, f32[4,8192]{1,0:T(4,128)S(1)}, u32[]{:S(2)}, u32[]{:S(2)}) %collective-permute-start.2) | collective-permute-done | bytes 131104 | tf_op jit(solution)/shard_map/ppermute | solution.py:234
  17.7 0.1 collective-permute-done.3.refs_3_
  17.8 0.9 %own_scores.1 = (f32[32,16]{1,0:T(8,128)S(1)}, bf16[32,8192]{1,0:T(8,128)(2,1)S(1)}) custom-call(f32[4,8192]{1,0:T(4,128)S(1)} %pad_maximum_fusion.refs_0_, f32[4,8192]{1,0:T(4,128)S(1)} %collective-permute-done.1.refs_1_, f32[4,8192]{1,0:T(4,128)S(1)} %collective-permute-done.2.refs_2_, f32[4,8192]{1,0:T(4,128)S(1)} %collective-permute-done.3.refs_3_, ...), custom_call_target="tpu_custom_call" | custom-call | flops 10000000000 | bytes 1048576 | tf_op jit(solution)/shard_map/own_scores/pallas_call | solution.py:291
  18.7 0.0 collective-permute-done.4.other_ref
  18.7 1.2 %scores.1 = f32[32,64]{1,0:T(8,128)S(1)} custom-call(s32[1,128]{1,0:T(1,128)S(1)} %broadcast_in_dim.6.place_ref, bf16[32,8192]{1,0:T(8,128)(2,1)S(1)} %get-tuple-element.15.q_ref, f32[32,16]{1,0:T(8,128)S(1)} %get-tuple-element.16.own_ref, f32[8,128]{1,0:T(8,128)S(1)} %broadcast_in_dim.8.id_ref, f32[2056,128]{1,0:T(8,128)S(1)} %collective-permute-done.4.other_ref), custom_call_target="tpu_custom_call" | custom-call | tf_op jit(solution)/shard_map/scores/pallas_call | solution.py:301
  19.9 11.2 %all_to_all.9 = f32[32,1,64]{2,1,0:T(1,128)S(1)} all-to-all(f32[32,1,64]{2,1,0:T(1,128)S(1)} %bitcast.11), channel_id=1, replica_groups=mesh['ex'=16,'tok'=2] {'ex','tok'}, dimensions={0} | all-to-all | bytes 16384 | tf_op jit(solution)/shard_map/all_to_all | solution.py:307
  31.1 0.1 reduce_sum.9
  31.2 0.7 %mul.24 = f32[4,16]{1,0:T(4,128)} reshape(f32[64]{0:T(128)S(1)} %broadcast_multiply_fusion) | data formatting | bytes 512 | tf_op jit(solution)/shard_map/mul | solution.py:308
  (6 shorter events, 0.0 us)
Async XLA Ops:
  0.0 5.7 %copy-start.2 = (bf16[2,1024,64]{1,2,0:T(8,128)(2,1)S(1)}, bf16[2,1024,64]{1,2,0:T(8,128)(2,1)}, u32[]{:S(2)}) copy-start(bf16[2,1024,64]{1,2,0:T(8,128)(2,1)} %param.15) | copy-start | bytes 786436
  0.0 5.7 %copy-start = (bf16[32,32,2,1024]{3,2,1,0:T(2,128)(2,1)S(1)}, bf16[32,32,2,1024]{3,2,1,0:T(2,128)(2,1)}, u32[]{:S(2)}) copy-start(bf16[32,32,2,1024]{3,2,1,0:T(2,128)(2,1)} %grad_ref.1) | copy-start | bytes 12582916
  0.0 8.9 %collective-permute-start = (f32[2,8192]{1,0:T(2,128)}, f32[2,8192]{1,0:T(2,128)S(1)}, u32[]{:S(2)}, u32[]{:S(2)}) collective-permute-start(f32[2,8192]{1,0:T(2,128)} %param.16), channel_id=1, source_target_pairs={{0,16},{2,18},{4,20},{6,22},{8,24},{10,26},{12,28},{14,30},{16,0},... | collective-permute-start | bytes 196616 | tf_op jit(solution)/shard_map/ppermute | solution.py:234
  4.0 0.9 %copy-start.3 = (f32[2,2,64,64]{3,2,1,0:T(8,128)S(1)}, f32[2,2,64,64]{3,2,1,0:T(8,128)}, u32[]{:S(2)}) copy-start(f32[2,2,64,64]{3,2,1,0:T(8,128)} %precond_ref.1) | copy-start | bytes 196612
  4.9 0.7 %copy-start.5 = (s32[32]{0:T(128)S(1)}, s32[32]{0:T(128)}, u32[]{:S(2)}) copy-start(s32[32]{0:T(128)} %param.11) | copy-start | bytes 388
  4.9 7.6 %slice-start = ((s8[8388608]{0:T(1024)(128)(4,1)}), s8[4194304]{0:T(1024)(128)(4,1)S(1)}, s32[]{:S(2)}) async-start(s8[8388608]{0:T(1024)(128)(4,1)} %bitcast.12), calls=%async_computation.1 | async-start | bytes 8388608
  5.7 3.2 %copy-start.6 = (s32[32]{0:T(128)S(1)}, s32[32]{0:T(128)}, u32[]{:S(2)}) copy-start(s32[32]{0:T(128)} %param.13) | copy-start | bytes 388
  5.7 3.2 %copy-start.7 = (s32[32,1]{0,1:T(1,128)S(1)}, s32[32,1]{0,1:T(1,128)}, u32[]{:S(2)}) copy-start(s32[32,1]{0,1:T(1,128)} %param.12) | copy-start | bytes 388
  5.7 3.2 %copy-start.4 = (f32[2,8192]{1,0:T(2,128)S(1)}, f32[2,8192]{1,0:T(2,128)}, u32[]{:S(2)}) copy-start(f32[2,8192]{1,0:T(2,128)} %param.16) | copy-start | bytes 196612
  5.7 6.9 %slice-start.1 = ((s8[8388608]{0:T(1024)(128)(4,1)}), s8[4194304]{0:T(1024)(128)(4,1)S(1)}, s32[]{:S(2)}) async-start(s8[8388608]{0:T(1024)(128)(4,1)} %bitcast.12), calls=%async_computation.2 | async-start | bytes 8388608
  5.7 6.9 %copy-start.1 = (bf16[4096,128]{1,0:T(8,128)(2,1)S(1)}, bf16[4096,128]{1,0:T(8,128)(2,1)}, u32[]{:S(2)}) copy-start(bf16[4096,128]{1,0:T(8,128)(2,1)} %w_ref.1) | copy-start | bytes 3145732
  9.0 7.3 %collective-permute-start.1 = (f32[4,8192]{1,0:T(4,128)S(1)}, f32[4,8192]{1,0:T(4,128)S(1)}, u32[]{:S(2)}, u32[]{:S(2)}) collective-permute-start(f32[4,8192]{1,0:T(4,128)S(1)} %pad_maximum_fusion.refs_0_), channel_id=1, source_target_pairs={{0,12},{2,14},{4,8},{6,10},{8,4},{10,6},{12,0},{14,2},{16,28},{18,... | collective-permute-start | bytes 393224 | tf_op jit(solution)/shard_map/ppermute | solution.py:234
  11.6 6.1 %collective-permute-start.2 = (f32[4,8192]{1,0:T(4,128)S(1)}, f32[4,8192]{1,0:T(4,128)S(1)}, u32[]{:S(2)}, u32[]{:S(2)}) collective-permute-start(f32[4,8192]{1,0:T(4,128)S(1)} %pad_maximum_fusion.refs_0_), channel_id=1, source_target_pairs={{0,4},{2,6},{4,0},{6,2},{8,12},{10,14},{12,8},{14,10},{16,20},{18,... | collective-permute-start | bytes 393224 | tf_op jit(solution)/shard_map/ppermute | solution.py:234
  12.1 5.7 %collective-permute-start.3 = (f32[4,8192]{1,0:T(4,128)S(1)}, f32[4,8192]{1,0:T(4,128)S(1)}, u32[]{:S(2)}, u32[]{:S(2)}) collective-permute-start(f32[4,8192]{1,0:T(4,128)S(1)} %pad_maximum_fusion.refs_0_), channel_id=1, source_target_pairs={{0,8},{2,10},{4,12},{6,14},{8,0},{10,2},{12,4},{14,6},{16,24},{18,... | collective-permute-start | bytes 393224 | tf_op jit(solution)/shard_map/ppermute | solution.py:234
  15.6 3.1 %collective-permute-start.4 = (f32[2056,128]{1,0:T(8,128)S(1)}, f32[2056,128]{1,0:T(8,128)S(1)}, u32[]{:S(2)}, u32[]{:S(2)}) collective-permute-start(f32[2056,128]{1,0:T(8,128)S(1)} %features.1.feat_ref), channel_id=1, source_target_pairs={{0,2},{2,0},{4,6},{6,4},{8,10},{10,8},{12,14},{14,12},{16,18},{18,... | collective-permute-start | bytes 3158024 | tf_op jit(solution)/shard_map/ppermute | solution.py:234

commit v9 on v7

--- a/solution.py
+++ b/solution.py
@@ -166,33 +166,24 @@
     score_ref[...] = products(q_ref, mine_ref)
 
 
-def scores_kernel(ex_count, tok_count, own, masks, place_ref, q_ref, own_ref, id_ref, other_ref, out_ref):
+def scores_kernel(order_ref, target_ref, tok_ref, q_ref, own_ref, id_ref, other_ref, out_ref):
     acc = jnp.concatenate([own_ref[...], products(q_ref, other_ref)], axis=0)
-    blocks, count = acc.shape
-
-    queries = own * ex_count
-    piece = iota((count, queries), 0) // own
-    mask = jnp.zeros((count, queries), jnp.int32)
-    for k, m in enumerate(masks):
-        mask = jnp.where(piece == k, m, mask)
-    query = jnp.bitwise_xor(mask, place_ref[:, :1]) * own + iota((count, queries), 0) % own
-    order = (query == iota((count, queries), 1)).astype(jnp.float32).astype(jnp.bfloat16)
+    blocks = acc.shape[0]
+    order = order_ref[...]
+    queries = order.shape[1]
     high, low = split(acc)
     acc = mm(high, order) + mm(low, order)
     targets = out_ref.shape[0]
     last = other_ref.shape[0] - id_ref.shape[0]
     ids = [ref[start : start + 1, : blocks // 2] for ref, start in ((id_ref, 0), (other_ref, last))]
-    ids = jnp.concatenate(ids, axis=1).astype(jnp.int32)
-    row = iota((targets * EX_DEV, blocks), 0)
-    owner = row % targets // tok_count * EX_DEV + row // targets == ids
+    owner = target_ref[...] == jnp.concatenate(ids, axis=1)
     owner = owner.astype(jnp.float32).astype(jnp.bfloat16)
     high, low = split(acc)
     full = mm(owner, high) + mm(owner, low)
-    each = queries // tok_count
-    tok = iota((targets * EX_DEV, each), 0) % tok_count
+    each = tok_ref.shape[1]
     result = full[:, :each]
-    for t in range(1, tok_count):
-        result = jnp.where(tok == t, full[:, t * each : (t + 1) * each], result)
+    for t in range(1, queries // each):
+        result = jnp.where(tok_ref[...] == t, full[:, t * each : (t + 1) * each], result)
     out_ref[...] = jnp.concatenate(
         [result[k * targets : (k + 1) * targets] for k in range(EX_DEV)], axis=1
     )
@@ -277,12 +268,20 @@
         cost_estimate=pl.CostEstimate(flops=10**10, bytes_accessed=2**20, transcendentals=0),
         name="own_scores",
     )(*pieces, right, mine)
+    query = (place ^ jnp.repeat(jnp.asarray(masks, jnp.int32), own)) * own
+    query = query + jnp.arange(own * len(masks), dtype=jnp.int32) % own
+    order = (query[:, None] == jnp.arange(own * ex_count)[None, :]).astype(jnp.bfloat16)
+    targets = ex_count * tok_count
+    row = jnp.arange(targets * EX_DEV, dtype=jnp.int32)[:, None]
+    target = (row % targets // tok_count * EX_DEV + row // targets).astype(jnp.float32)
+    target = jnp.broadcast_to(target, (targets * EX_DEV, 2 * nb))
+    tok = jnp.broadcast_to((row % tok_count).astype(jnp.float32), (targets * EX_DEV, each))
     chunks = pl.pallas_call(
-        functools.partial(scores_kernel, ex_count, tok_count, own, masks),
+        scores_kernel,
         out_shape=jax.ShapeDtypeStruct((ex_count * tok_count, EX_DEV * each), jnp.float32),
         compiler_params=pltpu.CompilerParams(vmem_limit_bytes=8 * 1024 * 1024),
         name="scores",
-    )(jnp.full((1, 2 * r), place), split_queries, own_scores, ids, other)
+    )(order, target, tok, split_queries, own_scores, ids, other)
     arrived = lax.all_to_all(chunks, ("ex", "tok"), split_axis=0, concat_axis=0, tiled=True)
     total = jnp.sum(arrived, axis=0) * (1.0 / (r * size))
     return total.reshape(EX_DEV, each).T

time: 32 us -> 33.8 us (1.056)
  local copies, waits for them, and re-layouts: 2.03 us -> 4.52 us
  blocking collectives: 11 us -> 10.2 us
    unnamed x20, local copies, waits for them, and re-layouts: 1.29 us -> 3.47 us
    all_to_all x1, blocking collectives: 11 us -> 10.2 us  [on_device(): lax.all_to_all(chunks, ('ex', 'tok'), split_axis=0, concat_axis=0, tiled=...]
  transfers between devices with their start and end apart: 5 -> 5, of which waited for: 2 -> 2; matrix products, arithmetic and copies ran while one was open for 0% -> 1% of each run, Pallas kernels for 24% -> 22%
where the time goes in v9:
time: 33.8 us; the launch traced here: 33.6 us
  blocking collectives  10.2 us (30%)
  Pallas kernels  8.69 us (26%)
  starting transfers between devices  7.66 us (23%)
  local copies, waits for them, and re-layouts  4.52 us (13%)
  waiting for transfers between devices  2.14 us (6%)
    all_to_all x1, blocking collectives, on_device(): lax.all_to_all(chunks, ('ex', 'tok'), split_axis=0, concat_axis=0, tiled=...  10.2 us
    ppermute x5, starting transfers between devices, swapped(): return lax.ppermute(x, 'ex', [(i, i ^ mask) for i in range(ex_count)])  7.66 us
    unnamed x20, local copies, waits for them, and re-layouts  3.47 us
    pallas_call x1, Pallas kernels, on_device(): pl.pallas_call(outputs_kernel, in_specs=[pl.BlockSpec(), VMEM, pl.BlockSp...  3.12 us
    pallas_call x1, Pallas kernels, on_device(): pl.pallas_call(features_kernel, in_specs=[pl.BlockSpec(), VMEM, pl.BlockS...  2.98 us
    ppermute x5, waiting for transfers between devices, swapped(): return lax.ppermute(x, 'ex', [(i, i ^ mask) for i in range(ex_count)])  2.14 us
    pallas_call x1, Pallas kernels, on_device(): pl.pallas_call(scores_kernel, out_shape=jax.ShapeDtypeStruct((ex_count *...  1.23 us
    pallas_call x1, Pallas kernels, on_device(): pl.pallas_call(own_scores_kernel, out_shape=[jax.ShapeDtypeStruct((nb, ow...  1.06 us
  transfers between devices with their start and end apart: 5, of which 2 were waited for; matrix products, arithmetic and copies ran while one was open for 1% of the time, Pallas kernels for 22%

profile of v9, /device:TPU:0, one launch (start us, length us, event | category | flops | bytes accessed | tf_op | source)
XLA Modules:
  0.0 33.6 jit_solution(6673989404728156401)
XLA Ops:
  0.0 4.0 %collective-permute-start = (f32[2,8192]{1,0:T(2,128)}, f32[2,8192]{1,0:T(2,128)S(1)}, u32[]{:S(2)}, u32[]{:S(2)}) collective-permute-start(f32[2,8192]{1,0:T(2,128)} %param.17), channel_id=1, source_target_pairs={{0,16},{2,18},{4,20},{6,22},{8,24},{10,26},{12,28},{14,30},{16,0},... | collective-permute-start | bytes 196616 | tf_op jit(solution)/shard_map/ppermute | solution.py:211
  4.0 0.0 copy-start.4
  4.0 0.9 %copy-done.4 = f32[2,2,64,64]{3,2,1,0:T(8,128)S(1)} copy-done((f32[2,2,64,64]{3,2,1,0:T(8,128)S(1)}, f32[2,2,64,64]{3,2,1,0:T(8,128)}, u32[]{:S(2)}) %copy-start.4) | copy-done | bytes 65560
  4.9 0.0 copy-start.9
  4.9 0.0 copy-start.6
  4.9 0.0 copy-start.3
  4.9 0.3 factors.1
  5.3 0.3 %copy-done.9 = s32[8]{0:T(128)S(1)} copy-done((s32[8]{0:T(128)S(1)}, s32[8]{0:T(128)}, u32[]{:S(2)}) %copy-start.9) | copy-done | bytes 56
  5.6 0.1 broadcast_in_dim.10
  5.7 0.1 mul.42
  5.8 0.1 fusion.order_ref
  5.8 0.0 copy-done.6
  5.8 0.1 broadcast_in_dim.13.len_ref
  5.9 0.0 copy-done.3
  5.9 0.0 copy-start.1
  5.9 2.2 %copy-done.1 = bf16[32,32,2,1024]{3,2,1,0:T(2,128)(2,1)S(1)} copy-done((bf16[32,32,2,1024]{3,2,1,0:T(2,128)(2,1)S(1)}, bf16[32,32,2,1024]{3,2,1,0:T(2,128)(2,1)}, u32[]{:S(2)}) %copy-start.1) | copy-done | bytes 4194328
  8.1 0.0 copy-start.7
  8.1 0.0 copy-start.8
  8.1 0.0 copy-start.5
  8.1 0.0 copy-start
  8.1 0.0 copy-start.2
  8.1 3.1 %outputs.1.out_ref = bf16[2,128,1024]{2,1,0:T(8,128)(2,1)S(1)} custom-call(s32[32,128]{1,0:T(8,128)S(1)} %broadcast_in_dim.13.len_ref, bf16[32,32,2,1024]{3,2,1,0:T(2,128)(2,1)S(1)} %copy-done.1, bf16[128,1024]{1,0:T(8,128)(2,1)S(1)} %bitcast.12, bf16[256,128]{1,0:T(8,128)(2,1)S(1)} %get-tuple-element.11.left_ref), custom_call_target="tpu_custom_call" | custom-call | flops 10000000000 | bytes 1048576 | tf_op jit(solution)/shard_map/outputs/pallas_call | solution.py:225
  11.3 0.0 copy-done.7
  11.3 0.0 copy-done.8
  11.3 0.0 collective-permute-done
  11.3 0.0 copy-done.5
  11.3 0.1 pad_maximum_fusion.refs_0_
  11.4 2.6 %collective-permute-start.1 = (f32[4,8192]{1,0:T(4,128)S(1)}, f32[4,8192]{1,0:T(4,128)S(1)}, u32[]{:S(2)}, u32[]{:S(2)}) collective-permute-start(f32[4,8192]{1,0:T(4,128)S(1)} %pad_maximum_fusion.refs_0_), channel_id=1, source_target_pairs={{0,12},{2,14},{4,8},{6,10},{8,4},{10,6},{12,0},{14,2},{16,28},{18,... | collective-permute-start | bytes 393224 | tf_op jit(solution)/shard_map/ppermute | solution.py:211
  14.0 0.5 %collective-permute-start.2 = (f32[4,8192]{1,0:T(4,128)S(1)}, f32[4,8192]{1,0:T(4,128)S(1)}, u32[]{:S(2)}, u32[]{:S(2)}) collective-permute-start(f32[4,8192]{1,0:T(4,128)S(1)} %pad_maximum_fusion.refs_0_), channel_id=1, source_target_pairs={{0,4},{2,6},{4,0},{6,2},{8,12},{10,14},{12,8},{14,10},{16,20},{18,... | collective-permute-start | bytes 393224 | tf_op jit(solution)/shard_map/ppermute | solution.py:211
  14.5 0.4 %collective-permute-start.3 = (f32[4,8192]{1,0:T(4,128)S(1)}, f32[4,8192]{1,0:T(4,128)S(1)}, u32[]{:S(2)}, u32[]{:S(2)}) collective-permute-start(f32[4,8192]{1,0:T(4,128)S(1)} %pad_maximum_fusion.refs_0_), channel_id=1, source_target_pairs={{0,8},{2,10},{4,12},{6,14},{8,0},{10,2},{12,4},{14,6},{16,24},{18,... | collective-permute-start | bytes 393224 | tf_op jit(solution)/shard_map/ppermute | solution.py:211
  15.0 0.0 copy-done
  15.0 0.0 copy-done.2
  15.0 3.0 %features.1.refs_5_ = f32[2056,128]{1,0:T(8,128)S(1)} custom-call(f32[8,128]{1,0:T(8,128)S(1)} %broadcast_in_dim.14.id_ref, bf16[32,32,4096]{2,1,0:T(8,128)(2,1)S(1)} %copy-done, bf16[2,128,1024]{2,1,0:T(8,128)(2,1)S(1)} %outputs.1.out_ref, bf16[4096,128]{1,0:T(8,128)(2,1)S(1)} %copy-done.2), custom_call_target="tpu_custom_call" | custom-call | flops 10000000000 | bytes 1048576 | tf_op jit(solution)/shard_map/features/pallas_call | solution.py:248
  17.9 0.1 collective-permute-start.4
  18.1 0.0 collective-permute-done.1.refs_1_
  18.1 2.1 %collective-permute-done.2.refs_2_ = f32[4,8192]{1,0:T(4,128)S(1)} collective-permute-done((f32[4,8192]{1,0:T(4,128)S(1)}, f32[4,8192]{1,0:T(4,128)S(1)}, u32[]{:S(2)}, u32[]{:S(2)}) %collective-permute-start.2) | collective-permute-done | bytes 131104 | tf_op jit(solution)/shard_map/ppermute | solution.py:211
  20.1 0.1 collective-permute-done.3.refs_3_
  20.2 1.1 %own_scores.1 = (f32[32,16]{1,0:T(8,128)S(1)}, bf16[32,8192]{1,0:T(8,128)(2,1)S(1)}) custom-call(f32[4,8192]{1,0:T(4,128)S(1)} %pad_maximum_fusion.refs_0_, f32[4,8192]{1,0:T(4,128)S(1)} %collective-permute-done.1.refs_1_, f32[4,8192]{1,0:T(4,128)S(1)} %collective-permute-done.2.refs_2_, f32[4,8192]{1,0:T(4,128)S(1)} %collective-permute-done.3.refs_3_, ...), custom_call_target="tpu_custom_call" | custom-call | flops 10000000000 | bytes 1048576 | tf_op jit(solution)/shard_map/own_scores/pallas_call | solution.py:261
  21.3 0.0 collective-permute-done.4.other_ref
  21.3 0.1 broadcast_in_dim.11.target_ref
  21.3 0.1 broadcast_in_dim.12.tok_ref
  21.4 1.2 %scores.1 = f32[32,64]{1,0:T(8,128)S(1)} custom-call(bf16[16,32]{1,0:T(8,128)(2,1)S(1)} %fusion.order_ref, f32[128,64]{1,0:T(8,128)S(1)} %broadcast_in_dim.11.target_ref, f32[128,16]{1,0:T(8,128)S(1)} %broadcast_in_dim.12.tok_ref, bf16[32,8192]{1,0:T(8,128)(2,1)S(1)} %get-tuple-element.15.q_ref, f32[32,16]{1,0:T(8,128)S(1)} %get-tuple-element.16.own_ref, ...), custom_call_target="tpu_custom_call" | custom-call | tf_op jit(solution)/shard_map/scores/pallas_call | solution.py:279
  22.7 10.2 %all_to_all.9 = f32[32,1,64]{2,1,0:T(1,128)S(1)} all-to-all(f32[32,1,64]{2,1,0:T(1,128)S(1)} %bitcast.11), channel_id=1, replica_groups=mesh['ex'=16,'tok'=2] {'ex','tok'}, dimensions={0} | all-to-all | bytes 16384 | tf_op jit(solution)/shard_map/all_to_all | solution.py:285
  32.9 0.1 reduce_sum.9
  33.0 0.7 %mul.50 = f32[4,16]{1,0:T(4,128)} reshape(f32[64]{0:T(128)S(1)} %broadcast_multiply_fusion) | data formatting | bytes 512 | tf_op jit(solution)/shard_map/mul | solution.py:286
  (8 shorter events, 0.0 us)
Async XLA Ops:
  0.0 11.3 %collective-permute-start = (f32[2,8192]{1,0:T(2,128)}, f32[2,8192]{1,0:T(2,128)S(1)}, u32[]{:S(2)}, u32[]{:S(2)}) collective-permute-start(f32[2,8192]{1,0:T(2,128)} %param.17), channel_id=1, source_target_pairs={{0,16},{2,18},{4,20},{6,22},{8,24},{10,26},{12,28},{14,30},{16,0},... | collective-permute-start | bytes 196616 | tf_op jit(solution)/shard_map/ppermute | solution.py:211
  4.0 0.9 %copy-start.4 = (f32[2,2,64,64]{3,2,1,0:T(8,128)S(1)}, f32[2,2,64,64]{3,2,1,0:T(8,128)}, u32[]{:S(2)}) copy-start(f32[2,2,64,64]{3,2,1,0:T(8,128)} %precond_ref.1) | copy-start | bytes 196612
  4.9 0.7 %copy-start.9 = (s32[8]{0:T(128)S(1)}, s32[8]{0:T(128)}, u32[]{:S(2)}) copy-start(s32[8]{0:T(128)} %constant.77.clone) | copy-start | bytes 100
  4.9 0.9 %copy-start.6 = (s32[32]{0:T(128)S(1)}, s32[32]{0:T(128)}, u32[]{:S(2)}) copy-start(s32[32]{0:T(128)} %param.12) | copy-start | bytes 388
  4.9 1.0 %copy-start.3 = (bf16[2,1024,64]{1,2,0:T(8,128)(2,1)S(1)}, bf16[2,1024,64]{1,2,0:T(8,128)(2,1)}, u32[]{:S(2)}) copy-start(bf16[2,1024,64]{1,2,0:T(8,128)(2,1)} %param.16) | copy-start | bytes 786436
  5.9 2.2 %copy-start.1 = (bf16[32,32,2,1024]{3,2,1,0:T(2,128)(2,1)S(1)}, bf16[32,32,2,1024]{3,2,1,0:T(2,128)(2,1)}, u32[]{:S(2)}) copy-start(bf16[32,32,2,1024]{3,2,1,0:T(2,128)(2,1)} %grad_ref.1) | copy-start | bytes 12582916
  8.1 3.2 %copy-start.7 = (s32[32]{0:T(128)S(1)}, s32[32]{0:T(128)}, u32[]{:S(2)}) copy-start(s32[32]{0:T(128)} %param.14) | copy-start | bytes 388
  8.1 3.2 %copy-start.8 = (s32[32,1]{0,1:T(1,128)S(1)}, s32[32,1]{0,1:T(1,128)}, u32[]{:S(2)}) copy-start(s32[32,1]{0,1:T(1,128)} %param.13) | copy-start | bytes 388
  8.1 3.2 %copy-start.5 = (f32[2,8192]{1,0:T(2,128)S(1)}, f32[2,8192]{1,0:T(2,128)}, u32[]{:S(2)}) copy-start(f32[2,8192]{1,0:T(2,128)} %param.17) | copy-start | bytes 196612
  8.1 6.8 %copy-start = (bf16[32,32,4096]{2,1,0:T(8,128)(2,1)S(1)}, bf16[32,32,4096]{2,1,0:T(8,128)(2,1)}, u32[]{:S(2)}) copy-start(bf16[32,32,4096]{2,1,0:T(8,128)(2,1)} %act_ref.1) | copy-start | bytes 25165828
  8.1 6.8 %copy-start.2 = (bf16[4096,128]{1,0:T(8,128)(2,1)S(1)}, bf16[4096,128]{1,0:T(8,128)(2,1)}, u32[]{:S(2)}) copy-start(bf16[4096,128]{1,0:T(8,128)(2,1)} %w_ref.1) | copy-start | bytes 3145732
  11.4 6.7 %collective-permute-start.1 = (f32[4,8192]{1,0:T(4,128)S(1)}, f32[4,8192]{1,0:T(4,128)S(1)}, u32[]{:S(2)}, u32[]{:S(2)}) collective-permute-start(f32[4,8192]{1,0:T(4,128)S(1)} %pad_maximum_fusion.refs_0_), channel_id=1, source_target_pairs={{0,12},{2,14},{4,8},{6,10},{8,4},{10,6},{12,0},{14,2},{16,28},{18,... | collective-permute-start | bytes 393224 | tf_op jit(solution)/shard_map/ppermute | solution.py:211
  14.0 6.1 %collective-permute-start.2 = (f32[4,8192]{1,0:T(4,128)S(1)}, f32[4,8192]{1,0:T(4,128)S(1)}, u32[]{:S(2)}, u32[]{:S(2)}) collective-permute-start(f32[4,8192]{1,0:T(4,128)S(1)} %pad_maximum_fusion.refs_0_), channel_id=1, source_target_pairs={{0,4},{2,6},{4,0},{6,2},{8,12},{10,14},{12,8},{14,10},{16,20},{18,... | collective-permute-start | bytes 393224 | tf_op jit(solution)/shard_map/ppermute | solution.py:211
  14.5 5.7 %collective-permute-start.3 = (f32[4,8192]{1,0:T(4,128)S(1)}, f32[4,8192]{1,0:T(4,128)S(1)}, u32[]{:S(2)}, u32[]{:S(2)}) collective-permute-start(f32[4,8192]{1,0:T(4,128)S(1)} %pad_maximum_fusion.refs_0_), channel_id=1, source_target_pairs={{0,8},{2,10},{4,12},{6,14},{8,0},{10,2},{12,4},{14,6},{16,24},{18,... | collective-permute-start | bytes 393224 | tf_op jit(solution)/shard_map/ppermute | solution.py:211
  17.9 3.3 %collective-permute-start.4 = (f32[2056,128]{1,0:T(8,128)S(1)}, f32[2056,128]{1,0:T(8,128)S(1)}, u32[]{:S(2)}, u32[]{:S(2)}) collective-permute-start(f32[2056,128]{1,0:T(8,128)S(1)} %features.1.refs_5_), channel_id=1, source_target_pairs={{0,2},{2,0},{4,6},{6,4},{8,10},{10,8},{12,14},{14,12},{16,18},{18,... | collective-permute-start | bytes 3158024 | tf_op jit(solution)/shard_map/ppermute | solution.py:211
